TPU v7x, 32 devices: a whole 2x2x4 slice. The times are simulated.
32 devices in a mesh: grp: 4 (over y, core), wide: 8 (over z, x).
Axes of the slice: x: 2, y: 2, z: 4, core: 2. Of those that a mesh axis runs over, the one named last changes fastest.
Arguments:
- codes: bfloat16 [768, 16384], P(('grp', 'wide')), may hold values from -6 to 6
- exponents: int32 [768], P(('grp', 'wide')), may hold values from -2 to 1
- precond: bfloat16 [16384, 16384], P(None, 'wide')
- partner: int32 [4], replicated, may hold values from 0 to 3, each once
Outputs:
- kernel_diag: float32 [768, 192], P(('grp', 'wide'))
- kernel_pair: float32 [768, 192], P(('grp', 'wide'))
- kernel_back: float32 [768, 192], P(('grp', 'wide'))
Inputs may be any that keep to these rules, and one draw needn't show every extreme that they name: `partner`: every row group index appears exactly once.
All inputs are finite; a program needn't handle non-finite values.
Results may differ from a plain program's by a relative error of at most 0.0029.
Values may be sent and summed in bfloat16 or wider, within the bound.
No kernel may reach another device: no remote copies, remote signals or barrier semaphores. Data moves between devices by JAX's collectives and lax.ppermute only.
A program may use at most 128 MiB of HBM per device.

v0:
```python
import math

import jax
import jax.numpy as jnp
from jax import lax
from jax.sharding import PartitionSpec as P


def contract(left, right):
    return lax.dot_general(
        left, right, (((1,), (1,)), ((), ())), preferred_element_type=jnp.float32
    )


def shards(codes, exponents, precond, partner):
    width = codes.shape[1]
    cols = precond.shape[1]
    factor = 1.0 / math.sqrt(width)
    col_start = lax.axis_index("wide") * cols
    group_index = lax.axis_index("grp")
    scaled = (codes.astype(jnp.float32) * jnp.exp2(exponents.astype(jnp.float32))[:, None]).astype(
        jnp.bfloat16
    )
    piece = lax.all_gather(scaled, "wide", axis=0, tiled=True)
    image = jnp.dot(piece, precond, preferred_element_type=jnp.float32).astype(jnp.bfloat16)
    slab = lax.dynamic_slice_in_dim(piece, col_start, cols, 1)
    stacked = lax.all_gather(slab[None], "grp", axis=0, tiled=True)
    partner_index = lax.dynamic_index_in_dim(partner, group_index, 0, keepdims=False)
    other_cols = lax.dynamic_index_in_dim(stacked, partner_index, 0, keepdims=False)
    kernel_diag = (
        lax.psum_scatter(contract(image, slab), "wide", scatter_dimension=0, tiled=True) * factor
    )
    pair_rows = lax.psum_scatter(
        contract(image, other_cols), "wide", scatter_dimension=0, tiled=True
    )
    back_rows = lax.psum_scatter(
        contract(other_cols, image), "wide", scatter_dimension=0, tiled=True
    )
    returned = lax.all_gather(back_rows[None], "grp", axis=0, tiled=True)
    picker = (partner == group_index).astype(jnp.float32)
    kernel_back = jnp.sum(picker[:, None, None] * returned, axis=0) * factor
    kernel_pair = pair_rows * factor
    return (kernel_diag, kernel_pair, kernel_back)


def solution(mesh):
    return jax.shard_map(
        shards,
        mesh=mesh,
        in_specs=(P(("grp", "wide"), None), P(("grp", "wide")), P(None, "wide"), P()),
        out_specs=(P(("grp", "wide"), None), P(("grp", "wide"), None), P(("grp", "wide"), None)),
        check_vma=False,
    )
```

profile of v0, /device:TPU:0, one launch (start us, length us, event | category | flops | bytes accessed | tf_op | source)
XLA Modules:
  0.0 339.7 jit_solution(2709743857198347549)
XLA Ops:
  7.2 0.0 all-gather.5.cloned.1.call-start
  7.2 0.7 multiply_exponential_fusion
  7.9 2.2 multiply_convert_fusion
  10.1 0.0 all-gather.5.cloned.1.call-update
  10.1 0.0 all-gather.7.cloned.1.call-start
  10.2 101.8 %all-gather.5.cloned.1.call-done = bf16[192,16384]{1,0:T(8,128)(2,1)} async-done(((bf16[24,16384]{1,0:T(8,128)(2,1)}), bf16[192,16384]{1,0:T(8,128)(2,1)}) %all-gather.5.cloned.1.call-update) | async-done | bytes 6291472 | tf_op jit(solution)/shard_map/all_gather | solution.py:24
  112.0 2.1 constant_dynamic-slice_fusion
  114.1 0.0 all-gather.7.cloned.1.call-update
  114.1 0.0 reduce-scatter.4.cloned.1.call-start
  114.1 0.0 copy-start
  114.1 0.0 copy-start.1
  114.2 28.2 %convolution_convert_fusion = bf16[192,2048]{1,0:T(8,128)(2,1)S(1)} fusion(bf16[192,16384]{1,0:T(8,128)(2,1)} %all-gather.5.cloned.1.call-done, bf16[16384,2048]{1,0:T(8,128)(2,1)} %param.6), kind=kOutput, calls=%fused_computation | convolution fusion | flops 12885295104 | bytes 74186752 | tf_op jit(solution)/shard_map/dot_general | solution.py:25
  142.4 0.0 copy-done
  142.4 1.1 fusion.8
  143.5 0.0 reduce-scatter.4.cloned.1.call-update
  143.5 0.0 reduce-scatter.8.cloned.1.call-start
  143.6 0.0 copy-done.1
  143.6 0.6 dynamic_slice.12
  146.1 0.0 all-gather.7.cloned.1.call-done
  146.1 2.2 fusion
  148.3 0.0 reduce-scatter.8.cloned.1.call-update
  148.4 0.0 reduce-scatter.6.cloned.1.call-start
  148.4 56.9 %reduce-scatter.4.cloned.1.call-done = f32[24,192]{1,0:T(8,128)} async-done(((f32[192,192]{1,0:T(8,128)}), f32[24,192]{1,0:T(8,128)}) %reduce-scatter.4.cloned.1.call-update) | async-done | bytes 18448 | tf_op jit(solution)/shard_map/reduce_scatter | solution.py:31
  205.3 1.3 broadcast_multiply_fusion.2
  206.7 2.2 fusion.2
  208.9 0.0 reduce-scatter.6.cloned.1.call-update
  208.9 59.7 %reduce-scatter.8.cloned.1.call-done = f32[24,192]{1,0:T(8,128)} async-done(((f32[192,192]{1,0:T(8,128)}), f32[24,192]{1,0:T(8,128)}) %reduce-scatter.8.cloned.1.call-update) | async-done | bytes 18448 | tf_op jit(solution)/shard_map/reduce_scatter | solution.py:36
  268.6 5.5 %all-gather.1 = f32[96,192]{1,0:T(8,128)S(1)} all-gather(f32[24,192]{1,0:T(8,128)} %reduce-scatter.8.cloned.1.call-done), channel_id=3, replica_groups=mesh['grp'=4,'wide'=8] {'grp'}, dimensions={0}, use_global_device_ids=true | all-gather | bytes 92160 | tf_op jit(solution)/shard_map/all_gather | solution.py:39
  274.1 0.1 multiply_reduce_fusion
  274.2 0.6 broadcast_multiply_fusion
  274.8 57.0 %reduce-scatter.6.cloned.1.call-done = f32[24,192]{1,0:T(8,128)} async-done(((f32[192,192]{1,0:T(8,128)}), f32[24,192]{1,0:T(8,128)}) %reduce-scatter.6.cloned.1.call-update) | async-done | bytes 18448 | tf_op jit(solution)/shard_map/reduce_scatter | solution.py:33
  331.8 1.3 broadcast_multiply_fusion.1
  (1 shorter events, 0.0 us)
Async XLA Ops:
  7.2 104.8 %all-gather.5.cloned.1.call-start = ((), (), s32[]{:S(2)}) async-start(), calls=%async_computation.3 | async-start | bytes 7077888 | tf_op jit(solution)/shard_map/all_gather | solution.py:24
  10.1 136.0 %all-gather.7.cloned.1.call-start = ((), (), s32[]{:S(2)}) async-start(), calls=%async_computation.7 | async-start | bytes 3932160 | tf_op jit(solution)/shard_map/all_gather | solution.py:27
  114.1 91.2 %reduce-scatter.4.cloned.1.call-start = ((), (), s32[]{:S(2)}) async-start(), calls=%async_computation.4 | async-start | bytes 221184 | tf_op jit(solution)/shard_map/reduce_scatter | solution.py:31
  114.1 28.3 %copy-start = (bf16[192,2048]{1,0:T(8,128)(2,1)S(1)}, bf16[192,2048]{1,0:T(8,128)(2,1)}, u32[]{:S(2)}) copy-start(bf16[192,2048]{1,0:T(8,128)(2,1)} %constant_dynamic-slice_fusion) | copy-start | bytes 2359300
  114.1 29.4 %copy-start.1 = (s32[4]{0:T(128)S(1)}, s32[4]{0:T(128)}, u32[]{:S(2)}) copy-start(s32[4]{0:T(128)} %param.7) | copy-start | bytes 52
  143.5 125.1 %reduce-scatter.8.cloned.1.call-start = ((), (), s32[]{:S(2)}) async-start(), calls=%async_computation.6 | async-start | bytes 221184 | tf_op jit(solution)/shard_map/reduce_scatter | solution.py:36
  148.4 183.5 %reduce-scatter.6.cloned.1.call-start = ((), (), s32[]{:S(2)}) async-start(), calls=%async_computation.5 | async-start | bytes 221184 | tf_op jit(solution)/shard_map/reduce_scatter | solution.py:33
Sparse Core Ops, SparseCore 0:
  10.2 101.7 all-gather.4
  114.2 26.7 all-gather.6
  144.2 61.0 reduce-scatter.3
  208.4 60.0 reduce-scatter.7
  271.7 60.0 reduce-scatter.5
where the time goes:
time: 340 us
  waiting for transfers between devices  276 us (81%)
  matrix products  33.7 us (10%)
  between operations  15.8 us (5%)
  other arithmetic  6.26 us (2%)
  blocking collectives  5.53 us (2%)
    all_gather x1, waiting for transfers between devices, shards(): piece = lax.all_gather(scaled, 'wide', axis=0, tiled=True)  102 us
    reduce_scatter x1, waiting for transfers between devices, shards(): lax.psum_scatter(contract(other_cols, image), 'wide', scatter_dimension=0...  59.7 us
    reduce_scatter x1, waiting for transfers between devices, shards(): lax.psum_scatter(contract(image, other_cols), 'wide', scatter_dimension=0...  57 us
    reduce_scatter x1, waiting for transfers between devices, shards(): lax.psum_scatter(contract(image, slab), 'wide', scatter_dimension=0, tile...  56.9 us
    dot_general x1, matrix products, shards(): jnp.dot(piece, precond, preferred_element_type=jnp.float32)  28.2 us
  transfers between devices with their start and end apart: 5, of which 4 were waited for; matrix products, arithmetic and copies ran while one was open for 11% of the time, Pallas kernels for 0%

commit v1 on v0

v1 whole, which is shorter than its diff:
```python
import functools
import math

import jax
import jax.numpy as jnp
from jax import lax
from jax.experimental import pallas as pl
from jax.experimental.pallas import tpu as pltpu
from jax.sharding import PartitionSpec as P

CHUNKS = 4
VMEM_LIMIT = 48 * 2**20


def snake(n):
    return list(range(0, n, 2)) + list(range(n - 1, 0, -2))


def load_rows(mat_hbm, buf, sem, chunk):
    n, depth = buf.shape[0], buf.shape[1]
    return [
        pltpu.make_async_copy(
            mat_hbm.at[pl.ds((w * CHUNKS + chunk) * depth, depth)], buf.at[w], sem.at[w]
        )
        for w in range(n)
    ]


def accumulate(chunk, rows_ref, mat_hbm, buf, sem, total_ref):
    n, depth = buf.shape[0], buf.shape[1]
    copies = load_rows(mat_hbm, buf, sem, chunk)
    for copy in copies:
        copy.start()

    def step(w, carry):
        pltpu.make_async_copy(mat_hbm.at[pl.ds(0, depth)], buf.at[w], sem.at[w]).wait()
        columns = pl.ds(pl.multiple_of(w * depth, depth), depth)
        total_ref[...] += jnp.dot(
            rows_ref[:, columns], buf[w], preferred_element_type=jnp.float32
        )
        return carry

    lax.fori_loop(0, n, step, 0)


def first_kernel(chunk, rows_ref, mat_hbm, total_ref, buf, sem):
    total_ref[...] = jnp.zeros_like(total_ref)
    accumulate(chunk, rows_ref, mat_hbm, buf, sem, total_ref)


def next_kernel(chunk, rows_ref, mat_hbm, before_ref, total_ref, buf, sem):
    total_ref[...] = before_ref[...]
    accumulate(chunk, rows_ref, mat_hbm, buf, sem, total_ref)


def contract(left, right):
    return lax.dot_general(
        left, right, (((1,), (1,)), ((), ())), preferred_element_type=jnp.float32
    )


def last_kernel(
    chunk, n, order_ref, rows_ref, mat_hbm, before_ref, own_ref, other_ref, out_ref, buf, sem, total, held, placed
):
    total[...] = before_ref[...]
    accumulate(chunk, rows_ref, mat_hbm, buf, sem, total)
    image = total[...].astype(jnp.bfloat16)
    size = image.shape[0]
    step = size // n

    def reorder(block):
        held[...] = block
        for i in range(n):
            placed[pl.ds(pl.multiple_of(order_ref[i] * step, 8), step), :] = held[i * step : (i + 1) * step, :]
        return placed[...]

    diag = reorder(reorder(contract(image, own_ref[...])).T).T
    back = reorder(reorder(contract(image, other_ref[...])).T)
    out_ref[:, :size] = diag
    out_ref[:, size : 2 * size] = back.T
    out_ref[:, 2 * size :] = back


def multiply(chunk, rows, mat, before=None, tail=None):
    size, width = rows.shape
    n = width // (mat.shape[0] // (mat.shape[0] // mat.shape[1]) // CHUNKS)
    depth = width // n
    cols = mat.shape[1]
    scratch = [pltpu.VMEM((n, depth, cols), mat.dtype), pltpu.SemaphoreType.DMA((n,))]
    whole = pl.BlockSpec(memory_space=pltpu.VMEM)
    common = dict(
        compiler_params=pltpu.CompilerParams(vmem_limit_bytes=VMEM_LIMIT),
        cost_estimate=pl.CostEstimate(
            flops=2 * size * width * cols, bytes_accessed=2 * width * cols, transcendentals=0
        ),
    )
    total = jax.ShapeDtypeStruct((size, cols), jnp.float32)
    hbm = pl.BlockSpec(memory_space=pl.ANY)
    if before is None:
        return pl.pallas_call(
            functools.partial(first_kernel, chunk),
            in_specs=[whole, hbm],
            out_specs=whole,
            out_shape=total,
            scratch_shapes=scratch,
            **common,
        )(rows, mat)
    if tail is None:
        return pl.pallas_call(
            functools.partial(next_kernel, chunk),
            in_specs=[whole, hbm, whole],
            out_specs=whole,
            out_shape=total,
            scratch_shapes=scratch,
            **common,
        )(rows, mat, before)
    order, own, other = tail
    return pl.pallas_call(
        functools.partial(last_kernel, chunk, n),
        in_specs=[pl.BlockSpec(memory_space=pltpu.SMEM), whole, hbm, whole, whole, whole],
        out_specs=whole,
        out_shape=jax.ShapeDtypeStruct((size, 3 * size), jnp.float32),
        scratch_shapes=scratch
        + [pltpu.VMEM((size, cols), jnp.float32), pltpu.VMEM((size, size), jnp.float32),
        pltpu.VMEM((size, size), jnp.float32)],
        **common,
    )(order, rows, mat, before, own, other)


def after(value, *others):
    return lax.optimization_barrier((value, *others))[0]


def fetch(value, source):
    me = lax.axis_index("grp")
    near = lax.ppermute(value, "grp", [(i, i ^ 1) for i in range(4)])
    wanted = lax.dynamic_index_in_dim(source, me ^ 2, 0, keepdims=False)
    sent = jnp.where(wanted == me, value, near)
    far = lax.ppermute(sent, "grp", [(i, i ^ 2) for i in range(4)])
    mine = lax.dynamic_index_in_dim(source, me, 0, keepdims=False)
    return jnp.where(mine == me, value, jnp.where(mine == me ^ 1, near, far))


def shards(codes, exponents, precond, partner, n):
    rows, width = codes.shape
    cols = precond.shape[1]
    depth = cols // CHUNKS
    factor = 1.0 / math.sqrt(width)
    me = lax.axis_index("wide")
    group = lax.axis_index("grp")
    ring = snake(n)
    forth = [(ring[i], ring[(i + 1) % n]) for i in range(n)]
    back = [(ring[(i + 1) % n], ring[i]) for i in range(n)]
    place = jnp.array([ring.index(i) for i in range(n)], jnp.int32)[me]

    scale = jnp.exp2(exponents.astype(jnp.float32))[:, None]
    scaled = (codes.astype(jnp.float32) * scale).astype(jnp.bfloat16)
    parts = scaled.reshape(rows, n, CHUNKS, depth)
    parts = [parts[:, :, k].reshape(rows, n * depth) for k in range(CHUNKS)]

    hops = [0]
    for s in range(1, n // 2):
        hops += [-s, s]
    hops.append(n // 2)
    order = jnp.array(ring, jnp.int32)[(place + jnp.array(hops, jnp.int32)) % n]

    gathered = [None] * CHUNKS
    half = n * depth // 2
    tie = [None, None]
    for pair in range(0, CHUNKS, 2):
        lanes = []
        for lane in range(2):
            own = parts[pair + lane]
            if tie[lane] is not None:
                own = after(own, *tie[lane])
            lanes.append((own, own, [own]))
        for _ in range(1, n // 2):
            for lane in range(2):
                up, down, held = lanes[lane]
                up, down = lax.ppermute(up, "wide", forth), lax.ppermute(down, "wide", back)
                lanes[lane] = (up, down, held + [up, down])
        for lane in range(2):
            up, down, held = lanes[lane]
            tie[lane] = (up, down)
            end = jnp.concatenate(
                [
                    lax.ppermute(up[:, :half], "wide", forth),
                    lax.ppermute(down[:, half:], "wide", back),
                ],
                axis=1,
            )
            gathered[pair + lane] = jnp.concatenate(held + [end], axis=0)

    slabs, others = [], []
    for k in range(CHUNKS):
        slabs.append(lax.dynamic_slice_in_dim(gathered[k], me * depth, depth, 1))
    for pair in range(0, CHUNKS, 2):
        others.append(fetch(jnp.concatenate(slabs[pair : pair + 2], axis=1), partner))
    own = jnp.concatenate(slabs, axis=1)
    other = jnp.concatenate(others, axis=1)

    total = None
    for k in range(CHUNKS):
        tail = (order, own, other) if k == CHUNKS - 1 else None
        total = multiply(k, gathered[k], precond, total, tail)

    sums = total.reshape(n, rows, total.shape[1])
    bit = 1
    while bit < n:
        pairs = sums.reshape(sums.shape[0] // 2, 2, rows, sums.shape[2])
        mine = (me // bit) % 2
        kept = lax.dynamic_index_in_dim(pairs, mine, 1, keepdims=False)
        given = lax.dynamic_index_in_dim(pairs, 1 - mine, 1, keepdims=False)
        sums = kept + lax.ppermute(given, "wide", [(i, i ^ bit) for i in range(n)])
        bit *= 2
    sums = sums[0] * factor
    size = n * rows
    inverse = jnp.argmax(partner == group).astype(jnp.int32)
    returned = lax.all_gather(sums[None, :, 2 * size :], "grp", axis=0, tiled=True)
    kernel_back = lax.dynamic_index_in_dim(returned, inverse, 0, keepdims=False)
    return (sums[:, :size], sums[:, size : 2 * size], kernel_back)


def solution(mesh):
    return jax.shard_map(
        functools.partial(shards, n=mesh.shape["wide"]),
        mesh=mesh,
        in_specs=(P(("grp", "wide"), None), P(("grp", "wide")), P(None, "wide"), P()),
        out_specs=(P(("grp", "wide"), None), P(("grp", "wide"), None), P(("grp", "wide"), None)),
        check_vma=False,
    )
```

time: 340 us -> 154 us (0.45)
  waiting for transfers between devices: 276 us -> 54.3 us
  starting transfers between devices: 0.21 us -> 40.9 us
  matrix products: 33.7 us -> 0 us
  Pallas kernels: 0 us -> 27.9 us
  local copies, waits for them, and re-layouts: 2.68 us -> 15.7 us
  between operations: 15.8 us -> 5.17 us
    reduce_scatter x3 -> x0, waiting for transfers between devices: 174 us -> none  [the longest x1 59.7 us: shards(): lax.psum_scatter(contract(other_cols, image), 'wide', scatter_dimension=0...]
    all_gather x2 -> x0, waiting for transfers between devices: 102 us -> none  [the longest x1 102 us: shards(): piece = lax.all_gather(scaled, 'wide', axis=0, tiled=True)]
    ppermute x0 -> x39, waiting for transfers between devices: none -> 54.3 us  [the longest x12 14.4 us: shards(): lax.ppermute(up, 'wide', forth)]
    ppermute x0 -> x39, starting transfers between devices: none -> 40.9 us  [the longest x12 22.9 us: shards(): lax.ppermute(up, 'wide', forth)]
    dot_general x4 -> x0, matrix products: 33.7 us -> none  [the longest x1 28.2 us: shards(): jnp.dot(piece, precond, preferred_element_type=jnp.float32)]
    pallas_call x0 -> x4, Pallas kernels: none -> 27.9 us  [the longest x2 13.1 us: multiply(): pl.pallas_call(functools.partial(next_kernel, chunk), in_specs=[whole, hb...]
    unnamed x4 -> x42, local copies, waits for them, and re-layouts: 0.01 us -> 8.38 us
    slice x0 -> x10, local copies, waits for them, and re-layouts: none -> 4.14 us  [the longest x1 3.39 us: shards(): parts = [parts[:, :, k].reshape(rows, n * depth) for k in range(CHUNKS)]]
  transfers between devices with their start and end apart: 5 -> 39, of which waited for: 4 -> 23; matrix products, arithmetic and copies ran while one was open for 11% -> 7% of each run, Pallas kernels for 0% -> 13%
where the time goes in v1:
time: 154 us; the launch traced here: 153 us
  waiting for transfers between devices  54.3 us (35%)
  starting transfers between devices  40.9 us (27%)
  Pallas kernels  27.9 us (18%)
  local copies, waits for them, and re-layouts  15.7 us (10%)
  blocking collectives  5.32 us (3%)
  between operations  5.17 us (3%)
  other arithmetic  4.19 us (3%)
    ppermute x12, starting transfers between devices, shards(): lax.ppermute(up, 'wide', forth)  22.9 us
    ppermute x12, waiting for transfers between devices, shards(): lax.ppermute(up, 'wide', forth)  14.4 us
    pallas_call x2, Pallas kernels, multiply(): pl.pallas_call(functools.partial(next_kernel, chunk), in_specs=[whole, hb...  13.1 us
    ppermute x2, waiting for transfers between devices, fetch(): far = lax.ppermute(sent, 'grp', [(i, i ^ 2) for i in range(4)])  10.9 us
    ppermute x3, waiting for transfers between devices, shards(): sums = kept + lax.ppermute(given, 'wide', [(i, i ^ bit) for i in range(n)])  10.7 us
    ppermute x4, waiting for transfers between devices, shards(): lax.ppermute(up[:, :half], 'wide', forth)  9.55 us
    unnamed x42, local copies, waits for them, and re-layouts  8.38 us
    pallas_call x1, Pallas kernels, multiply(): pl.pallas_call(functools.partial(last_kernel, chunk, n), in_specs=[pl.Blo...  8.37 us
  transfers between devices with their start and end apart: 39, of which 23 were waited for; matrix products, arithmetic and copies ran while one was open for 7% of the time, Pallas kernels for 13%

profile of v1, /device:TPU:0, one launch (start us, length us, event | category | flops | bytes accessed | tf_op | source)
XLA Modules:
  0.0 153.5 jit_solution(7038754518702968303)
XLA Ops:
  3.2 3.4 %slice_reduce_fusion = (bf16[24,8,512]{2,1,0:T(8,128)(2,1)S(1)}, bf16[24,8,512]{2,1,0:T(8,128)(2,1)S(1)}, bf16[24,8,512]{2,1,0:T(8,128)(2,1)S(1)}, bf16[24,8,512]{2,1,0:T(8,128)(2,1)S(1)}) fusion(bf16[24,8,4,512]{3,2,1,0:T(4,128)(2,1)S(1)} %reshape.20), kind=kLoop, calls=%fused_computation.4 | loop fusion | bytes 1572864 | tf_op jit(solution)/shard_map/slice | solution.py:159
  7.4 3.0 %collective-permute-start = (bf16[24,4096]{1,0:T(8,128)(2,1)}, bf16[24,4096]{1,0:T(8,128)(2,1)}, u32[]{:S(2)}, u32[]{:S(2)}) collective-permute-start(bf16[24,4096]{1,0:T(8,128)(2,1)} %bitcast.15), channel_id=1, source_target_pairs={{0,2},{2,4},{4,6},{6,7},{7,5},{5,3},{3,1},{1,0},{8,10},{10,12},{12... | collective-permute-start | bytes 589832 | tf_op jit(solution)/shard_map/ppermute | solution.py:180
  11.2 2.0 %collective-permute-start.14 = (bf16[24,4096]{1,0:T(8,128)(2,1)}, bf16[24,4096]{1,0:T(8,128)(2,1)}, u32[]{:S(2)}, u32[]{:S(2)}) collective-permute-start(bf16[24,4096]{1,0:T(8,128)(2,1)} %bitcast.19), channel_id=1, source_target_pairs={{0,2},{2,4},{4,6},{6,7},{7,5},{5,3},{3,1},{1,0},{8,10},{10,12},{12... | collective-permute-start | bytes 589832 | tf_op jit(solution)/shard_map/ppermute | solution.py:180
  20.4 2.1 %collective-permute-start.1 = (bf16[24,4096]{1,0:T(8,128)(2,1)}, bf16[24,4096]{1,0:T(8,128)(2,1)S(1)}, u32[]{:S(2)}, u32[]{:S(2)}) collective-permute-start(bf16[24,4096]{1,0:T(8,128)(2,1)} %collective-permute-done), channel_id=1, source_target_pairs={{0,2},{2,4},{4,6},{6,7},{7,5},{5,3},{3,1},{1,0},{8,10},{10,12},{12... | collective-permute-start | bytes 589832 | tf_op jit(solution)/shard_map/ppermute | solution.py:180
  24.5 2.1 %collective-permute-start.15 = (bf16[24,4096]{1,0:T(8,128)(2,1)}, bf16[24,4096]{1,0:T(8,128)(2,1)S(1)}, u32[]{:S(2)}, u32[]{:S(2)}) collective-permute-start(bf16[24,4096]{1,0:T(8,128)(2,1)} %collective-permute-done.14), channel_id=1, source_target_pairs={{0,2},{2,4},{4,6},{6,7},{7,5},{5,3},{3,1},{1,0},{8,10},{10,12},{12... | collective-permute-start | bytes 589832 | tf_op jit(solution)/shard_map/ppermute | solution.py:180
  28.6 2.1 %collective-permute-start.2 = (bf16[24,4096]{1,0:T(8,128)(2,1)S(1)}, bf16[24,4096]{1,0:T(8,128)(2,1)S(1)}, u32[]{:S(2)}, u32[]{:S(2)}) collective-permute-start(bf16[24,4096]{1,0:T(8,128)(2,1)S(1)} %collective-permute-done.1), channel_id=1, source_target_pairs={{0,2},{2,4},{4,6},{6,7},{7,5},{5,3},{3,1},{1,0},{8,10},{10,12},{12... | collective-permute-start | bytes 589832 | tf_op jit(solution)/shard_map/ppermute | solution.py:180
  32.3 2.1 %collective-permute-start.16 = (bf16[24,4096]{1,0:T(8,128)(2,1)S(1)}, bf16[24,4096]{1,0:T(8,128)(2,1)S(1)}, u32[]{:S(2)}, u32[]{:S(2)}) collective-permute-start(bf16[24,4096]{1,0:T(8,128)(2,1)S(1)} %collective-permute-done.15), channel_id=1, source_target_pairs={{0,2},{2,4},{4,6},{6,7},{7,5},{5,3},{3,1},{1,0},{8,10},{10,12},{12... | collective-permute-start | bytes 589832 | tf_op jit(solution)/shard_map/ppermute | solution.py:180
  35.7 3.4 %collective-permute-done.16 = bf16[24,4096]{1,0:T(8,128)(2,1)S(1)} collective-permute-done((bf16[24,4096]{1,0:T(8,128)(2,1)S(1)}, bf16[24,4096]{1,0:T(8,128)(2,1)S(1)}, u32[]{:S(2)}, u32[]{:S(2)}) %collective-permute-start.16) | collective-permute-done | bytes 196640 | tf_op jit(solution)/shard_map/ppermute | solution.py:180
  39.1 2.9 %collective-permute-done.19 = bf16[24,4096]{1,0:T(8,128)(2,1)S(1)} collective-permute-done((bf16[24,4096]{1,0:T(8,128)(2,1)S(1)}, bf16[24,4096]{1,0:T(8,128)(2,1)S(1)}, u32[]{:S(2)}, u32[]{:S(2)}) %collective-permute-start.19) | collective-permute-done | bytes 196640 | tf_op jit(solution)/shard_map/ppermute | solution.py:180
  45.8 1.6 %collective-permute-start.28 = (bf16[24,2048]{1,0:T(8,128)(2,1)S(1)}, bf16[24,2048]{1,0:T(8,128)(2,1)S(1)}, u32[]{:S(2)}, u32[]{:S(2)}) collective-permute-start(bf16[24,2048]{1,0:T(8,128)(2,1)S(1)} %slice.70), channel_id=1, source_target_pairs={{0,2},{2,4},{4,6},{6,7},{7,5},{5,3},{3,1},{1,0},{8,10},{10,12},{12... | collective-permute-start | bytes 294920 | tf_op jit(solution)/shard_map/ppermute | solution.py:187
  48.0 5.4 %collective-permute-done.28 = bf16[24,2048]{1,0:T(8,128)(2,1)S(1)} collective-permute-done((bf16[24,2048]{1,0:T(8,128)(2,1)S(1)}, bf16[24,2048]{1,0:T(8,128)(2,1)S(1)}, u32[]{:S(2)}, u32[]{:S(2)}) %collective-permute-start.28) | collective-permute-done | bytes 98336 | tf_op jit(solution)/shard_map/ppermute | solution.py:187
  55.5 2.5 %collective-permute-done.30 = bf16[24,2048]{1,0:T(8,128)(2,1)S(1)} collective-permute-done((bf16[24,2048]{1,0:T(8,128)(2,1)S(1)}, bf16[24,2048]{1,0:T(8,128)(2,1)S(1)}, u32[]{:S(2)}, u32[]{:S(2)}) %collective-permute-start.30) | collective-permute-done | bytes 98336 | tf_op jit(solution)/shard_map/ppermute | solution.py:187
  58.1 1.8 %collective-permute-done.31 = bf16[24,2048]{1,0:T(8,128)(2,1)S(1)} collective-permute-done((bf16[24,2048]{1,0:T(8,128)(2,1)S(1)}, bf16[24,2048]{1,0:T(8,128)(2,1)S(1)}, u32[]{:S(2)}, u32[]{:S(2)}) %collective-permute-start.31) | collective-permute-done | bytes 98336 | tf_op jit(solution)/shard_map/ppermute | solution.py:188
  60.0 6.5 %shard_map.94.before_ref = f32[192,2048]{1,0:T(8,128)S(1)} custom-call(bf16[192,4096]{1,0:T(8,128)(2,1)S(1)} %maximum_dynamic-update-slice_fusion.3.rows_ref, bf16[16384,2048]{1,0:T(8,128)(2,1)} %mat_hbm.7), custom_call_target="tpu_custom_call" | custom-call | flops 3221225472 | bytes 16777216 | tf_op jit(solution)/shard_map/pallas_call | solution.py:100
  66.6 6.5 %shard_map.95.before_ref = f32[192,2048]{1,0:T(8,128)S(1)} custom-call(bf16[192,4096]{1,0:T(8,128)(2,1)S(1)} %maximum_dynamic-update-slice_fusion.2.rows_ref, bf16[16384,2048]{1,0:T(8,128)(2,1)} %mat_hbm.7, f32[192,2048]{1,0:T(8,128)S(1)} %shard_map.94.before_ref), custom_call_target="tpu_custom_call" | custom-call | flops 3221225472 | bytes 16777216 | tf_op jit(solution)/shard_map/pallas_call | solution.py:109
  73.1 1.6 %collective-permute-start.22 = (bf16[24,4096]{1,0:T(8,128)(2,1)S(1)}, bf16[24,4096]{1,0:T(8,128)(2,1)S(1)}, u32[]{:S(2)}, u32[]{:S(2)}) collective-permute-start(bf16[24,4096]{1,0:T(8,128)(2,1)S(1)} %collective-permute-done.20), channel_id=1, source_target_pairs={{0,2},{2,4},{4,6},{6,7},{7,5},{5,3},{3,1},{1,0},{8,10},{10,12},{12... | collective-permute-start | bytes 589832 | tf_op jit(solution)/shard_map/ppermute | solution.py:180
  75.3 1.6 %collective-permute-start.8 = (bf16[24,4096]{1,0:T(8,128)(2,1)S(1)}, bf16[24,4096]{1,0:T(8,128)(2,1)S(1)}, u32[]{:S(2)}, u32[]{:S(2)}) collective-permute-start(bf16[24,4096]{1,0:T(8,128)(2,1)S(1)} %collective-permute-done.6), channel_id=1, source_target_pairs={{0,2},{2,4},{4,6},{6,7},{7,5},{5,3},{3,1},{1,0},{8,10},{10,12},{12... | collective-permute-start | bytes 589832 | tf_op jit(solution)/shard_map/ppermute | solution.py:180
  77.5 3.4 %collective-permute-done.22 = bf16[24,4096]{1,0:T(8,128)(2,1)S(1)} collective-permute-done((bf16[24,4096]{1,0:T(8,128)(2,1)S(1)}, bf16[24,4096]{1,0:T(8,128)(2,1)S(1)}, u32[]{:S(2)}, u32[]{:S(2)}) %collective-permute-start.22) | collective-permute-done | bytes 196640 | tf_op jit(solution)/shard_map/ppermute | solution.py:180
  83.0 2.1 %collective-permute-done.8 = bf16[24,4096]{1,0:T(8,128)(2,1)S(1)} collective-permute-done((bf16[24,4096]{1,0:T(8,128)(2,1)S(1)}, bf16[24,4096]{1,0:T(8,128)(2,1)S(1)}, u32[]{:S(2)}, u32[]{:S(2)}) %collective-permute-start.8) | collective-permute-done | bytes 196640 | tf_op jit(solution)/shard_map/ppermute | solution.py:180
  87.2 2.1 %collective-permute-done.24 = bf16[24,4096]{1,0:T(8,128)(2,1)S(1)} collective-permute-done((bf16[24,4096]{1,0:T(8,128)(2,1)S(1)}, bf16[24,4096]{1,0:T(8,128)(2,1)S(1)}, u32[]{:S(2)}, u32[]{:S(2)}) %collective-permute-start.24) | collective-permute-done | bytes 196640 | tf_op jit(solution)/shard_map/ppermute | solution.py:180
  89.3 1.6 %collective-permute-start.26 = (bf16[24,2048]{1,0:T(8,128)(2,1)S(1)}, bf16[24,2048]{1,0:T(8,128)(2,1)S(1)}, u32[]{:S(2)}, u32[]{:S(2)}) collective-permute-start(bf16[24,2048]{1,0:T(8,128)(2,1)S(1)} %slice.68), channel_id=1, source_target_pairs={{0,2},{2,4},{4,6},{6,7},{7,5},{5,3},{3,1},{1,0},{8,10},{10,12},{12... | collective-permute-start | bytes 294920 | tf_op jit(solution)/shard_map/ppermute | solution.py:187
  91.5 2.0 %collective-permute-done.10 = bf16[24,4096]{1,0:T(8,128)(2,1)S(1)} collective-permute-done((bf16[24,4096]{1,0:T(8,128)(2,1)S(1)}, bf16[24,4096]{1,0:T(8,128)(2,1)S(1)}, u32[]{:S(2)}, u32[]{:S(2)}) %collective-permute-start.10) | collective-permute-done | bytes 196640 | tf_op jit(solution)/shard_map/ppermute | solution.py:180
  98.2 1.9 %collective-permute-done.13 = bf16[24,2048]{1,0:T(8,128)(2,1)S(1)} collective-permute-done((bf16[24,2048]{1,0:T(8,128)(2,1)S(1)}, bf16[24,2048]{1,0:T(8,128)(2,1)S(1)}, u32[]{:S(2)}, u32[]{:S(2)}) %collective-permute-start.13) | collective-permute-done | bytes 98336 | tf_op jit(solution)/shard_map/ppermute | solution.py:188
  102.0 6.5 %shard_map.96.before_ref = f32[192,2048]{1,0:T(8,128)S(1)} custom-call(bf16[192,4096]{1,0:T(8,128)(2,1)S(1)} %maximum_dynamic-update-slice_fusion.1.rows_ref, bf16[16384,2048]{1,0:T(8,128)(2,1)} %mat_hbm.7, f32[192,2048]{1,0:T(8,128)S(1)} %shard_map.95.before_ref), custom_call_target="tpu_custom_call" | custom-call | flops 3221225472 | bytes 16777216 | tf_op jit(solution)/shard_map/pallas_call | solution.py:109
  109.3 3.1 %collective-permute-done.33 = bf16[192,1024]{1,0:T(8,128)(2,1)S(1)} collective-permute-done((bf16[192,1024]{1,0:T(8,128)(2,1)S(1)}, bf16[192,1024]{1,0:T(8,128)(2,1)S(1)}, u32[]{:S(2)}, u32[]{:S(2)}) %collective-permute-start.33) | collective-permute-done | bytes 393248 | tf_op jit(solution)/shard_map/ppermute | solution.py:139
  112.5 7.8 %collective-permute-done.35 = bf16[192,1024]{1,0:T(8,128)(2,1)S(1)} collective-permute-done((bf16[192,1024]{1,0:T(8,128)(2,1)S(1)}, bf16[192,1024]{1,0:T(8,128)(2,1)S(1)}, u32[]{:S(2)}, u32[]{:S(2)}) %collective-permute-start.35) | collective-permute-done | bytes 393248 | tf_op jit(solution)/shard_map/ppermute | solution.py:139
  120.6 8.4 %shard_map.97 = f32[192,576]{1,0:T(8,128)S(1)} custom-call(s32[8]{0:T(128)S(1)} %gather_fusion, bf16[192,4096]{1,0:T(8,128)(2,1)S(1)} %maximum_dynamic-update-slice_fusion.rows_ref, bf16[16384,2048]{1,0:T(8,128)(2,1)} %mat_hbm.7, f32[192,2048]{1,0:T(8,128)S(1)} %shard_map.96.before_ref, bf16[192,2048]{1,0:T(8,128)(2,1)S(1)} %pad_maximum_fusion.own_ref, ...), custom_call_target="tpu_custom_call" | custom-call | flops 3221225472 | bytes 16777216 | tf_op jit(solution)/shard_map/pallas_call | solution.py:118
  129.5 7.1 %collective-permute-done.36 = f32[4,24,576]{2,1,0:T(8,128)S(1)} collective-permute-done((f32[4,24,576]{2,1,0:T(8,128)S(1)}, f32[4,24,576]{2,1,0:T(8,128)S(1)}, u32[]{:S(2)}, u32[]{:S(2)}) %collective-permute-start.36) | collective-permute-done | bytes 221216 | tf_op jit(solution)/shard_map/ppermute | solution.py:214
  136.7 1.7 %collective-permute-start.37 = (f32[2,24,576]{2,1,0:T(8,128)S(1)}, f32[2,24,576]{2,1,0:T(8,128)S(1)}, u32[]{:S(2)}, u32[]{:S(2)}) collective-permute-start(f32[2,24,576]{2,1,0:T(8,128)S(1)} %dynamic-slice_bitcast_fusion.1), channel_id=1, source_target_pairs={{0,2},{1,3},{2,0},{3,1},{4,6},{5,7},{6,4},{7,5},{8,10},{9,11},{10,... | collective-permute-start | bytes 331784 | tf_op jit(solution)/shard_map/ppermute | solution.py:214
  138.4 3.3 %collective-permute-done.37 = f32[2,24,576]{2,1,0:T(8,128)S(1)} collective-permute-done((f32[2,24,576]{2,1,0:T(8,128)S(1)}, f32[2,24,576]{2,1,0:T(8,128)S(1)}, u32[]{:S(2)}, u32[]{:S(2)}) %collective-permute-start.37) | collective-permute-done | bytes 110624 | tf_op jit(solution)/shard_map/ppermute | solution.py:214
  141.7 2.3 %collective-permute-start.38 = (f32[1,24,576]{2,1,0:T(8,128)S(1)}, f32[1,24,576]{2,1,0:T(8,128)S(1)}, u32[]{:S(2)}, u32[]{:S(2)}) collective-permute-start(f32[1,24,576]{2,1,0:T(8,128)S(1)} %constant_dynamic-slice_fusion), channel_id=1, source_target_pairs={{0,4},{1,5},{2,6},{3,7},{4,0},{5,1},{6,2},{7,3},{8,12},{9,13},{10,... | collective-permute-start | bytes 165896 | tf_op jit(solution)/shard_map/ppermute | solution.py:214
  147.6 5.3 %all-gather = f32[96,192]{1,0:T(8,128)S(1)} all-gather(f32[24,192]{1,0:T(8,128)S(1)} %get-tuple-element.13), channel_id=2, replica_groups=mesh['grp'=4,'wide'=8] {'grp'}, dimensions={0}, use_global_device_ids=true | all-gather | bytes 92160 | tf_op jit(solution)/shard_map/all_gather | solution.py:219
  (135 shorter events, 39.2 us)
Async XLA Ops:
  7.4 13.0 %collective-permute-start = (bf16[24,4096]{1,0:T(8,128)(2,1)}, bf16[24,4096]{1,0:T(8,128)(2,1)}, u32[]{:S(2)}, u32[]{:S(2)}) collective-permute-start(bf16[24,4096]{1,0:T(8,128)(2,1)} %bitcast.15), channel_id=1, source_target_pairs={{0,2},{2,4},{4,6},{6,7},{7,5},{5,3},{3,1},{1,0},{8,10},{10,12},{12... | collective-permute-start | bytes 589832 | tf_op jit(solution)/shard_map/ppermute | solution.py:180
  10.4 13.1 %collective-permute-start.3 = (bf16[24,4096]{1,0:T(8,128)(2,1)}, bf16[24,4096]{1,0:T(8,128)(2,1)}, u32[]{:S(2)}, u32[]{:S(2)}) collective-permute-start(bf16[24,4096]{1,0:T(8,128)(2,1)} %bitcast.15), channel_id=1, source_target_pairs={{2,0},{4,2},{6,4},{7,6},{5,7},{3,5},{1,3},{0,1},{10,8},{12,10},{14... | collective-permute-start | bytes 589832 | tf_op jit(solution)/shard_map/ppermute | solution.py:180
  11.2 13.4 %collective-permute-start.14 = (bf16[24,4096]{1,0:T(8,128)(2,1)}, bf16[24,4096]{1,0:T(8,128)(2,1)}, u32[]{:S(2)}, u32[]{:S(2)}) collective-permute-start(bf16[24,4096]{1,0:T(8,128)(2,1)} %bitcast.19), channel_id=1, source_target_pairs={{0,2},{2,4},{4,6},{6,7},{7,5},{5,3},{3,1},{1,0},{8,10},{10,12},{12... | collective-permute-start | bytes 589832 | tf_op jit(solution)/shard_map/ppermute | solution.py:180
  13.2 14.4 %collective-permute-start.17 = (bf16[24,4096]{1,0:T(8,128)(2,1)}, bf16[24,4096]{1,0:T(8,128)(2,1)}, u32[]{:S(2)}, u32[]{:S(2)}) collective-permute-start(bf16[24,4096]{1,0:T(8,128)(2,1)} %bitcast.19), channel_id=1, source_target_pairs={{2,0},{4,2},{6,4},{7,6},{5,7},{3,5},{1,3},{0,1},{10,8},{12,10},{14... | collective-permute-start | bytes 589832 | tf_op jit(solution)/shard_map/ppermute | solution.py:180
  20.4 8.2 %collective-permute-start.1 = (bf16[24,4096]{1,0:T(8,128)(2,1)}, bf16[24,4096]{1,0:T(8,128)(2,1)S(1)}, u32[]{:S(2)}, u32[]{:S(2)}) collective-permute-start(bf16[24,4096]{1,0:T(8,128)(2,1)} %collective-permute-done), channel_id=1, source_target_pairs={{0,2},{2,4},{4,6},{6,7},{7,5},{5,3},{3,1},{1,0},{8,10},{10,12},{12... | collective-permute-start | bytes 589832 | tf_op jit(solution)/shard_map/ppermute | solution.py:180
  23.5 7.2 %collective-permute-start.4 = (bf16[24,4096]{1,0:T(8,128)(2,1)}, bf16[24,4096]{1,0:T(8,128)(2,1)S(1)}, u32[]{:S(2)}, u32[]{:S(2)}) collective-permute-start(bf16[24,4096]{1,0:T(8,128)(2,1)} %collective-permute-done.3), channel_id=1, source_target_pairs={{2,0},{4,2},{6,4},{7,6},{5,7},{3,5},{1,3},{0,1},{10,8},{12,10},{14... | collective-permute-start | bytes 589832 | tf_op jit(solution)/shard_map/ppermute | solution.py:180
  24.5 7.7 %collective-permute-start.15 = (bf16[24,4096]{1,0:T(8,128)(2,1)}, bf16[24,4096]{1,0:T(8,128)(2,1)S(1)}, u32[]{:S(2)}, u32[]{:S(2)}) collective-permute-start(bf16[24,4096]{1,0:T(8,128)(2,1)} %collective-permute-done.14), channel_id=1, source_target_pairs={{0,2},{2,4},{4,6},{6,7},{7,5},{5,3},{3,1},{1,0},{8,10},{10,12},{12... | collective-permute-start | bytes 589832 | tf_op jit(solution)/shard_map/ppermute | solution.py:180
  27.6 8.1 %collective-permute-start.18 = (bf16[24,4096]{1,0:T(8,128)(2,1)}, bf16[24,4096]{1,0:T(8,128)(2,1)S(1)}, u32[]{:S(2)}, u32[]{:S(2)}) collective-permute-start(bf16[24,4096]{1,0:T(8,128)(2,1)} %collective-permute-done.17), channel_id=1, source_target_pairs={{2,0},{4,2},{6,4},{7,6},{5,7},{3,5},{1,3},{0,1},{10,8},{12,10},{14... | collective-permute-start | bytes 589832 | tf_op jit(solution)/shard_map/ppermute | solution.py:180
  28.6 15.5 %collective-permute-start.2 = (bf16[24,4096]{1,0:T(8,128)(2,1)S(1)}, bf16[24,4096]{1,0:T(8,128)(2,1)S(1)}, u32[]{:S(2)}, u32[]{:S(2)}) collective-permute-start(bf16[24,4096]{1,0:T(8,128)(2,1)S(1)} %collective-permute-done.1), channel_id=1, source_target_pairs={{0,2},{2,4},{4,6},{6,7},{7,5},{5,3},{3,1},{1,0},{8,10},{10,12},{12... | collective-permute-start | bytes 589832 | tf_op jit(solution)/shard_map/ppermute | solution.py:180
  30.7 13.4 %collective-permute-start.5 = (bf16[24,4096]{1,0:T(8,128)(2,1)S(1)}, bf16[24,4096]{1,0:T(8,128)(2,1)S(1)}, u32[]{:S(2)}, u32[]{:S(2)}) collective-permute-start(bf16[24,4096]{1,0:T(8,128)(2,1)S(1)} %collective-permute-done.4), channel_id=1, source_target_pairs={{2,0},{4,2},{6,4},{7,6},{5,7},{3,5},{1,3},{0,1},{10,8},{12,10},{14... | collective-permute-start | bytes 589832 | tf_op jit(solution)/shard_map/ppermute | solution.py:180
  32.3 6.9 %collective-permute-start.16 = (bf16[24,4096]{1,0:T(8,128)(2,1)S(1)}, bf16[24,4096]{1,0:T(8,128)(2,1)S(1)}, u32[]{:S(2)}, u32[]{:S(2)}) collective-permute-start(bf16[24,4096]{1,0:T(8,128)(2,1)S(1)} %collective-permute-done.15), channel_id=1, source_target_pairs={{0,2},{2,4},{4,6},{6,7},{7,5},{5,3},{3,1},{1,0},{8,10},{10,12},{12... | collective-permute-start | bytes 589832 | tf_op jit(solution)/shard_map/ppermute | solution.py:180
  35.7 6.4 %collective-permute-start.19 = (bf16[24,4096]{1,0:T(8,128)(2,1)S(1)}, bf16[24,4096]{1,0:T(8,128)(2,1)S(1)}, u32[]{:S(2)}, u32[]{:S(2)}) collective-permute-start(bf16[24,4096]{1,0:T(8,128)(2,1)S(1)} %collective-permute-done.18), channel_id=1, source_target_pairs={{2,0},{4,2},{6,4},{7,6},{5,7},{3,5},{1,3},{0,1},{10,8},{12,10},{14... | collective-permute-start | bytes 589832 | tf_op jit(solution)/shard_map/ppermute | solution.py:180
  42.1 31.0 %collective-permute-start.20 = (bf16[24,4096]{1,0:T(8,128)(2,1)S(1)}, bf16[24,4096]{1,0:T(8,128)(2,1)S(1)}, u32[]{:S(2)}, u32[]{:S(2)}) collective-permute-start(bf16[24,4096]{1,0:T(8,128)(2,1)S(1)} %bitcast.37), channel_id=1, source_target_pairs={{0,2},{2,4},{4,6},{6,7},{7,5},{5,3},{3,1},{1,0},{8,10},{10,12},{12... | collective-permute-start | bytes 589832 | tf_op jit(solution)/shard_map/ppermute | solution.py:180
  43.7 31.1 %collective-permute-start.21 = (bf16[24,4096]{1,0:T(8,128)(2,1)S(1)}, bf16[24,4096]{1,0:T(8,128)(2,1)S(1)}, u32[]{:S(2)}, u32[]{:S(2)}) collective-permute-start(bf16[24,4096]{1,0:T(8,128)(2,1)S(1)} %bitcast.39), channel_id=1, source_target_pairs={{2,0},{4,2},{6,4},{7,6},{5,7},{3,5},{1,3},{0,1},{10,8},{12,10},{14... | collective-permute-start | bytes 589832 | tf_op jit(solution)/shard_map/ppermute | solution.py:180
  44.2 31.1 %collective-permute-start.6 = (bf16[24,4096]{1,0:T(8,128)(2,1)S(1)}, bf16[24,4096]{1,0:T(8,128)(2,1)S(1)}, u32[]{:S(2)}, u32[]{:S(2)}) collective-permute-start(bf16[24,4096]{1,0:T(8,128)(2,1)S(1)} %bitcast.34), channel_id=1, source_target_pairs={{0,2},{2,4},{4,6},{6,7},{7,5},{5,3},{3,1},{1,0},{8,10},{10,12},{12... | collective-permute-start | bytes 589832 | tf_op jit(solution)/shard_map/ppermute | solution.py:180
  45.8 7.7 %collective-permute-start.28 = (bf16[24,2048]{1,0:T(8,128)(2,1)S(1)}, bf16[24,2048]{1,0:T(8,128)(2,1)S(1)}, u32[]{:S(2)}, u32[]{:S(2)}) collective-permute-start(bf16[24,2048]{1,0:T(8,128)(2,1)S(1)} %slice.70), channel_id=1, source_target_pairs={{0,2},{2,4},{4,6},{6,7},{7,5},{5,3},{3,1},{1,0},{8,10},{10,12},{12... | collective-permute-start | bytes 294920 | tf_op jit(solution)/shard_map/ppermute | solution.py:187
  47.4 7.6 %collective-permute-start.29 = (bf16[24,2048]{1,0:T(8,128)(2,1)S(1)}, bf16[24,2048]{1,0:T(8,128)(2,1)S(1)}, u32[]{:S(2)}, u32[]{:S(2)}) collective-permute-start(bf16[24,2048]{1,0:T(8,128)(2,1)S(1)} %slice.71), channel_id=1, source_target_pairs={{2,0},{4,2},{6,4},{7,6},{5,7},{3,5},{1,3},{0,1},{10,8},{12,10},{14... | collective-permute-start | bytes 294920 | tf_op jit(solution)/shard_map/ppermute | solution.py:188
  58.1 18.9 %collective-permute-start.7 = (bf16[24,4096]{1,0:T(8,128)(2,1)S(1)}, bf16[24,4096]{1,0:T(8,128)(2,1)S(1)}, u32[]{:S(2)}, u32[]{:S(2)}) collective-permute-start(bf16[24,4096]{1,0:T(8,128)(2,1)S(1)} %bitcast.36), channel_id=1, source_target_pairs={{2,0},{4,2},{6,4},{7,6},{5,7},{3,5},{1,3},{0,1},{10,8},{12,10},{14... | collective-permute-start | bytes 589832 | tf_op jit(solution)/shard_map/ppermute | solution.py:180
  60.0 40.3 %collective-permute-start.32 = (bf16[192,1024]{1,0:T(8,128)(2,1)S(1)}, bf16[192,1024]{1,0:T(8,128)(2,1)S(1)}, u32[]{:S(2)}, u32[]{:S(2)}) collective-permute-start(bf16[192,1024]{1,0:T(8,128)(2,1)S(1)} %pad_maximum_fusion.2), channel_id=1, source_target_pairs={{0,8},{8,0},{16,24},{24,16},{1,9},{9,1},{17,25},{25,17},{2,10},{10... | collective-permute-start | bytes 1179656 | tf_op jit(solution)/shard_map/ppermute | solution.py:136
  73.1 7.7 %collective-permute-start.22 = (bf16[24,4096]{1,0:T(8,128)(2,1)S(1)}, bf16[24,4096]{1,0:T(8,128)(2,1)S(1)}, u32[]{:S(2)}, u32[]{:S(2)}) collective-permute-start(bf16[24,4096]{1,0:T(8,128)(2,1)S(1)} %collective-permute-done.20), channel_id=1, source_target_pairs={{0,2},{2,4},{4,6},{6,7},{7,5},{5,3},{3,1},{1,0},{8,10},{10,12},{12... | collective-permute-start | bytes 589832 | tf_op jit(solution)/shard_map/ppermute | solution.py:180
  74.7 7.8 %collective-permute-start.23 = (bf16[24,4096]{1,0:T(8,128)(2,1)S(1)}, bf16[24,4096]{1,0:T(8,128)(2,1)S(1)}, u32[]{:S(2)}, u32[]{:S(2)}) collective-permute-start(bf16[24,4096]{1,0:T(8,128)(2,1)S(1)} %collective-permute-done.21), channel_id=1, source_target_pairs={{2,0},{4,2},{6,4},{7,6},{5,7},{3,5},{1,3},{0,1},{10,8},{12,10},{14... | collective-permute-start | bytes 589832 | tf_op jit(solution)/shard_map/ppermute | solution.py:180
  75.3 9.8 %collective-permute-start.8 = (bf16[24,4096]{1,0:T(8,128)(2,1)S(1)}, bf16[24,4096]{1,0:T(8,128)(2,1)S(1)}, u32[]{:S(2)}, u32[]{:S(2)}) collective-permute-start(bf16[24,4096]{1,0:T(8,128)(2,1)S(1)} %collective-permute-done.6), channel_id=1, source_target_pairs={{0,2},{2,4},{4,6},{6,7},{7,5},{5,3},{3,1},{1,0},{8,10},{10,12},{12... | collective-permute-start | bytes 589832 | tf_op jit(solution)/shard_map/ppermute | solution.py:180
  76.9 9.8 %collective-permute-start.9 = (bf16[24,4096]{1,0:T(8,128)(2,1)S(1)}, bf16[24,4096]{1,0:T(8,128)(2,1)S(1)}, u32[]{:S(2)}, u32[]{:S(2)}) collective-permute-start(bf16[24,4096]{1,0:T(8,128)(2,1)S(1)} %collective-permute-done.7), channel_id=1, source_target_pairs={{2,0},{4,2},{6,4},{7,6},{5,7},{3,5},{1,3},{0,1},{10,8},{12,10},{14... | collective-permute-start | bytes 589832 | tf_op jit(solution)/shard_map/ppermute | solution.py:180
  80.9 8.4 %collective-permute-start.24 = (bf16[24,4096]{1,0:T(8,128)(2,1)S(1)}, bf16[24,4096]{1,0:T(8,128)(2,1)S(1)}, u32[]{:S(2)}, u32[]{:S(2)}) collective-permute-start(bf16[24,4096]{1,0:T(8,128)(2,1)S(1)} %collective-permute-done.22), channel_id=1, source_target_pairs={{0,2},{2,4},{4,6},{6,7},{7,5},{5,3},{3,1},{1,0},{8,10},{10,12},{12... | collective-permute-start | bytes 589832 | tf_op jit(solution)/shard_map/ppermute | solution.py:180
  82.5 8.4 %collective-permute-start.25 = (bf16[24,4096]{1,0:T(8,128)(2,1)S(1)}, bf16[24,4096]{1,0:T(8,128)(2,1)S(1)}, u32[]{:S(2)}, u32[]{:S(2)}) collective-permute-start(bf16[24,4096]{1,0:T(8,128)(2,1)S(1)} %collective-permute-done.23), channel_id=1, source_target_pairs={{2,0},{4,2},{6,4},{7,6},{5,7},{3,5},{1,3},{0,1},{10,8},{12,10},{14... | collective-permute-start | bytes 589832 | tf_op jit(solution)/shard_map/ppermute | solution.py:180
  85.1 8.4 %collective-permute-start.10 = (bf16[24,4096]{1,0:T(8,128)(2,1)S(1)}, bf16[24,4096]{1,0:T(8,128)(2,1)S(1)}, u32[]{:S(2)}, u32[]{:S(2)}) collective-permute-start(bf16[24,4096]{1,0:T(8,128)(2,1)S(1)} %collective-permute-done.8), channel_id=1, source_target_pairs={{0,2},{2,4},{4,6},{6,7},{7,5},{5,3},{3,1},{1,0},{8,10},{10,12},{12... | collective-permute-start | bytes 589832 | tf_op jit(solution)/shard_map/ppermute | solution.py:180
  86.7 8.4 %collective-permute-start.11 = (bf16[24,4096]{1,0:T(8,128)(2,1)S(1)}, bf16[24,4096]{1,0:T(8,128)(2,1)S(1)}, u32[]{:S(2)}, u32[]{:S(2)}) collective-permute-start(bf16[24,4096]{1,0:T(8,128)(2,1)S(1)} %collective-permute-done.9), channel_id=1, source_target_pairs={{2,0},{4,2},{6,4},{7,6},{5,7},{3,5},{1,3},{0,1},{10,8},{12,10},{14... | collective-permute-start | bytes 589832 | tf_op jit(solution)/shard_map/ppermute | solution.py:180
  89.3 6.7 %collective-permute-start.26 = (bf16[24,2048]{1,0:T(8,128)(2,1)S(1)}, bf16[24,2048]{1,0:T(8,128)(2,1)S(1)}, u32[]{:S(2)}, u32[]{:S(2)}) collective-permute-start(bf16[24,2048]{1,0:T(8,128)(2,1)S(1)} %slice.68), channel_id=1, source_target_pairs={{0,2},{2,4},{4,6},{6,7},{7,5},{5,3},{3,1},{1,0},{8,10},{10,12},{12... | collective-permute-start | bytes 294920 | tf_op jit(solution)/shard_map/ppermute | solution.py:187
  100.2 8.3 %collective-permute-start.34 = (bf16[192,1024]{1,0:T(8,128)(2,1)S(1)}, bf16[192,1024]{1,0:T(8,128)(2,1)S(1)}, u32[]{:S(2)}, u32[]{:S(2)}) collective-permute-start(bf16[192,1024]{1,0:T(8,128)(2,1)S(1)} %pad_maximum_fusion.3), channel_id=1, source_target_pairs={{0,8},{8,0},{16,24},{24,16},{1,9},{9,1},{17,25},{25,17},{2,10},{10... | collective-permute-start | bytes 1179656 | tf_op jit(solution)/shard_map/ppermute | solution.py:136
  100.4 12.0 %collective-permute-start.33 = (bf16[192,1024]{1,0:T(8,128)(2,1)S(1)}, bf16[192,1024]{1,0:T(8,128)(2,1)S(1)}, u32[]{:S(2)}, u32[]{:S(2)}) collective-permute-start(bf16[192,1024]{1,0:T(8,128)(2,1)S(1)} %broadcast_select_fusion.1), channel_id=1, source_target_pairs={{0,16},{8,24},{16,0},{24,8},{1,17},{9,25},{17,1},{25,9},{2,18},{10... | collective-permute-start | bytes 1179656 | tf_op jit(solution)/shard_map/ppermute | solution.py:139
  108.6 11.7 %collective-permute-start.35 = (bf16[192,1024]{1,0:T(8,128)(2,1)S(1)}, bf16[192,1024]{1,0:T(8,128)(2,1)S(1)}, u32[]{:S(2)}, u32[]{:S(2)}) collective-permute-start(bf16[192,1024]{1,0:T(8,128)(2,1)S(1)} %broadcast_select_fusion), channel_id=1, source_target_pairs={{0,16},{8,24},{16,0},{24,8},{1,17},{9,25},{17,1},{25,9},{2,18},{10... | collective-permute-start | bytes 1179656 | tf_op jit(solution)/shard_map/ppermute | solution.py:139
  129.0 7.6 %collective-permute-start.36 = (f32[4,24,576]{2,1,0:T(8,128)S(1)}, f32[4,24,576]{2,1,0:T(8,128)S(1)}, u32[]{:S(2)}, u32[]{:S(2)}) collective-permute-start(f32[4,24,576]{2,1,0:T(8,128)S(1)} %dynamic-slice_bitcast_fusion), channel_id=1, source_target_pairs={{0,1},{1,0},{2,3},{3,2},{4,5},{5,4},{6,7},{7,6},{8,9},{9,8},{10,11... | collective-permute-start | bytes 663560 | tf_op jit(solution)/shard_map/ppermute | solution.py:214
  (12 other events, 107.0 us)

commit v2 on v0

v2 whole, which is shorter than its diff:
```python
import functools
import math

import jax
import jax.numpy as jnp
from jax import lax
from jax.experimental import pallas as pl
from jax.experimental.pallas import tpu as pltpu
from jax.sharding import PartitionSpec as P

CHUNKS = 4
VMEM_LIMIT = 28 * 2**20
WHOLE = pl.BlockSpec(memory_space=pltpu.VMEM)
SCALARS = pl.BlockSpec(memory_space=pltpu.SMEM)
HBM = pl.BlockSpec(memory_space=pl.ANY)


def call(kernel, out_shape, in_specs, scratch=(), flops=0, moved=0):
    return pl.pallas_call(
        kernel,
        in_specs=in_specs,
        out_specs=jax.tree.map(lambda _: WHOLE, out_shape),
        out_shape=out_shape,
        scratch_shapes=list(scratch),
        compiler_params=pltpu.CompilerParams(vmem_limit_bytes=VMEM_LIMIT),
        cost_estimate=pl.CostEstimate(flops=flops, bytes_accessed=moved, transcendentals=0),
    )


def contract(left, right):
    return lax.dot_general(
        left, right, (((1,), (1,)), ((), ())), preferred_element_type=jnp.float32
    )


def stack(blocks):
    return jnp.concatenate([b.astype(jnp.float32) for b in blocks], axis=0).astype(jnp.bfloat16)


def ring_member(place, n):
    return jnp.where(place < n // 2, 2 * place, 2 * (n - 1 - place) + 1)


def snake(n):
    return list(range(0, n, 2)) + list(range(n - 1, 0, -2))


def offsets(n):
    found = [0]
    for s in range(1, n // 2):
        found += [-s, s]
    return found + [n // 2]


def cut_kernel(n, exponents_ref, codes_ref, *out_refs):
    rows, width = codes_ref.shape
    depth = width // (n * CHUNKS)
    line = lax.broadcasted_iota(jnp.int32, (rows, 128), 0)
    power = jnp.zeros((rows, 128), jnp.int32)
    for r in range(rows):
        power = jnp.where(line == r, exponents_ref[r], power)
    scale = jnp.where(power < 0, jnp.where(power < -1, 0.25, 0.5), jnp.where(power > 0, 2.0, 1.0))
    for k, out_ref in enumerate(out_refs):
        for w in range(n):
            for part in range(0, depth, 128):
                start = (w * CHUNKS + k) * depth + part
                block = codes_ref[:, start : start + 128].astype(jnp.float32) * scale
                out_ref[:, w * depth + part : w * depth + part + 128] = block.astype(jnp.bfloat16)


def cut(codes, exponents, n):
    rows, width = codes.shape
    piece = jax.ShapeDtypeStruct((rows, width // CHUNKS), jnp.bfloat16)
    return call(functools.partial(cut_kernel, n), [piece] * CHUNKS, [SCALARS, WHOLE])(
        exponents, codes
    )


def slab_kernel(depth, per, *refs):
    out_ref = refs[-1]
    me = lax.axis_index("wide")
    columns = pl.ds(pl.multiple_of(me * depth, depth), depth)
    for at, ref in enumerate(refs[:-1]):
        chunk, i = divmod(at, per)
        out_ref[i, :, chunk * depth : (chunk + 1) * depth] = ref[:, columns]


def slabs(chunks, n):
    rows, width = chunks[0][0].shape
    depth = width // n
    out = jax.ShapeDtypeStruct((n, rows, depth * len(chunks)), jnp.bfloat16)
    flat = [p for c in chunks for p in c]
    return call(functools.partial(slab_kernel, depth, n), out, [WHOLE] * len(flat))(*flat)


def accumulate(chunk, first, piece_refs, mat_hbm, buf, sem, rows, total_ref):
    count, depth, cols = buf.shape
    copies = []
    for w in range(count):
        cuts = 2 if w in (0, count - 1) and depth % 32 == 0 and depth > 256 else 1
        for part in range(cuts):
            size = depth // cuts
            start = ((first + w) * CHUNKS + chunk) * depth + part * size
            target = buf.at[w, pl.ds(part * size, size)]
            at = len(copies)
            copy = pltpu.make_async_copy(mat_hbm.at[pl.ds(start, size)], target, sem.at[at])
            copy.start()
            copies.append((w, part * size, size, copy))
    rows[...] = stack([ref[:, first * depth : (first + count) * depth] for ref in piece_refs])
    while copies:
        w, inner, size, copy = copies.pop(0)
        copy.wait()
        begin = w * depth + inner
        total_ref[...] += jnp.dot(
            rows[:, begin : begin + size], buf[w, inner : inner + size], preferred_element_type=jnp.float32
        )


def part_kernel(chunk, first, n, fresh, *refs):
    pieces, (mat_hbm, before_ref), (total_ref, buf, sem, rows) = refs[:n], refs[n : n + 2], refs[-4:]
    total_ref[...] = jnp.zeros_like(total_ref) if fresh else before_ref[...]
    accumulate(chunk, first, pieces, mat_hbm, buf, sem, rows, total_ref)


def contract_kernel(n, partner_ref, *refs):
    total_ref, own_refs, other_refs = refs[0], refs[1:3], refs[3:9]
    cross_ref, pair_ref, held, placed, chosen = refs[9:]
    image = total_ref[...].astype(jnp.bfloat16)
    size = image.shape[0]
    step = size // n
    me = lax.axis_index("wide")
    group = lax.axis_index("grp")
    place = jnp.where(me % 2 == 0, me // 2, n - 1 - me // 2)
    which = partner_ref[group]

    def reorder(block):
        held[...] = block
        for i, hop in enumerate(offsets(n)):
            to = ring_member(lax.rem(place + hop + n, n), n)
            placed[pl.ds(pl.multiple_of(to * step, 8), step), :] = held[i * step : (i + 1) * step, :]
        return placed[...]

    width = own_refs[0].shape[2]
    own = [stack([ref[i] for i in range(n)]) for ref in own_refs]
    diag = sum(contract(image[:, k * width : (k + 1) * width], own[k]) for k in range(2))
    for k in range(2):
        for flip, ref in enumerate((own_refs[k], *other_refs[3 * k : 3 * k + 3])):

            @pl.when(which == group ^ flip)
            def _():
                chosen[:, k * width : (k + 1) * width] = stack([ref[i] for i in range(n)])

    pair = contract(image, chosen[...])
    back = reorder(reorder(pair).T)
    pair_ref[...] = back
    cross_ref[:, :size] = reorder(reorder(diag).T).T
    cross_ref[:, size:] = back.T


def contractions(partner, total, own, other, n):
    size, cols = total.shape
    out = [
        jax.ShapeDtypeStruct((size, 2 * size), jnp.float32),
        jax.ShapeDtypeStruct((size, size), jnp.float32),
    ]
    square = pltpu.VMEM((size, size), jnp.float32)
    kernel = functools.partial(contract_kernel, n)
    scratch = [square, square, pltpu.VMEM((size, cols), jnp.bfloat16)]
    return call(kernel, out, [SCALARS] + [WHOLE] * 9, scratch)(partner, total, *own, *other)


def multiply(chunk, first, count, pieces, mat, before, later=()):
    n = len(pieces)
    rows, width = pieces[0].shape
    depth, size, cols = width // n, n * rows, mat.shape[1]
    total = jax.ShapeDtypeStruct((size, cols), jnp.float32)
    scratch = [
        pltpu.VMEM((count, depth, cols), mat.dtype),
        pltpu.SemaphoreType.DMA((count + 2,)),
        pltpu.VMEM((size, count * depth), jnp.bfloat16),
    ]
    flops = 2 * size * count * depth * cols * WEIGHT
    moved = 2 * count * depth * cols * WEIGHT
    fresh = before is None
    kernel = functools.partial(part_kernel, chunk, first, n, fresh)
    before = mat if fresh else before
    specs = [WHOLE] * n + [HBM, HBM if fresh else WHOLE] + [HBM] * len(later)
    return call(kernel, total, specs, scratch, flops, moved)(*pieces, mat, before, *later)


WEIGHT = 3


def after(value, *others):
    return lax.optimization_barrier((value, *others))[0]


def spread(value):
    far = lax.ppermute(value, "grp", [(i, i ^ 2) for i in range(4)])
    near = lax.ppermute(value, "grp", [(i, i ^ 1) for i in range(4)])
    return near, far


def relay(far):
    return lax.ppermute(far, "grp", [(i, i ^ 1) for i in range(4)])


def shards(codes, exponents, precond, partner, n):
    rows, width = codes.shape
    factor = 1.0 / math.sqrt(width)
    me = lax.axis_index("wide")
    group = lax.axis_index("grp")
    ring = snake(n)
    forth = [(ring[i], ring[(i + 1) % n]) for i in range(n)]
    back = [(ring[(i + 1) % n], ring[i]) for i in range(n)]

    def both_ways(lane):
        up, down, held = lane
        up, down = lax.ppermute(up, "wide", forth), lax.ppermute(down, "wide", back)
        return up, down, held + [up, down]

    def last_hops(lanes):
        one = lax.ppermute(lanes[0][0], "wide", forth)
        two = lax.ppermute(lanes[1][1], "wide", back)
        return lanes[0][2] + [one], lanes[1][2] + [two]

    parts = cut(codes, exponents, n)
    lanes = [(p, p, [p]) for p in parts[:2]]
    for _ in range(1, n // 2):
        lanes = [both_ways(lane) for lane in lanes]
    early = last_hops(lanes)
    starts = [after(p, *lane[:2]) for p, lane in zip(parts[2:], lanes)]
    lanes = [(p, p, [p]) for p in starts]

    first_own = slabs(early, n)
    first_near, first_far = spread(first_own)
    halves = [(k, h) for k in range(2) for h in range(2)]
    total = None
    steps = n // 2
    for s in range(1, steps):
        lanes = [both_ways(lane) for lane in lanes]
        while halves and len(halves) > 4 - -(-4 * s // steps):
            k, h = halves.pop(0)
            total = multiply(k, h * (n // 2), n // 2, early[k], precond, total)
        lanes = [(after(up, total), down, held) for up, down, held in lanes]
    late = last_hops(lanes)
    for k, h in halves:
        total = multiply(k, h * (n // 2), n // 2, early[k], precond, total)

    last_own = slabs([[after(p, total) for p in c] for c in late], n)
    last_near, last_far = spread(last_own)
    first_both = relay(first_far)
    total = multiply(2, 0, n, late[0], precond, total)
    total = multiply(3, 0, n // 2, late[1], precond, total)
    last_both = relay(last_far)
    total = multiply(3, n // 2, n // 2, late[1], precond, total)
    other = [first_near, first_far, first_both, last_near, last_far, last_both]
    cross, pair = contractions(partner, total, [first_own, last_own], other, n)

    sums = [block.reshape(n, rows, block.shape[1]) for block in (pair, cross)]
    bit = 1
    while bit < n:
        mine = (me // bit) % 2
        for at, block in enumerate(sums):
            pairs = block.reshape(block.shape[0] // 2, 2, *block.shape[1:])
            kept = lax.dynamic_index_in_dim(pairs, mine, 1, keepdims=False)
            given = lax.dynamic_index_in_dim(pairs, 1 - mine, 1, keepdims=False)
            sums[at] = kept + lax.ppermute(given, "wide", [(i, i ^ bit) for i in range(n)])
        bit *= 2
    size = n * rows
    cross = sums[1][0] * factor
    back_rows = sums[0][0] * factor
    kernel_back = back_rows
    for flip in (1, 2, 3):
        block = lax.ppermute(back_rows, "grp", [(i, i ^ flip) for i in range(4)])
        source = lax.dynamic_index_in_dim(partner, group ^ flip, 0, keepdims=False)
        kernel_back = jnp.where(source == group, block, kernel_back)
    return (cross[:, :size], cross[:, size:], kernel_back)


def solution(mesh):
    return jax.shard_map(
        functools.partial(shards, n=mesh.shape["wide"]),
        mesh=mesh,
        in_specs=(P(("grp", "wide"), None), P(("grp", "wide")), P(None, "wide"), P()),
        out_specs=(P(("grp", "wide"), None), P(("grp", "wide"), None), P(("grp", "wide"), None)),
        check_vma=False,
    )
```

time: 340 us -> 113 us (0.33)
  waiting for transfers between devices: 276 us -> 25.8 us
  starting transfers between devices: 0.21 us -> 46.2 us
  Pallas kernels: 0 us -> 33.9 us
  matrix products: 33.7 us -> 0 us
  between operations: 15.8 us -> 2.93 us
  other arithmetic: 6.26 us -> 0.68 us
  blocking collectives: 5.53 us -> 0 us
    reduce_scatter x3 -> x0, waiting for transfers between devices: 174 us -> none  [the longest x1 59.7 us: shards(): lax.psum_scatter(contract(other_cols, image), 'wide', scatter_dimension=0...]
    all_gather x2 -> x0, waiting for transfers between devices: 102 us -> none  [the longest x1 102 us: shards(): piece = lax.all_gather(scaled, 'wide', axis=0, tiled=True)]
    ppermute x0 -> x43, starting transfers between devices: none -> 46.2 us  [the longest x12 15.8 us: both_ways(): lax.ppermute(down, 'wide', back)]
    pallas_call x0 -> x11, Pallas kernels: none -> 33.9 us  [the longest x7 30.8 us: multiply(): call(kernel, total, specs, scratch, flops, moved)]
    dot_general x4 -> x0, matrix products: 33.7 us -> none  [the longest x1 28.2 us: shards(): jnp.dot(piece, precond, preferred_element_type=jnp.float32)]
    ppermute x0 -> x43, waiting for transfers between devices: none -> 25.8 us  [the longest x12 13.1 us: both_ways(): lax.ppermute(up, 'wide', forth)]
    all_gather x1 -> x0, blocking collectives: 5.53 us -> none  [shards(): returned = lax.all_gather(back_rows[None], 'grp', axis=0, tiled=True)]
  transfers between devices with their start and end apart: 5 -> 43, of which waited for: 4 -> 16; matrix products, arithmetic and copies ran while one was open for 11% -> 1% of each run, Pallas kernels for 0% -> 27%
where the time goes in v2:
time: 113 us
  starting transfers between devices  46.2 us (41%)
  Pallas kernels  33.9 us (30%)
  waiting for transfers between devices  25.8 us (23%)
  local copies, waits for them, and re-layouts  3.13 us (3%)
  between operations  2.93 us (3%)
    pallas_call x7, Pallas kernels, multiply(): call(kernel, total, specs, scratch, flops, moved)  30.8 us
    ppermute x12, starting transfers between devices, both_ways(): lax.ppermute(down, 'wide', back)  15.8 us
    ppermute x12, waiting for transfers between devices, both_ways(): lax.ppermute(up, 'wide', forth)  13.1 us
    ppermute x12, starting transfers between devices, both_ways(): lax.ppermute(up, 'wide', forth)  11.4 us
    ppermute x6, starting transfers between devices, shards(): lax.ppermute(given, 'wide', [(i, i ^ bit) for i in range(n)])  9.73 us
    ppermute x6, waiting for transfers between devices, shards(): lax.ppermute(given, 'wide', [(i, i ^ bit) for i in range(n)])  6.46 us
    ppermute x12, waiting for transfers between devices, both_ways(): lax.ppermute(down, 'wide', back)  5.18 us
    ppermute x2, starting transfers between devices, spread(): far = lax.ppermute(value, 'grp', [(i, i ^ 2) for i in range(4)])  2.49 us
  transfers between devices with their start and end apart: 43, of which 16 were waited for; matrix products, arithmetic and copies ran while one was open for 1% of the time, Pallas kernels for 27%

profile of v2, /device:TPU:0, one launch (start us, length us, event | category | flops | bytes accessed | tf_op | source)
XLA Modules:
  0.0 112.5 jit_solution(9751617774172498853)
XLA Ops:
  3.1 3.0 %collective-permute-start.3 = (bf16[24,4096]{1,0:T(8,128)(2,1)S(1)}, bf16[24,4096]{1,0:T(8,128)(2,1)S(1)}, u32[]{:S(2)}, u32[]{:S(2)}) collective-permute-start(bf16[24,4096]{1,0:T(8,128)(2,1)S(1)} %get-tuple-element.33.refs_0_.refs_8_), channel_id=1, source_target_pairs={{2,0},{4,2},{6,4},{7,6},{5,7},{3,5},{1,3},{0,1},{10,8},{12,10},{14... | collective-permute-start | bytes 589832 | tf_op jit(solution)/shard_map/ppermute | solution.py:219
  6.3 2.0 %collective-permute-start = (bf16[24,4096]{1,0:T(8,128)(2,1)S(1)}, bf16[24,4096]{1,0:T(8,128)(2,1)S(1)}, u32[]{:S(2)}, u32[]{:S(2)}) collective-permute-start(bf16[24,4096]{1,0:T(8,128)(2,1)S(1)} %get-tuple-element.33.refs_0_.refs_8_), channel_id=1, source_target_pairs={{0,2},{2,4},{4,6},{6,7},{7,5},{5,3},{3,1},{1,0},{8,10},{10,12},{12... | collective-permute-start | bytes 589832 | tf_op jit(solution)/shard_map/ppermute | solution.py:219
  8.3 3.6 %collective-permute-done.3.refs_2_.refs_10_ = bf16[24,4096]{1,0:T(8,128)(2,1)S(1)} collective-permute-done((bf16[24,4096]{1,0:T(8,128)(2,1)S(1)}, bf16[24,4096]{1,0:T(8,128)(2,1)S(1)}, u32[]{:S(2)}, u32[]{:S(2)}) %collective-permute-start.3) | collective-permute-done | bytes 196640 | tf_op jit(solution)/shard_map/ppermute | solution.py:219
  11.9 2.0 %collective-permute-start.4 = (bf16[24,4096]{1,0:T(8,128)(2,1)S(1)}, bf16[24,4096]{1,0:T(8,128)(2,1)S(1)}, u32[]{:S(2)}, u32[]{:S(2)}) collective-permute-start(bf16[24,4096]{1,0:T(8,128)(2,1)S(1)} %collective-permute-done.3.refs_2_.refs_10_), channel_id=1, source_target_pairs={{2,0},{4,2},{6,4},{7,6},{5,7},{3,5},{1,3},{0,1},{10,8},{12,10},{14... | collective-permute-start | bytes 589832 | tf_op jit(solution)/shard_map/ppermute | solution.py:219
  14.1 4.1 %collective-permute-done.refs_1_.refs_9_ = bf16[24,4096]{1,0:T(8,128)(2,1)S(1)} collective-permute-done((bf16[24,4096]{1,0:T(8,128)(2,1)S(1)}, bf16[24,4096]{1,0:T(8,128)(2,1)S(1)}, u32[]{:S(2)}, u32[]{:S(2)}) %collective-permute-start) | collective-permute-done | bytes 196640 | tf_op jit(solution)/shard_map/ppermute | solution.py:219
  18.3 1.9 %collective-permute-start.11 = (bf16[24,4096]{1,0:T(8,128)(2,1)S(1)}, bf16[24,4096]{1,0:T(8,128)(2,1)S(1)}, u32[]{:S(2)}, u32[]{:S(2)}) collective-permute-start(bf16[24,4096]{1,0:T(8,128)(2,1)S(1)} %collective-permute-done.9.refs_2_), channel_id=1, source_target_pairs={{2,0},{4,2},{6,4},{7,6},{5,7},{3,5},{1,3},{0,1},{10,8},{12,10},{14... | collective-permute-start | bytes 589832 | tf_op jit(solution)/shard_map/ppermute | solution.py:219
  20.4 2.0 %collective-permute-start.5 = (bf16[24,4096]{1,0:T(8,128)(2,1)S(1)}, bf16[24,4096]{1,0:T(8,128)(2,1)S(1)}, u32[]{:S(2)}, u32[]{:S(2)}) collective-permute-start(bf16[24,4096]{1,0:T(8,128)(2,1)S(1)} %collective-permute-done.4.refs_4_.refs_12_), channel_id=1, source_target_pairs={{2,0},{4,2},{6,4},{7,6},{5,7},{3,5},{1,3},{0,1},{10,8},{12,10},{14... | collective-permute-start | bytes 589832 | tf_op jit(solution)/shard_map/ppermute | solution.py:219
  22.5 4.1 %collective-permute-done.1.refs_3_.refs_11_ = bf16[24,4096]{1,0:T(8,128)(2,1)S(1)} collective-permute-done((bf16[24,4096]{1,0:T(8,128)(2,1)S(1)}, bf16[24,4096]{1,0:T(8,128)(2,1)S(1)}, u32[]{:S(2)}, u32[]{:S(2)}) %collective-permute-start.1) | collective-permute-done | bytes 196640 | tf_op jit(solution)/shard_map/ppermute | solution.py:219
  26.7 1.9 %collective-permute-start.13 = (bf16[24,4096]{1,0:T(8,128)(2,1)S(1)}, bf16[24,4096]{1,0:T(8,128)(2,1)S(1)}, u32[]{:S(2)}, u32[]{:S(2)}) collective-permute-start(bf16[24,4096]{1,0:T(8,128)(2,1)S(1)} %collective-permute-done.11.refs_4_), channel_id=1, source_target_pairs={{2,0},{4,2},{6,4},{7,6},{5,7},{3,5},{1,3},{0,1},{10,8},{12,10},{14... | collective-permute-start | bytes 589832 | tf_op jit(solution)/shard_map/ppermute | solution.py:219
  29.0 2.0 %collective-permute-start.26 = (bf16[24,4096]{1,0:T(8,128)(2,1)S(1)}, bf16[24,4096]{1,0:T(8,128)(2,1)S(1)}, u32[]{:S(2)}, u32[]{:S(2)}) collective-permute-start(bf16[24,4096]{1,0:T(8,128)(2,1)S(1)} %collective-permute-done.5.refs_6_.refs_14_), channel_id=1, source_target_pairs={{2,0},{4,2},{6,4},{7,6},{5,7},{3,5},{1,3},{0,1},{10,8},{12,10},{14... | collective-permute-start | bytes 589832 | tf_op jit(solution)/shard_map/ppermute | solution.py:224
  31.2 3.9 %collective-permute-done.2.refs_5_.refs_13_ = bf16[24,4096]{1,0:T(8,128)(2,1)S(1)} collective-permute-done((bf16[24,4096]{1,0:T(8,128)(2,1)S(1)}, bf16[24,4096]{1,0:T(8,128)(2,1)S(1)}, u32[]{:S(2)}, u32[]{:S(2)}) %collective-permute-start.2) | collective-permute-done | bytes 196640 | tf_op jit(solution)/shard_map/ppermute | solution.py:219
  35.0 1.6 %collective-permute-start.7 = (bf16[24,4096]{1,0:T(8,128)(2,1)S(1)}, bf16[24,4096]{1,0:T(8,128)(2,1)S(1)}, u32[]{:S(2)}, u32[]{:S(2)}) collective-permute-start(bf16[24,4096]{1,0:T(8,128)(2,1)S(1)} %get-tuple-element.51.refs_0_.refs_8_), channel_id=1, source_target_pairs={{2,0},{4,2},{6,4},{7,6},{5,7},{3,5},{1,3},{0,1},{10,8},{12,10},{14... | collective-permute-start | bytes 589832 | tf_op jit(solution)/shard_map/ppermute | solution.py:219
  37.0 1.6 %collective-permute-start.21 = (bf16[24,4096]{1,0:T(8,128)(2,1)S(1)}, bf16[24,4096]{1,0:T(8,128)(2,1)S(1)}, u32[]{:S(2)}, u32[]{:S(2)}) collective-permute-start(bf16[24,4096]{1,0:T(8,128)(2,1)S(1)} %get-tuple-element.43.refs_0_), channel_id=1, source_target_pairs={{2,0},{4,2},{6,4},{7,6},{5,7},{3,5},{1,3},{0,1},{10,8},{12,10},{14... | collective-permute-start | bytes 589832 | tf_op jit(solution)/shard_map/ppermute | solution.py:219
  38.6 2.0 %collective-permute-start.20 = (bf16[24,4096]{1,0:T(8,128)(2,1)S(1)}, bf16[24,4096]{1,0:T(8,128)(2,1)S(1)}, u32[]{:S(2)}, u32[]{:S(2)}) collective-permute-start(bf16[24,4096]{1,0:T(8,128)(2,1)S(1)} %get-tuple-element.43.refs_0_), channel_id=1, source_target_pairs={{0,2},{2,4},{4,6},{6,7},{7,5},{5,3},{3,1},{1,0},{8,10},{10,12},{12... | collective-permute-start | bytes 589832 | tf_op jit(solution)/shard_map/ppermute | solution.py:219
  40.7 1.7 %collective-permute-start.29 = (bf16[8,24,1024]{2,1,0:T(8,128)(2,1)S(1)}, bf16[8,24,1024]{2,1,0:T(8,128)(2,1)S(1)}, u32[]{:S(2)}, u32[]{:S(2)}) collective-permute-start(bf16[8,24,1024]{2,1,0:T(8,128)(2,1)S(1)} %shard_map.75.refs_1_), channel_id=1, source_target_pairs={{0,16},{8,24},{16,0},{24,8},{1,17},{9,25},{17,1},{25,9},{2,18},{10... | collective-permute-start | bytes 1179656 | tf_op jit(solution)/shard_map/ppermute | solution.py:199
  42.4 4.1 %shard_map.68.refs_9_ = f32[192,2048]{1,0:T(8,128)S(1)} custom-call(bf16[24,4096]{1,0:T(8,128)(2,1)S(1)} %get-tuple-element.35.refs_0_, bf16[24,4096]{1,0:T(8,128)(2,1)S(1)} %collective-permute-done.8.refs_1_, bf16[24,4096]{1,0:T(8,128)(2,1)S(1)} %collective-permute-done.9.refs_2_, bf16[24,4096]{1,0:T(8,128)(2,1)S(1)} %collective-permute-done.10.refs_3_, ...), custom_call_target="tpu_custom_call" | custom-call | flops 4831838208 | bytes 25165824 | tf_op jit(solution)/shard_map/pallas_call | solution.py:188
  46.5 1.6 %collective-permute-start.15 = (bf16[24,4096]{1,0:T(8,128)(2,1)S(1)}, bf16[24,4096]{1,0:T(8,128)(2,1)S(1)}, u32[]{:S(2)}, u32[]{:S(2)}) collective-permute-start(bf16[24,4096]{1,0:T(8,128)(2,1)S(1)} %collective-permute-done.6.refs_1_.refs_9_), channel_id=1, source_target_pairs={{0,2},{2,4},{4,6},{6,7},{7,5},{5,3},{3,1},{1,0},{8,10},{10,12},{12... | collective-permute-start | bytes 589832 | tf_op jit(solution)/shard_map/ppermute | solution.py:219
  48.1 1.6 %collective-permute-start.22 = (bf16[24,4096]{1,0:T(8,128)(2,1)S(1)}, bf16[24,4096]{1,0:T(8,128)(2,1)S(1)}, u32[]{:S(2)}, u32[]{:S(2)}) collective-permute-start(bf16[24,4096]{1,0:T(8,128)(2,1)S(1)} %collective-permute-done.20.refs_1_), channel_id=1, source_target_pairs={{0,2},{2,4},{4,6},{6,7},{7,5},{5,3},{3,1},{1,0},{8,10},{10,12},{12... | collective-permute-start | bytes 589832 | tf_op jit(solution)/shard_map/ppermute | solution.py:219
  50.1 4.0 %shard_map.69.refs_9_ = f32[192,2048]{1,0:T(8,128)S(1)} custom-call(bf16[24,4096]{1,0:T(8,128)(2,1)S(1)} %get-tuple-element.35.refs_0_, bf16[24,4096]{1,0:T(8,128)(2,1)S(1)} %collective-permute-done.8.refs_1_, bf16[24,4096]{1,0:T(8,128)(2,1)S(1)} %collective-permute-done.9.refs_2_, bf16[24,4096]{1,0:T(8,128)(2,1)S(1)} %collective-permute-done.10.refs_3_, ...), custom_call_target="tpu_custom_call" | custom-call | flops 4831838208 | bytes 25165824 | tf_op jit(solution)/shard_map/pallas_call | solution.py:188
  55.6 1.6 %collective-permute-start.24 = (bf16[24,4096]{1,0:T(8,128)(2,1)S(1)}, bf16[24,4096]{1,0:T(8,128)(2,1)S(1)}, u32[]{:S(2)}, u32[]{:S(2)}) collective-permute-start(bf16[24,4096]{1,0:T(8,128)(2,1)S(1)} %collective-permute-done.22.refs_3_), channel_id=1, source_target_pairs={{0,2},{2,4},{4,6},{6,7},{7,5},{5,3},{3,1},{1,0},{8,10},{10,12},{12... | collective-permute-start | bytes 589832 | tf_op jit(solution)/shard_map/ppermute | solution.py:219
  57.8 4.1 %shard_map.70.refs_9_ = f32[192,2048]{1,0:T(8,128)S(1)} custom-call(bf16[24,4096]{1,0:T(8,128)(2,1)S(1)} %get-tuple-element.33.refs_0_.refs_8_, bf16[24,4096]{1,0:T(8,128)(2,1)S(1)} %collective-permute-done.refs_1_.refs_9_, bf16[24,4096]{1,0:T(8,128)(2,1)S(1)} %collective-permute-done.3.refs_2_.refs_10_, ...), custom_call_target="tpu_custom_call" | custom-call | flops 4831838208 | bytes 25165824 | tf_op jit(solution)/shard_map/pallas_call | solution.py:188
  61.9 1.7 %collective-permute-start.17 = (bf16[24,4096]{1,0:T(8,128)(2,1)S(1)}, bf16[24,4096]{1,0:T(8,128)(2,1)S(1)}, u32[]{:S(2)}, u32[]{:S(2)}) collective-permute-start(bf16[24,4096]{1,0:T(8,128)(2,1)S(1)} %collective-permute-done.15.refs_3_.refs_11_), channel_id=1, source_target_pairs={{0,2},{2,4},{4,6},{6,7},{7,5},{5,3},{3,1},{1,0},{8,10},{10,12},{12... | collective-permute-start | bytes 589832 | tf_op jit(solution)/shard_map/ppermute | solution.py:219
  64.0 1.6 %collective-permute-start.27 = (bf16[24,4096]{1,0:T(8,128)(2,1)S(1)}, bf16[24,4096]{1,0:T(8,128)(2,1)S(1)}, u32[]{:S(2)}, u32[]{:S(2)}) collective-permute-start(bf16[24,4096]{1,0:T(8,128)(2,1)S(1)} %collective-permute-done.24.refs_5_), channel_id=1, source_target_pairs={{0,2},{2,4},{4,6},{6,7},{7,5},{5,3},{3,1},{1,0},{8,10},{10,12},{12... | collective-permute-start | bytes 589832 | tf_op jit(solution)/shard_map/ppermute | solution.py:223
  66.3 4.1 %shard_map.71.refs_9_ = f32[192,2048]{1,0:T(8,128)S(1)} custom-call(bf16[24,4096]{1,0:T(8,128)(2,1)S(1)} %get-tuple-element.33.refs_0_.refs_8_, bf16[24,4096]{1,0:T(8,128)(2,1)S(1)} %collective-permute-done.refs_1_.refs_9_, bf16[24,4096]{1,0:T(8,128)(2,1)S(1)} %collective-permute-done.3.refs_2_.refs_10_, ...), custom_call_target="tpu_custom_call" | custom-call | flops 4831838208 | bytes 25165824 | tf_op jit(solution)/shard_map/pallas_call | solution.py:188
  72.8 6.5 %shard_map.72.refs_9_ = f32[192,2048]{1,0:T(8,128)S(1)} custom-call(bf16[24,4096]{1,0:T(8,128)(2,1)S(1)} %get-tuple-element.43.refs_0_, bf16[24,4096]{1,0:T(8,128)(2,1)S(1)} %collective-permute-done.20.refs_1_, bf16[24,4096]{1,0:T(8,128)(2,1)S(1)} %collective-permute-done.21.refs_2_, bf16[24,4096]{1,0:T(8,128)(2,1)S(1)} %collective-permute-done.22.refs_3_, ...), custom_call_target="tpu_custom_call" | custom-call | flops 9663676416 | bytes 50331648 | tf_op jit(solution)/shard_map/pallas_call | solution.py:188
  79.3 4.1 %shard_map.73.refs_9_ = f32[192,2048]{1,0:T(8,128)S(1)} custom-call(bf16[24,4096]{1,0:T(8,128)(2,1)S(1)} %get-tuple-element.51.refs_0_.refs_8_, bf16[24,4096]{1,0:T(8,128)(2,1)S(1)} %collective-permute-done.6.refs_1_.refs_9_, bf16[24,4096]{1,0:T(8,128)(2,1)S(1)} %collective-permute-done.7.refs_2_.refs_10_, ...), custom_call_target="tpu_custom_call" | custom-call | flops 4831838208 | bytes 25165824 | tf_op jit(solution)/shard_map/pallas_call | solution.py:188
  84.0 4.1 %shard_map.74.refs_0_ = f32[192,2048]{1,0:T(8,128)S(1)} custom-call(bf16[24,4096]{1,0:T(8,128)(2,1)S(1)} %get-tuple-element.51.refs_0_.refs_8_, bf16[24,4096]{1,0:T(8,128)(2,1)S(1)} %collective-permute-done.6.refs_1_.refs_9_, bf16[24,4096]{1,0:T(8,128)(2,1)S(1)} %collective-permute-done.7.refs_2_.refs_10_, ...), custom_call_target="tpu_custom_call" | custom-call | flops 4831838208 | bytes 25165824 | tf_op jit(solution)/shard_map/pallas_call | solution.py:188
  88.1 2.3 %shard_map.77 = (f32[192,384]{1,0:T(8,128)S(1)}, f32[192,192]{1,0:T(8,128)S(1)}) custom-call(s32[4]{0:T(128)S(1)} %copy-done.1, f32[192,2048]{1,0:T(8,128)S(1)} %shard_map.74.refs_0_, bf16[8,24,1024]{2,1,0:T(8,128)(2,1)S(1)} %shard_map.75.refs_1_, bf16[8,24,1024]{2,1,0:T(8,128)(2,1)S(1)} %shard_map.76.refs_2_, ...), custom_call_target="tpu_custom_call" | custom-call | tf_op jit(solution)/shard_map/pallas_call | solution.py:169
  95.2 1.6 %collective-permute-start.38 = (f32[2,24,192]{2,1,0:T(8,128)S(1)}, f32[2,24,192]{2,1,0:T(8,128)S(1)}, u32[]{:S(2)}, u32[]{:S(2)}) collective-permute-start(f32[2,24,192]{2,1,0:T(8,128)S(1)} %dynamic-slice_bitcast_fusion.3), channel_id=1, source_target_pairs={{0,2},{1,3},{2,0},{3,1},{4,6},{5,7},{6,4},{7,5},{8,10},{9,11},{10,... | collective-permute-start | bytes 110600 | tf_op jit(solution)/shard_map/ppermute | solution.py:268
  99.4 2.3 %collective-permute-start.39 = (f32[1,24,192]{2,1,0:T(8,128)S(1)}, f32[1,24,192]{2,1,0:T(8,128)S(1)}, u32[]{:S(2)}, u32[]{:S(2)}) collective-permute-start(f32[1,24,192]{2,1,0:T(8,128)S(1)} %constant_dynamic-slice_fusion), channel_id=1, source_target_pairs={{0,4},{1,5},{2,6},{3,7},{4,0},{5,1},{6,2},{7,3},{8,12},{9,13},{10,... | collective-permute-start | bytes 55304 | tf_op jit(solution)/shard_map/ppermute | solution.py:268
  106.5 2.5 %collective-permute-start.36 = (f32[1,24,384]{2,1,0:T(8,128)S(1)}, f32[1,24,384]{2,1,0:T(8,128)S(1)}, u32[]{:S(2)}, u32[]{:S(2)}) collective-permute-start(f32[1,24,384]{2,1,0:T(8,128)S(1)} %constant_dynamic-slice_fusion.1), channel_id=1, source_target_pairs={{0,4},{1,5},{2,6},{3,7},{4,0},{5,1},{6,2},{7,3},{8,12},{9,13},{10,... | collective-permute-start | bytes 110600 | tf_op jit(solution)/shard_map/ppermute | solution.py:268
  109.6 2.2 %collective-permute-done.36 = f32[1,24,384]{2,1,0:T(8,128)S(1)} collective-permute-done((f32[1,24,384]{2,1,0:T(8,128)S(1)}, f32[1,24,384]{2,1,0:T(8,128)S(1)}, u32[]{:S(2)}, u32[]{:S(2)}) %collective-permute-start.36) | collective-permute-done | bytes 36896 | tf_op jit(solution)/shard_map/ppermute | solution.py:268
  (86 shorter events, 22.6 us)
Async XLA Ops:
  3.1 8.8 %collective-permute-start.3 = (bf16[24,4096]{1,0:T(8,128)(2,1)S(1)}, bf16[24,4096]{1,0:T(8,128)(2,1)S(1)}, u32[]{:S(2)}, u32[]{:S(2)}) collective-permute-start(bf16[24,4096]{1,0:T(8,128)(2,1)S(1)} %get-tuple-element.33.refs_0_.refs_8_), channel_id=1, source_target_pairs={{2,0},{4,2},{6,4},{7,6},{5,7},{3,5},{1,3},{0,1},{10,8},{12,10},{14... | collective-permute-start | bytes 589832 | tf_op jit(solution)/shard_map/ppermute | solution.py:219
  6.1 7.8 %collective-permute-start.8 = (bf16[24,4096]{1,0:T(8,128)(2,1)S(1)}, bf16[24,4096]{1,0:T(8,128)(2,1)S(1)}, u32[]{:S(2)}, u32[]{:S(2)}) collective-permute-start(bf16[24,4096]{1,0:T(8,128)(2,1)S(1)} %get-tuple-element.35.refs_0_), channel_id=1, source_target_pairs={{0,2},{2,4},{4,6},{6,7},{7,5},{5,3},{3,1},{1,0},{8,10},{10,12},{12... | collective-permute-start | bytes 589832 | tf_op jit(solution)/shard_map/ppermute | solution.py:219
  6.3 11.9 %collective-permute-start = (bf16[24,4096]{1,0:T(8,128)(2,1)S(1)}, bf16[24,4096]{1,0:T(8,128)(2,1)S(1)}, u32[]{:S(2)}, u32[]{:S(2)}) collective-permute-start(bf16[24,4096]{1,0:T(8,128)(2,1)S(1)} %get-tuple-element.33.refs_0_.refs_8_), channel_id=1, source_target_pairs={{0,2},{2,4},{4,6},{6,7},{7,5},{5,3},{3,1},{1,0},{8,10},{10,12},{12... | collective-permute-start | bytes 589832 | tf_op jit(solution)/shard_map/ppermute | solution.py:219
  8.2 10.0 %collective-permute-start.9 = (bf16[24,4096]{1,0:T(8,128)(2,1)S(1)}, bf16[24,4096]{1,0:T(8,128)(2,1)S(1)}, u32[]{:S(2)}, u32[]{:S(2)}) collective-permute-start(bf16[24,4096]{1,0:T(8,128)(2,1)S(1)} %get-tuple-element.35.refs_0_), channel_id=1, source_target_pairs={{2,0},{4,2},{6,4},{7,6},{5,7},{3,5},{1,3},{0,1},{10,8},{12,10},{14... | collective-permute-start | bytes 589832 | tf_op jit(solution)/shard_map/ppermute | solution.py:219
  11.9 8.4 %collective-permute-start.4 = (bf16[24,4096]{1,0:T(8,128)(2,1)S(1)}, bf16[24,4096]{1,0:T(8,128)(2,1)S(1)}, u32[]{:S(2)}, u32[]{:S(2)}) collective-permute-start(bf16[24,4096]{1,0:T(8,128)(2,1)S(1)} %collective-permute-done.3.refs_2_.refs_10_), channel_id=1, source_target_pairs={{2,0},{4,2},{6,4},{7,6},{5,7},{3,5},{1,3},{0,1},{10,8},{12,10},{14... | collective-permute-start | bytes 589832 | tf_op jit(solution)/shard_map/ppermute | solution.py:219
  14.0 8.4 %collective-permute-start.10 = (bf16[24,4096]{1,0:T(8,128)(2,1)S(1)}, bf16[24,4096]{1,0:T(8,128)(2,1)S(1)}, u32[]{:S(2)}, u32[]{:S(2)}) collective-permute-start(bf16[24,4096]{1,0:T(8,128)(2,1)S(1)} %collective-permute-done.8.refs_1_), channel_id=1, source_target_pairs={{0,2},{2,4},{4,6},{6,7},{7,5},{5,3},{3,1},{1,0},{8,10},{10,12},{12... | collective-permute-start | bytes 589832 | tf_op jit(solution)/shard_map/ppermute | solution.py:219
  18.2 8.4 %collective-permute-start.1 = (bf16[24,4096]{1,0:T(8,128)(2,1)S(1)}, bf16[24,4096]{1,0:T(8,128)(2,1)S(1)}, u32[]{:S(2)}, u32[]{:S(2)}) collective-permute-start(bf16[24,4096]{1,0:T(8,128)(2,1)S(1)} %collective-permute-done.refs_1_.refs_9_), channel_id=1, source_target_pairs={{0,2},{2,4},{4,6},{6,7},{7,5},{5,3},{3,1},{1,0},{8,10},{10,12},{12... | collective-permute-start | bytes 589832 | tf_op jit(solution)/shard_map/ppermute | solution.py:219
  18.3 8.4 %collective-permute-start.11 = (bf16[24,4096]{1,0:T(8,128)(2,1)S(1)}, bf16[24,4096]{1,0:T(8,128)(2,1)S(1)}, u32[]{:S(2)}, u32[]{:S(2)}) collective-permute-start(bf16[24,4096]{1,0:T(8,128)(2,1)S(1)} %collective-permute-done.9.refs_2_), channel_id=1, source_target_pairs={{2,0},{4,2},{6,4},{7,6},{5,7},{3,5},{1,3},{0,1},{10,8},{12,10},{14... | collective-permute-start | bytes 589832 | tf_op jit(solution)/shard_map/ppermute | solution.py:219
  20.4 8.7 %collective-permute-start.5 = (bf16[24,4096]{1,0:T(8,128)(2,1)S(1)}, bf16[24,4096]{1,0:T(8,128)(2,1)S(1)}, u32[]{:S(2)}, u32[]{:S(2)}) collective-permute-start(bf16[24,4096]{1,0:T(8,128)(2,1)S(1)} %collective-permute-done.4.refs_4_.refs_12_), channel_id=1, source_target_pairs={{2,0},{4,2},{6,4},{7,6},{5,7},{3,5},{1,3},{0,1},{10,8},{12,10},{14... | collective-permute-start | bytes 589832 | tf_op jit(solution)/shard_map/ppermute | solution.py:219
  22.4 8.7 %collective-permute-start.12 = (bf16[24,4096]{1,0:T(8,128)(2,1)S(1)}, bf16[24,4096]{1,0:T(8,128)(2,1)S(1)}, u32[]{:S(2)}, u32[]{:S(2)}) collective-permute-start(bf16[24,4096]{1,0:T(8,128)(2,1)S(1)} %collective-permute-done.10.refs_3_), channel_id=1, source_target_pairs={{0,2},{2,4},{4,6},{6,7},{7,5},{5,3},{3,1},{1,0},{8,10},{10,12},{12... | collective-permute-start | bytes 589832 | tf_op jit(solution)/shard_map/ppermute | solution.py:219
  26.6 8.4 %collective-permute-start.2 = (bf16[24,4096]{1,0:T(8,128)(2,1)S(1)}, bf16[24,4096]{1,0:T(8,128)(2,1)S(1)}, u32[]{:S(2)}, u32[]{:S(2)}) collective-permute-start(bf16[24,4096]{1,0:T(8,128)(2,1)S(1)} %collective-permute-done.1.refs_3_.refs_11_), channel_id=1, source_target_pairs={{0,2},{2,4},{4,6},{6,7},{7,5},{5,3},{3,1},{1,0},{8,10},{10,12},{12... | collective-permute-start | bytes 589832 | tf_op jit(solution)/shard_map/ppermute | solution.py:219
  26.7 10.3 %collective-permute-start.13 = (bf16[24,4096]{1,0:T(8,128)(2,1)S(1)}, bf16[24,4096]{1,0:T(8,128)(2,1)S(1)}, u32[]{:S(2)}, u32[]{:S(2)}) collective-permute-start(bf16[24,4096]{1,0:T(8,128)(2,1)S(1)} %collective-permute-done.11.refs_4_), channel_id=1, source_target_pairs={{2,0},{4,2},{6,4},{7,6},{5,7},{3,5},{1,3},{0,1},{10,8},{12,10},{14... | collective-permute-start | bytes 589832 | tf_op jit(solution)/shard_map/ppermute | solution.py:219
  29.0 9.6 %collective-permute-start.26 = (bf16[24,4096]{1,0:T(8,128)(2,1)S(1)}, bf16[24,4096]{1,0:T(8,128)(2,1)S(1)}, u32[]{:S(2)}, u32[]{:S(2)}) collective-permute-start(bf16[24,4096]{1,0:T(8,128)(2,1)S(1)} %collective-permute-done.5.refs_6_.refs_14_), channel_id=1, source_target_pairs={{2,0},{4,2},{6,4},{7,6},{5,7},{3,5},{1,3},{0,1},{10,8},{12,10},{14... | collective-permute-start | bytes 589832 | tf_op jit(solution)/shard_map/ppermute | solution.py:224
  31.1 9.6 %collective-permute-start.14 = (bf16[24,4096]{1,0:T(8,128)(2,1)S(1)}, bf16[24,4096]{1,0:T(8,128)(2,1)S(1)}, u32[]{:S(2)}, u32[]{:S(2)}) collective-permute-start(bf16[24,4096]{1,0:T(8,128)(2,1)S(1)} %collective-permute-done.12.refs_5_), channel_id=1, source_target_pairs={{0,2},{2,4},{4,6},{6,7},{7,5},{5,3},{3,1},{1,0},{8,10},{10,12},{12... | collective-permute-start | bytes 589832 | tf_op jit(solution)/shard_map/ppermute | solution.py:223
  35.0 14.7 %collective-permute-start.7 = (bf16[24,4096]{1,0:T(8,128)(2,1)S(1)}, bf16[24,4096]{1,0:T(8,128)(2,1)S(1)}, u32[]{:S(2)}, u32[]{:S(2)}) collective-permute-start(bf16[24,4096]{1,0:T(8,128)(2,1)S(1)} %get-tuple-element.51.refs_0_.refs_8_), channel_id=1, source_target_pairs={{2,0},{4,2},{6,4},{7,6},{5,7},{3,5},{1,3},{0,1},{10,8},{12,10},{14... | collective-permute-start | bytes 589832 | tf_op jit(solution)/shard_map/ppermute | solution.py:219
  36.6 9.9 %collective-permute-start.6 = (bf16[24,4096]{1,0:T(8,128)(2,1)S(1)}, bf16[24,4096]{1,0:T(8,128)(2,1)S(1)}, u32[]{:S(2)}, u32[]{:S(2)}) collective-permute-start(bf16[24,4096]{1,0:T(8,128)(2,1)S(1)} %get-tuple-element.51.refs_0_.refs_8_), channel_id=1, source_target_pairs={{0,2},{2,4},{4,6},{6,7},{7,5},{5,3},{3,1},{1,0},{8,10},{10,12},{12... | collective-permute-start | bytes 589832 | tf_op jit(solution)/shard_map/ppermute | solution.py:219
  37.0 17.1 %collective-permute-start.21 = (bf16[24,4096]{1,0:T(8,128)(2,1)S(1)}, bf16[24,4096]{1,0:T(8,128)(2,1)S(1)}, u32[]{:S(2)}, u32[]{:S(2)}) collective-permute-start(bf16[24,4096]{1,0:T(8,128)(2,1)S(1)} %get-tuple-element.43.refs_0_), channel_id=1, source_target_pairs={{2,0},{4,2},{6,4},{7,6},{5,7},{3,5},{1,3},{0,1},{10,8},{12,10},{14... | collective-permute-start | bytes 589832 | tf_op jit(solution)/shard_map/ppermute | solution.py:219
  38.6 7.8 %collective-permute-start.20 = (bf16[24,4096]{1,0:T(8,128)(2,1)S(1)}, bf16[24,4096]{1,0:T(8,128)(2,1)S(1)}, u32[]{:S(2)}, u32[]{:S(2)}) collective-permute-start(bf16[24,4096]{1,0:T(8,128)(2,1)S(1)} %get-tuple-element.43.refs_0_), channel_id=1, source_target_pairs={{0,2},{2,4},{4,6},{6,7},{7,5},{5,3},{3,1},{1,0},{8,10},{10,12},{12... | collective-permute-start | bytes 589832 | tf_op jit(solution)/shard_map/ppermute | solution.py:219
  40.7 29.8 %collective-permute-start.29 = (bf16[8,24,1024]{2,1,0:T(8,128)(2,1)S(1)}, bf16[8,24,1024]{2,1,0:T(8,128)(2,1)S(1)}, u32[]{:S(2)}, u32[]{:S(2)}) collective-permute-start(bf16[8,24,1024]{2,1,0:T(8,128)(2,1)S(1)} %shard_map.75.refs_1_), channel_id=1, source_target_pairs={{0,16},{8,24},{16,0},{24,8},{1,17},{9,25},{17,1},{25,9},{2,18},{10... | collective-permute-start | bytes 1179656 | tf_op jit(solution)/shard_map/ppermute | solution.py:199
  46.5 15.4 %collective-permute-start.15 = (bf16[24,4096]{1,0:T(8,128)(2,1)S(1)}, bf16[24,4096]{1,0:T(8,128)(2,1)S(1)}, u32[]{:S(2)}, u32[]{:S(2)}) collective-permute-start(bf16[24,4096]{1,0:T(8,128)(2,1)S(1)} %collective-permute-done.6.refs_1_.refs_9_), channel_id=1, source_target_pairs={{0,2},{2,4},{4,6},{6,7},{7,5},{5,3},{3,1},{1,0},{8,10},{10,12},{12... | collective-permute-start | bytes 589832 | tf_op jit(solution)/shard_map/ppermute | solution.py:219
  48.1 7.5 %collective-permute-start.22 = (bf16[24,4096]{1,0:T(8,128)(2,1)S(1)}, bf16[24,4096]{1,0:T(8,128)(2,1)S(1)}, u32[]{:S(2)}, u32[]{:S(2)}) collective-permute-start(bf16[24,4096]{1,0:T(8,128)(2,1)S(1)} %collective-permute-done.20.refs_1_), channel_id=1, source_target_pairs={{0,2},{2,4},{4,6},{6,7},{7,5},{5,3},{3,1},{1,0},{8,10},{10,12},{12... | collective-permute-start | bytes 589832 | tf_op jit(solution)/shard_map/ppermute | solution.py:219
  49.7 7.7 %collective-permute-start.16 = (bf16[24,4096]{1,0:T(8,128)(2,1)S(1)}, bf16[24,4096]{1,0:T(8,128)(2,1)S(1)}, u32[]{:S(2)}, u32[]{:S(2)}) collective-permute-start(bf16[24,4096]{1,0:T(8,128)(2,1)S(1)} %collective-permute-done.7.refs_2_.refs_10_), channel_id=1, source_target_pairs={{2,0},{4,2},{6,4},{7,6},{5,7},{3,5},{1,3},{0,1},{10,8},{12,10},{14... | collective-permute-start | bytes 589832 | tf_op jit(solution)/shard_map/ppermute | solution.py:219
  54.2 9.3 %collective-permute-start.23 = (bf16[24,4096]{1,0:T(8,128)(2,1)S(1)}, bf16[24,4096]{1,0:T(8,128)(2,1)S(1)}, u32[]{:S(2)}, u32[]{:S(2)}) collective-permute-start(bf16[24,4096]{1,0:T(8,128)(2,1)S(1)} %collective-permute-done.21.refs_2_), channel_id=1, source_target_pairs={{2,0},{4,2},{6,4},{7,6},{5,7},{3,5},{1,3},{0,1},{10,8},{12,10},{14... | collective-permute-start | bytes 589832 | tf_op jit(solution)/shard_map/ppermute | solution.py:219
  55.6 8.3 %collective-permute-start.24 = (bf16[24,4096]{1,0:T(8,128)(2,1)S(1)}, bf16[24,4096]{1,0:T(8,128)(2,1)S(1)}, u32[]{:S(2)}, u32[]{:S(2)}) collective-permute-start(bf16[24,4096]{1,0:T(8,128)(2,1)S(1)} %collective-permute-done.22.refs_3_), channel_id=1, source_target_pairs={{0,2},{2,4},{4,6},{6,7},{7,5},{5,3},{3,1},{1,0},{8,10},{10,12},{12... | collective-permute-start | bytes 589832 | tf_op jit(solution)/shard_map/ppermute | solution.py:219
  57.4 8.9 %collective-permute-start.18 = (bf16[24,4096]{1,0:T(8,128)(2,1)S(1)}, bf16[24,4096]{1,0:T(8,128)(2,1)S(1)}, u32[]{:S(2)}, u32[]{:S(2)}) collective-permute-start(bf16[24,4096]{1,0:T(8,128)(2,1)S(1)} %collective-permute-done.16.refs_4_.refs_12_), channel_id=1, source_target_pairs={{2,0},{4,2},{6,4},{7,6},{5,7},{3,5},{1,3},{0,1},{10,8},{12,10},{14... | collective-permute-start | bytes 589832 | tf_op jit(solution)/shard_map/ppermute | solution.py:219
  61.9 8.5 %collective-permute-start.17 = (bf16[24,4096]{1,0:T(8,128)(2,1)S(1)}, bf16[24,4096]{1,0:T(8,128)(2,1)S(1)}, u32[]{:S(2)}, u32[]{:S(2)}) collective-permute-start(bf16[24,4096]{1,0:T(8,128)(2,1)S(1)} %collective-permute-done.15.refs_3_.refs_11_), channel_id=1, source_target_pairs={{0,2},{2,4},{4,6},{6,7},{7,5},{5,3},{3,1},{1,0},{8,10},{10,12},{12... | collective-permute-start | bytes 589832 | tf_op jit(solution)/shard_map/ppermute | solution.py:219
  63.5 6.9 %collective-permute-start.25 = (bf16[24,4096]{1,0:T(8,128)(2,1)S(1)}, bf16[24,4096]{1,0:T(8,128)(2,1)S(1)}, u32[]{:S(2)}, u32[]{:S(2)}) collective-permute-start(bf16[24,4096]{1,0:T(8,128)(2,1)S(1)} %collective-permute-done.23.refs_4_), channel_id=1, source_target_pairs={{2,0},{4,2},{6,4},{7,6},{5,7},{3,5},{1,3},{0,1},{10,8},{12,10},{14... | collective-permute-start | bytes 589832 | tf_op jit(solution)/shard_map/ppermute | solution.py:219
  64.0 8.0 %collective-permute-start.27 = (bf16[24,4096]{1,0:T(8,128)(2,1)S(1)}, bf16[24,4096]{1,0:T(8,128)(2,1)S(1)}, u32[]{:S(2)}, u32[]{:S(2)}) collective-permute-start(bf16[24,4096]{1,0:T(8,128)(2,1)S(1)} %collective-permute-done.24.refs_5_), channel_id=1, source_target_pairs={{0,2},{2,4},{4,6},{6,7},{7,5},{5,3},{3,1},{1,0},{8,10},{10,12},{12... | collective-permute-start | bytes 589832 | tf_op jit(solution)/shard_map/ppermute | solution.py:223
  70.4 17.7 %collective-permute-start.28 = (bf16[8,24,1024]{2,1,0:T(8,128)(2,1)S(1)}, bf16[8,24,1024]{2,1,0:T(8,128)(2,1)S(1)}, u32[]{:S(2)}, u32[]{:S(2)}) collective-permute-start(bf16[8,24,1024]{2,1,0:T(8,128)(2,1)S(1)} %shard_map.75.refs_1_), channel_id=1, source_target_pairs={{0,8},{8,0},{16,24},{24,16},{1,9},{9,1},{17,25},{25,17},{2,10},{10... | collective-permute-start | bytes 1179656 | tf_op jit(solution)/shard_map/ppermute | solution.py:200
  70.5 17.6 %collective-permute-start.30 = (bf16[8,24,1024]{2,1,0:T(8,128)(2,1)S(1)}, bf16[8,24,1024]{2,1,0:T(8,128)(2,1)S(1)}, u32[]{:S(2)}, u32[]{:S(2)}) collective-permute-start(bf16[8,24,1024]{2,1,0:T(8,128)(2,1)S(1)} %collective-permute-done.29.refs_4_), channel_id=1, source_target_pairs={{0,8},{8,0},{16,24},{24,16},{1,9},{9,1},{17,25},{25,17},{2,10},{10... | collective-permute-start | bytes 1179656 | tf_op jit(solution)/shard_map/ppermute | solution.py:205
  72.0 11.4 %collective-permute-start.32 = (bf16[8,24,1024]{2,1,0:T(8,128)(2,1)S(1)}, bf16[8,24,1024]{2,1,0:T(8,128)(2,1)S(1)}, u32[]{:S(2)}, u32[]{:S(2)}) collective-permute-start(bf16[8,24,1024]{2,1,0:T(8,128)(2,1)S(1)} %shard_map.76.refs_2_), channel_id=1, source_target_pairs={{0,16},{8,24},{16,0},{24,8},{1,17},{9,25},{17,1},{25,9},{2,18},{10... | collective-permute-start | bytes 1179656 | tf_op jit(solution)/shard_map/ppermute | solution.py:199
  72.8 15.2 %collective-permute-start.31 = (bf16[8,24,1024]{2,1,0:T(8,128)(2,1)S(1)}, bf16[8,24,1024]{2,1,0:T(8,128)(2,1)S(1)}, u32[]{:S(2)}, u32[]{:S(2)}) collective-permute-start(bf16[8,24,1024]{2,1,0:T(8,128)(2,1)S(1)} %shard_map.76.refs_2_), channel_id=1, source_target_pairs={{0,8},{8,0},{16,24},{24,16},{1,9},{9,1},{17,25},{25,17},{2,10},{10... | collective-permute-start | bytes 1179656 | tf_op jit(solution)/shard_map/ppermute | solution.py:200
  (14 other events, 58.5 us)

commit v3 on v2

--- a/solution.py
+++ b/solution.py
@@ -52,7 +52,16 @@
     return found + [n // 2]
 
 
-def cut_kernel(n, exponents_ref, codes_ref, *out_refs):
+def cut_kernel(n, exponents_hbm, codes_hbm, *refs):
+    out_refs, codes_ref, exponents_ref, sem = refs[:CHUNKS], *refs[CHUNKS:]
+    copies = [
+        pltpu.make_async_copy(codes_hbm, codes_ref, sem.at[0]),
+        pltpu.make_async_copy(exponents_hbm, exponents_ref, sem.at[1]),
+    ]
+    for copy in copies:
+        copy.start()
+    for copy in copies[::-1]:
+        copy.wait()
     rows, width = codes_ref.shape
     depth = width // (n * CHUNKS)
     line = lax.broadcasted_iota(jnp.int32, (rows, 128), 0)
@@ -71,7 +80,12 @@
 def cut(codes, exponents, n):
     rows, width = codes.shape
     piece = jax.ShapeDtypeStruct((rows, width // CHUNKS), jnp.bfloat16)
-    return call(functools.partial(cut_kernel, n), [piece] * CHUNKS, [SCALARS, WHOLE])(
+    scratch = [
+        pltpu.VMEM(codes.shape, codes.dtype),
+        pltpu.SMEM(exponents.shape, exponents.dtype),
+        pltpu.SemaphoreType.DMA((2,)),
+    ]
+    return call(functools.partial(cut_kernel, n), [piece] * CHUNKS, [HBM, HBM], scratch)(
         exponents, codes
     )
 
@@ -169,6 +183,26 @@
     return call(kernel, out, [SCALARS] + [WHOLE] * 9, scratch)(partner, total, *own, *other)
 
 
+def finish_kernel(factor, partner_ref, cross_ref, *refs):
+    blocks, (diag_ref, pair_ref, back_ref) = refs[:4], refs[4:]
+    group = lax.axis_index("grp")
+    size = diag_ref.shape[1]
+    diag_ref[...] = cross_ref[0, :, :size] * factor
+    pair_ref[...] = cross_ref[0, :, size:] * factor
+    for flip, block in enumerate(blocks):
+
+        @pl.when(partner_ref[group ^ flip] == group)
+        def _():
+            back_ref[...] = block[0] * factor
+
+
+def finish(partner, factor, cross, blocks):
+    _, rows, wide = cross.shape
+    out = [jax.ShapeDtypeStruct((rows, wide // 2), jnp.float32)] * 3
+    kernel = functools.partial(finish_kernel, factor)
+    return tuple(call(kernel, out, [SCALARS] + [WHOLE] * 5)(partner, cross, *blocks))
+
+
 def multiply(chunk, first, count, pieces, mat, before, later=()):
     n = len(pieces)
     rows, width = pieces[0].shape
@@ -242,7 +276,7 @@
         while halves and len(halves) > 4 - -(-4 * s // steps):
             k, h = halves.pop(0)
             total = multiply(k, h * (n // 2), n // 2, early[k], precond, total)
-        lanes = [(after(up, total), down, held) for up, down, held in lanes]
+        lanes = [(after(lanes[0][0], total), after(lanes[0][1], total), lanes[0][2]), lanes[1]]
     late = last_hops(lanes)
     for k, h in halves:
         total = multiply(k, h * (n // 2), n // 2, early[k], precond, total)
@@ -257,25 +291,28 @@
     other = [first_near, first_far, first_both, last_near, last_far, last_both]
     cross, pair = contractions(partner, total, [first_own, last_own], other, n)
 
+    size = n * rows
     sums = [block.reshape(n, rows, block.shape[1]) for block in (pair, cross)]
     bit = 1
     while bit < n:
-        mine = (me // bit) % 2
+        radix = 4 if 1 < bit < n // 2 else 2
+        mine = (me // bit) % radix
         for at, block in enumerate(sums):
-            pairs = block.reshape(block.shape[0] // 2, 2, *block.shape[1:])
-            kept = lax.dynamic_index_in_dim(pairs, mine, 1, keepdims=False)
-            given = lax.dynamic_index_in_dim(pairs, 1 - mine, 1, keepdims=False)
-            sums[at] = kept + lax.ppermute(given, "wide", [(i, i ^ bit) for i in range(n)])
-        bit *= 2
-    size = n * rows
-    cross = sums[1][0] * factor
-    back_rows = sums[0][0] * factor
-    kernel_back = back_rows
-    for flip in (1, 2, 3):
-        block = lax.ppermute(back_rows, "grp", [(i, i ^ flip) for i in range(4)])
-        source = lax.dynamic_index_in_dim(partner, group ^ flip, 0, keepdims=False)
-        kernel_back = jnp.where(source == group, block, kernel_back)
-    return (cross[:, :size], cross[:, size:], kernel_back)
+            split = block.reshape(block.shape[0] // radix, radix, *block.shape[1:])
+            block = lax.dynamic_index_in_dim(split, mine, 1, keepdims=False)
+            for flip in range(1, radix):
+                given = lax.dynamic_index_in_dim(split, mine ^ flip, 1, keepdims=False)
+                ways = [(i, i ^ flip * bit) for i in range(n)]
+                if bit == 1:
+                    block += lax.ppermute(given, "wide", ways)
+                else:
+                    block += lax.ppermute(given, "wide", ways)
+            sums[at] = block
+        bit *= radix
+    spread_rows = [
+        lax.ppermute(sums[0], "grp", [(i, i ^ flip) for i in range(4)]) for flip in (1, 2, 3)
+    ]
+    return finish(partner, factor, sums[1], [sums[0], *spread_rows])
 
 
 def solution(mesh):

time: 113 us -> 110 us (0.973)
  between operations: 2.93 us -> 0.95 us
  Pallas kernels: 33.9 us -> 35.2 us
  local copies, waits for them, and re-layouts: 3.13 us -> 1.84 us
    pallas_call x1 -> x2, Pallas kernels: 0.71 us -> 2.02 us  [the longest x1 1.24 us: finish(): call(kernel, out, [SCALARS] + [WHOLE] * 5)(partner, cross, *blocks)]
    ppermute x12, starting transfers between devices: 11.4 us -> 10.3 us  [both_ways(): lax.ppermute(up, 'wide', forth)]
    ppermute x9 -> x11, starting transfers between devices: 11.6 us -> 12 us  [the longest x8 10.1 us: shards(): block += lax.ppermute(given, 'wide', ways)]
    ppermute x9 -> x11, waiting for transfers between devices: 6.47 us -> 6.19 us  [the longest x8 6.19 us: shards(): block += lax.ppermute(given, 'wide', ways)]
  transfers between devices with their start and end apart: 43 -> 45, of which waited for: 16 -> 12; matrix products, arithmetic and copies ran while one was open for 1% -> 0% of each run, Pallas kernels for 27% -> 28%
where the time goes in v3:
time: 110 us
  starting transfers between devices  47 us (43%)
  Pallas kernels  35.2 us (32%)
  waiting for transfers between devices  24.8 us (23%)
  local copies, waits for them, and re-layouts  1.84 us (2%)
    pallas_call x7, Pallas kernels, multiply(): call(kernel, total, specs, scratch, flops, moved)  30.8 us
    ppermute x12, starting transfers between devices, both_ways(): lax.ppermute(down, 'wide', back)  16.6 us
    ppermute x12, waiting for transfers between devices, both_ways(): lax.ppermute(up, 'wide', forth)  12.2 us
    ppermute x12, starting transfers between devices, both_ways(): lax.ppermute(up, 'wide', forth)  10.3 us
    ppermute x8, starting transfers between devices, shards(): block += lax.ppermute(given, 'wide', ways)  10.1 us
    ppermute x8, waiting for transfers between devices, shards(): block += lax.ppermute(given, 'wide', ways)  6.19 us
    ppermute x12, waiting for transfers between devices, both_ways(): lax.ppermute(down, 'wide', back)  5.42 us
    ppermute x2, starting transfers between devices, spread(): far = lax.ppermute(value, 'grp', [(i, i ^ 2) for i in range(4)])  2.78 us
  transfers between devices with their start and end apart: 45, of which 12 were waited for; matrix products, arithmetic and copies ran while one was open for 0% of the time, Pallas kernels for 28%

profile of v3, /device:TPU:0, one launch (start us, length us, event | category | flops | bytes accessed | tf_op | source)
XLA Modules:
  0.0 109.7 jit_solution(8085569821184216598)
XLA Ops:
  3.2 3.0 %collective-permute-start.3 = (bf16[24,4096]{1,0:T(8,128)(2,1)S(1)}, bf16[24,4096]{1,0:T(8,128)(2,1)S(1)}, u32[]{:S(2)}, u32[]{:S(2)}) collective-permute-start(bf16[24,4096]{1,0:T(8,128)(2,1)S(1)} %get-tuple-element.33.refs_0_.refs_8_), channel_id=1, source_target_pairs={{2,0},{4,2},{6,4},{7,6},{5,7},{3,5},{1,3},{0,1},{10,8},{12,10},{14... | collective-permute-start | bytes 589832 | tf_op jit(solution)/shard_map/ppermute | solution.py:253
  6.3 2.0 %collective-permute-start = (bf16[24,4096]{1,0:T(8,128)(2,1)S(1)}, bf16[24,4096]{1,0:T(8,128)(2,1)S(1)}, u32[]{:S(2)}, u32[]{:S(2)}) collective-permute-start(bf16[24,4096]{1,0:T(8,128)(2,1)S(1)} %get-tuple-element.33.refs_0_.refs_8_), channel_id=1, source_target_pairs={{0,2},{2,4},{4,6},{6,7},{7,5},{5,3},{3,1},{1,0},{8,10},{10,12},{12... | collective-permute-start | bytes 589832 | tf_op jit(solution)/shard_map/ppermute | solution.py:253
  8.4 3.6 %collective-permute-done.3.refs_2_.refs_10_ = bf16[24,4096]{1,0:T(8,128)(2,1)S(1)} collective-permute-done((bf16[24,4096]{1,0:T(8,128)(2,1)S(1)}, bf16[24,4096]{1,0:T(8,128)(2,1)S(1)}, u32[]{:S(2)}, u32[]{:S(2)}) %collective-permute-start.3) | collective-permute-done | bytes 196640 | tf_op jit(solution)/shard_map/ppermute | solution.py:253
  12.0 2.0 %collective-permute-start.4 = (bf16[24,4096]{1,0:T(8,128)(2,1)S(1)}, bf16[24,4096]{1,0:T(8,128)(2,1)S(1)}, u32[]{:S(2)}, u32[]{:S(2)}) collective-permute-start(bf16[24,4096]{1,0:T(8,128)(2,1)S(1)} %collective-permute-done.3.refs_2_.refs_10_), channel_id=1, source_target_pairs={{2,0},{4,2},{6,4},{7,6},{5,7},{3,5},{1,3},{0,1},{10,8},{12,10},{14... | collective-permute-start | bytes 589832 | tf_op jit(solution)/shard_map/ppermute | solution.py:253
  14.1 4.1 %collective-permute-done.refs_1_.refs_9_ = bf16[24,4096]{1,0:T(8,128)(2,1)S(1)} collective-permute-done((bf16[24,4096]{1,0:T(8,128)(2,1)S(1)}, bf16[24,4096]{1,0:T(8,128)(2,1)S(1)}, u32[]{:S(2)}, u32[]{:S(2)}) %collective-permute-start) | collective-permute-done | bytes 196640 | tf_op jit(solution)/shard_map/ppermute | solution.py:253
  18.4 1.9 %collective-permute-start.17 = (bf16[24,4096]{1,0:T(8,128)(2,1)S(1)}, bf16[24,4096]{1,0:T(8,128)(2,1)S(1)}, u32[]{:S(2)}, u32[]{:S(2)}) collective-permute-start(bf16[24,4096]{1,0:T(8,128)(2,1)S(1)} %collective-permute-done.16.refs_2_), channel_id=1, source_target_pairs={{2,0},{4,2},{6,4},{7,6},{5,7},{3,5},{1,3},{0,1},{10,8},{12,10},{14... | collective-permute-start | bytes 589832 | tf_op jit(solution)/shard_map/ppermute | solution.py:253
  20.4 2.0 %collective-permute-start.5 = (bf16[24,4096]{1,0:T(8,128)(2,1)S(1)}, bf16[24,4096]{1,0:T(8,128)(2,1)S(1)}, u32[]{:S(2)}, u32[]{:S(2)}) collective-permute-start(bf16[24,4096]{1,0:T(8,128)(2,1)S(1)} %collective-permute-done.4.refs_4_.refs_12_), channel_id=1, source_target_pairs={{2,0},{4,2},{6,4},{7,6},{5,7},{3,5},{1,3},{0,1},{10,8},{12,10},{14... | collective-permute-start | bytes 589832 | tf_op jit(solution)/shard_map/ppermute | solution.py:253
  22.6 4.1 %collective-permute-done.1.refs_3_.refs_11_ = bf16[24,4096]{1,0:T(8,128)(2,1)S(1)} collective-permute-done((bf16[24,4096]{1,0:T(8,128)(2,1)S(1)}, bf16[24,4096]{1,0:T(8,128)(2,1)S(1)}, u32[]{:S(2)}, u32[]{:S(2)}) %collective-permute-start.1) | collective-permute-done | bytes 196640 | tf_op jit(solution)/shard_map/ppermute | solution.py:253
  26.8 1.9 %collective-permute-start.18 = (bf16[24,4096]{1,0:T(8,128)(2,1)S(1)}, bf16[24,4096]{1,0:T(8,128)(2,1)S(1)}, u32[]{:S(2)}, u32[]{:S(2)}) collective-permute-start(bf16[24,4096]{1,0:T(8,128)(2,1)S(1)} %collective-permute-done.17.refs_4_), channel_id=1, source_target_pairs={{2,0},{4,2},{6,4},{7,6},{5,7},{3,5},{1,3},{0,1},{10,8},{12,10},{14... | collective-permute-start | bytes 589832 | tf_op jit(solution)/shard_map/ppermute | solution.py:253
  29.1 2.0 %collective-permute-start.26 = (bf16[24,4096]{1,0:T(8,128)(2,1)S(1)}, bf16[24,4096]{1,0:T(8,128)(2,1)S(1)}, u32[]{:S(2)}, u32[]{:S(2)}) collective-permute-start(bf16[24,4096]{1,0:T(8,128)(2,1)S(1)} %collective-permute-done.5.refs_6_.refs_14_), channel_id=1, source_target_pairs={{2,0},{4,2},{6,4},{7,6},{5,7},{3,5},{1,3},{0,1},{10,8},{12,10},{14... | collective-permute-start | bytes 589832 | tf_op jit(solution)/shard_map/ppermute | solution.py:258
  31.2 3.9 %collective-permute-done.2.refs_5_.refs_13_ = bf16[24,4096]{1,0:T(8,128)(2,1)S(1)} collective-permute-done((bf16[24,4096]{1,0:T(8,128)(2,1)S(1)}, bf16[24,4096]{1,0:T(8,128)(2,1)S(1)}, u32[]{:S(2)}, u32[]{:S(2)}) %collective-permute-start.2) | collective-permute-done | bytes 196640 | tf_op jit(solution)/shard_map/ppermute | solution.py:253
  38.7 2.0 %collective-permute-start.19 = (bf16[24,4096]{1,0:T(8,128)(2,1)S(1)}, bf16[24,4096]{1,0:T(8,128)(2,1)S(1)}, u32[]{:S(2)}, u32[]{:S(2)}) collective-permute-start(bf16[24,4096]{1,0:T(8,128)(2,1)S(1)} %get-tuple-element.43.refs_0_), channel_id=1, source_target_pairs={{0,2},{2,4},{4,6},{6,7},{7,5},{5,3},{3,1},{1,0},{8,10},{10,12},{12... | collective-permute-start | bytes 589832 | tf_op jit(solution)/shard_map/ppermute | solution.py:253
  40.8 1.7 %collective-permute-start.29 = (bf16[8,24,1024]{2,1,0:T(8,128)(2,1)S(1)}, bf16[8,24,1024]{2,1,0:T(8,128)(2,1)S(1)}, u32[]{:S(2)}, u32[]{:S(2)}) collective-permute-start(bf16[8,24,1024]{2,1,0:T(8,128)(2,1)S(1)} %shard_map.75.refs_1_), channel_id=1, source_target_pairs={{0,16},{8,24},{16,0},{24,8},{1,17},{9,25},{17,1},{25,9},{2,18},{10... | collective-permute-start | bytes 1179656 | tf_op jit(solution)/shard_map/ppermute | solution.py:233
  42.5 4.1 %shard_map.68.refs_9_ = f32[192,2048]{1,0:T(8,128)S(1)} custom-call(bf16[24,4096]{1,0:T(8,128)(2,1)S(1)} %get-tuple-element.36.refs_0_, bf16[24,4096]{1,0:T(8,128)(2,1)S(1)} %collective-permute-done.13.refs_1_, bf16[24,4096]{1,0:T(8,128)(2,1)S(1)} %collective-permute-done.16.refs_2_, bf16[24,4096]{1,0:T(8,128)(2,1)S(1)} %collective-permute-done.14.refs_3_, ...), custom_call_target="tpu_custom_call" | custom-call | flops 4831838208 | bytes 25165824 | tf_op jit(solution)/shard_map/pallas_call | solution.py:222
  46.5 1.6 %collective-permute-start.22 = (bf16[24,4096]{1,0:T(8,128)(2,1)S(1)}, bf16[24,4096]{1,0:T(8,128)(2,1)S(1)}, u32[]{:S(2)}, u32[]{:S(2)}) collective-permute-start(bf16[24,4096]{1,0:T(8,128)(2,1)S(1)} %collective-permute-done.19.refs_1_), channel_id=1, source_target_pairs={{0,2},{2,4},{4,6},{6,7},{7,5},{5,3},{3,1},{1,0},{8,10},{10,12},{12... | collective-permute-start | bytes 589832 | tf_op jit(solution)/shard_map/ppermute | solution.py:253
  49.9 4.0 %shard_map.69.refs_9_ = f32[192,2048]{1,0:T(8,128)S(1)} custom-call(bf16[24,4096]{1,0:T(8,128)(2,1)S(1)} %get-tuple-element.36.refs_0_, bf16[24,4096]{1,0:T(8,128)(2,1)S(1)} %collective-permute-done.13.refs_1_, bf16[24,4096]{1,0:T(8,128)(2,1)S(1)} %collective-permute-done.16.refs_2_, bf16[24,4096]{1,0:T(8,128)(2,1)S(1)} %collective-permute-done.14.refs_3_, ...), custom_call_target="tpu_custom_call" | custom-call | flops 4831838208 | bytes 25165824 | tf_op jit(solution)/shard_map/pallas_call | solution.py:222
  54.8 1.6 %collective-permute-start.24 = (bf16[24,4096]{1,0:T(8,128)(2,1)S(1)}, bf16[24,4096]{1,0:T(8,128)(2,1)S(1)}, u32[]{:S(2)}, u32[]{:S(2)}) collective-permute-start(bf16[24,4096]{1,0:T(8,128)(2,1)S(1)} %collective-permute-done.22.refs_3_), channel_id=1, source_target_pairs={{0,2},{2,4},{4,6},{6,7},{7,5},{5,3},{3,1},{1,0},{8,10},{10,12},{12... | collective-permute-start | bytes 589832 | tf_op jit(solution)/shard_map/ppermute | solution.py:253
  57.5 4.1 %shard_map.70.refs_9_ = f32[192,2048]{1,0:T(8,128)S(1)} custom-call(bf16[24,4096]{1,0:T(8,128)(2,1)S(1)} %get-tuple-element.33.refs_0_.refs_8_, bf16[24,4096]{1,0:T(8,128)(2,1)S(1)} %collective-permute-done.refs_1_.refs_9_, bf16[24,4096]{1,0:T(8,128)(2,1)S(1)} %collective-permute-done.3.refs_2_.refs_10_, ...), custom_call_target="tpu_custom_call" | custom-call | flops 4831838208 | bytes 25165824 | tf_op jit(solution)/shard_map/pallas_call | solution.py:222
  63.8 2.0 %collective-permute-start.27 = (bf16[24,4096]{1,0:T(8,128)(2,1)S(1)}, bf16[24,4096]{1,0:T(8,128)(2,1)S(1)}, u32[]{:S(2)}, u32[]{:S(2)}) collective-permute-start(bf16[24,4096]{1,0:T(8,128)(2,1)S(1)} %collective-permute-done.24.refs_5_), channel_id=1, source_target_pairs={{0,2},{2,4},{4,6},{6,7},{7,5},{5,3},{3,1},{1,0},{8,10},{10,12},{12... | collective-permute-start | bytes 589832 | tf_op jit(solution)/shard_map/ppermute | solution.py:257
  65.8 4.0 %shard_map.71.refs_9_ = f32[192,2048]{1,0:T(8,128)S(1)} custom-call(bf16[24,4096]{1,0:T(8,128)(2,1)S(1)} %get-tuple-element.33.refs_0_.refs_8_, bf16[24,4096]{1,0:T(8,128)(2,1)S(1)} %collective-permute-done.refs_1_.refs_9_, bf16[24,4096]{1,0:T(8,128)(2,1)S(1)} %collective-permute-done.3.refs_2_.refs_10_, ...), custom_call_target="tpu_custom_call" | custom-call | flops 4831838208 | bytes 25165824 | tf_op jit(solution)/shard_map/pallas_call | solution.py:222
  72.5 6.5 %shard_map.72.refs_9_ = f32[192,2048]{1,0:T(8,128)S(1)} custom-call(bf16[24,4096]{1,0:T(8,128)(2,1)S(1)} %get-tuple-element.43.refs_0_, bf16[24,4096]{1,0:T(8,128)(2,1)S(1)} %collective-permute-done.19.refs_1_, bf16[24,4096]{1,0:T(8,128)(2,1)S(1)} %collective-permute-done.20.refs_2_, bf16[24,4096]{1,0:T(8,128)(2,1)S(1)} %collective-permute-done.22.refs_3_, ...), custom_call_target="tpu_custom_call" | custom-call | flops 9663676416 | bytes 50331648 | tf_op jit(solution)/shard_map/pallas_call | solution.py:222
  79.0 4.1 %shard_map.73.refs_9_ = f32[192,2048]{1,0:T(8,128)S(1)} custom-call(bf16[24,4096]{1,0:T(8,128)(2,1)S(1)} %get-tuple-element.51.refs_0_.refs_8_, bf16[24,4096]{1,0:T(8,128)(2,1)S(1)} %collective-permute-done.6.refs_1_.refs_9_, bf16[24,4096]{1,0:T(8,128)(2,1)S(1)} %collective-permute-done.7.refs_2_.refs_10_, ...), custom_call_target="tpu_custom_call" | custom-call | flops 4831838208 | bytes 25165824 | tf_op jit(solution)/shard_map/pallas_call | solution.py:222
  83.7 4.1 %shard_map.74.refs_0_ = f32[192,2048]{1,0:T(8,128)S(1)} custom-call(bf16[24,4096]{1,0:T(8,128)(2,1)S(1)} %get-tuple-element.51.refs_0_.refs_8_, bf16[24,4096]{1,0:T(8,128)(2,1)S(1)} %collective-permute-done.6.refs_1_.refs_9_, bf16[24,4096]{1,0:T(8,128)(2,1)S(1)} %collective-permute-done.7.refs_2_.refs_10_, ...), custom_call_target="tpu_custom_call" | custom-call | flops 4831838208 | bytes 25165824 | tf_op jit(solution)/shard_map/pallas_call | solution.py:222
  87.8 2.3 %shard_map.77 = (f32[192,384]{1,0:T(8,128)S(1)}, f32[192,192]{1,0:T(8,128)S(1)}) custom-call(s32[4]{0:T(128)S(1)} %copy-done.1, f32[192,2048]{1,0:T(8,128)S(1)} %shard_map.74.refs_0_, bf16[8,24,1024]{2,1,0:T(8,128)(2,1)S(1)} %shard_map.75.refs_1_, bf16[8,24,1024]{2,1,0:T(8,128)(2,1)S(1)} %shard_map.76.refs_2_, ...), custom_call_target="tpu_custom_call" | custom-call | tf_op jit(solution)/shard_map/pallas_call | solution.py:183
  90.1 1.8 %collective-permute-start.38 = (f32[4,24,192]{2,1,0:T(8,128)S(1)}, f32[4,24,192]{2,1,0:T(8,128)S(1)}, u32[]{:S(2)}, u32[]{:S(2)}) collective-permute-start(f32[4,24,192]{2,1,0:T(8,128)S(1)} %dynamic-slice_bitcast_fusion.1), channel_id=1, source_target_pairs={{0,1},{1,0},{2,3},{3,2},{4,5},{5,4},{6,7},{7,6},{8,9},{9,8},{10,11... | collective-permute-start | bytes 221192 | tf_op jit(solution)/shard_map/ppermute | solution.py:307
  92.3 3.3 %collective-permute-done.38 = f32[4,24,192]{2,1,0:T(8,128)S(1)} collective-permute-done((f32[4,24,192]{2,1,0:T(8,128)S(1)}, f32[4,24,192]{2,1,0:T(8,128)S(1)}, u32[]{:S(2)}, u32[]{:S(2)}) %collective-permute-start.38) | collective-permute-done | bytes 73760 | tf_op jit(solution)/shard_map/ppermute | solution.py:307
  95.6 1.8 %collective-permute-start.39 = (f32[1,24,192]{2,1,0:T(8,128)S(1)}, f32[1,24,192]{2,1,0:T(8,128)S(1)}, u32[]{:S(2)}, u32[]{:S(2)}) collective-permute-start(f32[1,24,192]{2,1,0:T(8,128)S(1)} %get-tuple-element.64), channel_id=1, source_target_pairs={{0,2},{1,3},{2,0},{3,1},{4,6},{5,7},{6,4},{7,5},{8,10},{9,11},{10,... | collective-permute-start | bytes 55304 | tf_op jit(solution)/shard_map/ppermute | solution.py:309
  97.4 1.7 %collective-permute-start.41 = (f32[1,24,192]{2,1,0:T(8,128)S(1)}, f32[1,24,192]{2,1,0:T(8,128)S(1)}, u32[]{:S(2)}, u32[]{:S(2)}) collective-permute-start(f32[1,24,192]{2,1,0:T(8,128)S(1)} %get-tuple-element.65), channel_id=1, source_target_pairs={{0,6},{1,7},{2,4},{3,5},{4,2},{5,3},{6,0},{7,1},{8,14},{9,15},{10,... | collective-permute-start | bytes 55304 | tf_op jit(solution)/shard_map/ppermute | solution.py:309
  99.2 2.7 %collective-permute-start.35 = (f32[1,24,384]{2,1,0:T(8,128)S(1)}, f32[1,24,384]{2,1,0:T(8,128)S(1)}, u32[]{:S(2)}, u32[]{:S(2)}) collective-permute-start(f32[1,24,384]{2,1,0:T(8,128)S(1)} %get-tuple-element.61), channel_id=1, source_target_pairs={{0,2},{1,3},{2,0},{3,1},{4,6},{5,7},{6,4},{7,5},{8,10},{9,11},{10,... | collective-permute-start | bytes 110600 | tf_op jit(solution)/shard_map/ppermute | solution.py:309
  101.9 1.7 %collective-permute-start.37 = (f32[1,24,384]{2,1,0:T(8,128)S(1)}, f32[1,24,384]{2,1,0:T(8,128)S(1)}, u32[]{:S(2)}, u32[]{:S(2)}) collective-permute-start(f32[1,24,384]{2,1,0:T(8,128)S(1)} %get-tuple-element.62), channel_id=1, source_target_pairs={{0,6},{1,7},{2,4},{3,5},{4,2},{5,3},{6,0},{7,1},{8,14},{9,15},{10,... | collective-permute-start | bytes 110600 | tf_op jit(solution)/shard_map/ppermute | solution.py:309
  104.1 1.8 %collective-permute-start.43 = (f32[1,24,192]{2,1,0:T(8,128)S(1)}, f32[1,24,192]{2,1,0:T(8,128)S(1)}, u32[]{:S(2)}, u32[]{:S(2)}) collective-permute-start(f32[1,24,192]{2,1,0:T(8,128)S(1)} %add_add_fusion.1.refs_0_), channel_id=1, source_target_pairs={{0,16},{8,24},{16,0},{24,8},{1,17},{9,25},{17,1},{25,9},{2,18},{10... | collective-permute-start | bytes 55304 | tf_op jit(solution)/shard_map/ppermute | solution.py:313
  106.0 1.7 %collective-permute-done.37 = f32[1,24,384]{2,1,0:T(8,128)S(1)} collective-permute-done((f32[1,24,384]{2,1,0:T(8,128)S(1)}, f32[1,24,384]{2,1,0:T(8,128)S(1)}, u32[]{:S(2)}, u32[]{:S(2)}) %collective-permute-start.37) | collective-permute-done | bytes 36896 | tf_op jit(solution)/shard_map/ppermute | solution.py:309
  (84 shorter events, 19.9 us)
Async XLA Ops:
  3.2 8.8 %collective-permute-start.3 = (bf16[24,4096]{1,0:T(8,128)(2,1)S(1)}, bf16[24,4096]{1,0:T(8,128)(2,1)S(1)}, u32[]{:S(2)}, u32[]{:S(2)}) collective-permute-start(bf16[24,4096]{1,0:T(8,128)(2,1)S(1)} %get-tuple-element.33.refs_0_.refs_8_), channel_id=1, source_target_pairs={{2,0},{4,2},{6,4},{7,6},{5,7},{3,5},{1,3},{0,1},{10,8},{12,10},{14... | collective-permute-start | bytes 589832 | tf_op jit(solution)/shard_map/ppermute | solution.py:253
  6.2 7.8 %collective-permute-start.13 = (bf16[24,4096]{1,0:T(8,128)(2,1)S(1)}, bf16[24,4096]{1,0:T(8,128)(2,1)S(1)}, u32[]{:S(2)}, u32[]{:S(2)}) collective-permute-start(bf16[24,4096]{1,0:T(8,128)(2,1)S(1)} %get-tuple-element.36.refs_0_), channel_id=1, source_target_pairs={{0,2},{2,4},{4,6},{6,7},{7,5},{5,3},{3,1},{1,0},{8,10},{10,12},{12... | collective-permute-start | bytes 589832 | tf_op jit(solution)/shard_map/ppermute | solution.py:253
  6.3 11.9 %collective-permute-start = (bf16[24,4096]{1,0:T(8,128)(2,1)S(1)}, bf16[24,4096]{1,0:T(8,128)(2,1)S(1)}, u32[]{:S(2)}, u32[]{:S(2)}) collective-permute-start(bf16[24,4096]{1,0:T(8,128)(2,1)S(1)} %get-tuple-element.33.refs_0_.refs_8_), channel_id=1, source_target_pairs={{0,2},{2,4},{4,6},{6,7},{7,5},{5,3},{3,1},{1,0},{8,10},{10,12},{12... | collective-permute-start | bytes 589832 | tf_op jit(solution)/shard_map/ppermute | solution.py:253
  8.3 10.0 %collective-permute-start.16 = (bf16[24,4096]{1,0:T(8,128)(2,1)S(1)}, bf16[24,4096]{1,0:T(8,128)(2,1)S(1)}, u32[]{:S(2)}, u32[]{:S(2)}) collective-permute-start(bf16[24,4096]{1,0:T(8,128)(2,1)S(1)} %get-tuple-element.36.refs_0_), channel_id=1, source_target_pairs={{2,0},{4,2},{6,4},{7,6},{5,7},{3,5},{1,3},{0,1},{10,8},{12,10},{14... | collective-permute-start | bytes 589832 | tf_op jit(solution)/shard_map/ppermute | solution.py:253
  12.0 8.4 %collective-permute-start.4 = (bf16[24,4096]{1,0:T(8,128)(2,1)S(1)}, bf16[24,4096]{1,0:T(8,128)(2,1)S(1)}, u32[]{:S(2)}, u32[]{:S(2)}) collective-permute-start(bf16[24,4096]{1,0:T(8,128)(2,1)S(1)} %collective-permute-done.3.refs_2_.refs_10_), channel_id=1, source_target_pairs={{2,0},{4,2},{6,4},{7,6},{5,7},{3,5},{1,3},{0,1},{10,8},{12,10},{14... | collective-permute-start | bytes 589832 | tf_op jit(solution)/shard_map/ppermute | solution.py:253
  14.0 8.4 %collective-permute-start.14 = (bf16[24,4096]{1,0:T(8,128)(2,1)S(1)}, bf16[24,4096]{1,0:T(8,128)(2,1)S(1)}, u32[]{:S(2)}, u32[]{:S(2)}) collective-permute-start(bf16[24,4096]{1,0:T(8,128)(2,1)S(1)} %collective-permute-done.13.refs_1_), channel_id=1, source_target_pairs={{0,2},{2,4},{4,6},{6,7},{7,5},{5,3},{3,1},{1,0},{8,10},{10,12},{12... | collective-permute-start | bytes 589832 | tf_op jit(solution)/shard_map/ppermute | solution.py:253
  18.2 8.4 %collective-permute-start.1 = (bf16[24,4096]{1,0:T(8,128)(2,1)S(1)}, bf16[24,4096]{1,0:T(8,128)(2,1)S(1)}, u32[]{:S(2)}, u32[]{:S(2)}) collective-permute-start(bf16[24,4096]{1,0:T(8,128)(2,1)S(1)} %collective-permute-done.refs_1_.refs_9_), channel_id=1, source_target_pairs={{0,2},{2,4},{4,6},{6,7},{7,5},{5,3},{3,1},{1,0},{8,10},{10,12},{12... | collective-permute-start | bytes 589832 | tf_op jit(solution)/shard_map/ppermute | solution.py:253
  18.4 8.4 %collective-permute-start.17 = (bf16[24,4096]{1,0:T(8,128)(2,1)S(1)}, bf16[24,4096]{1,0:T(8,128)(2,1)S(1)}, u32[]{:S(2)}, u32[]{:S(2)}) collective-permute-start(bf16[24,4096]{1,0:T(8,128)(2,1)S(1)} %collective-permute-done.16.refs_2_), channel_id=1, source_target_pairs={{2,0},{4,2},{6,4},{7,6},{5,7},{3,5},{1,3},{0,1},{10,8},{12,10},{14... | collective-permute-start | bytes 589832 | tf_op jit(solution)/shard_map/ppermute | solution.py:253
  20.4 8.7 %collective-permute-start.5 = (bf16[24,4096]{1,0:T(8,128)(2,1)S(1)}, bf16[24,4096]{1,0:T(8,128)(2,1)S(1)}, u32[]{:S(2)}, u32[]{:S(2)}) collective-permute-start(bf16[24,4096]{1,0:T(8,128)(2,1)S(1)} %collective-permute-done.4.refs_4_.refs_12_), channel_id=1, source_target_pairs={{2,0},{4,2},{6,4},{7,6},{5,7},{3,5},{1,3},{0,1},{10,8},{12,10},{14... | collective-permute-start | bytes 589832 | tf_op jit(solution)/shard_map/ppermute | solution.py:253
  22.4 8.7 %collective-permute-start.15 = (bf16[24,4096]{1,0:T(8,128)(2,1)S(1)}, bf16[24,4096]{1,0:T(8,128)(2,1)S(1)}, u32[]{:S(2)}, u32[]{:S(2)}) collective-permute-start(bf16[24,4096]{1,0:T(8,128)(2,1)S(1)} %collective-permute-done.14.refs_3_), channel_id=1, source_target_pairs={{0,2},{2,4},{4,6},{6,7},{7,5},{5,3},{3,1},{1,0},{8,10},{10,12},{12... | collective-permute-start | bytes 589832 | tf_op jit(solution)/shard_map/ppermute | solution.py:253
  26.7 8.4 %collective-permute-start.2 = (bf16[24,4096]{1,0:T(8,128)(2,1)S(1)}, bf16[24,4096]{1,0:T(8,128)(2,1)S(1)}, u32[]{:S(2)}, u32[]{:S(2)}) collective-permute-start(bf16[24,4096]{1,0:T(8,128)(2,1)S(1)} %collective-permute-done.1.refs_3_.refs_11_), channel_id=1, source_target_pairs={{0,2},{2,4},{4,6},{6,7},{7,5},{5,3},{3,1},{1,0},{8,10},{10,12},{12... | collective-permute-start | bytes 589832 | tf_op jit(solution)/shard_map/ppermute | solution.py:253
  26.8 10.3 %collective-permute-start.18 = (bf16[24,4096]{1,0:T(8,128)(2,1)S(1)}, bf16[24,4096]{1,0:T(8,128)(2,1)S(1)}, u32[]{:S(2)}, u32[]{:S(2)}) collective-permute-start(bf16[24,4096]{1,0:T(8,128)(2,1)S(1)} %collective-permute-done.17.refs_4_), channel_id=1, source_target_pairs={{2,0},{4,2},{6,4},{7,6},{5,7},{3,5},{1,3},{0,1},{10,8},{12,10},{14... | collective-permute-start | bytes 589832 | tf_op jit(solution)/shard_map/ppermute | solution.py:253
  29.1 9.6 %collective-permute-start.26 = (bf16[24,4096]{1,0:T(8,128)(2,1)S(1)}, bf16[24,4096]{1,0:T(8,128)(2,1)S(1)}, u32[]{:S(2)}, u32[]{:S(2)}) collective-permute-start(bf16[24,4096]{1,0:T(8,128)(2,1)S(1)} %collective-permute-done.5.refs_6_.refs_14_), channel_id=1, source_target_pairs={{2,0},{4,2},{6,4},{7,6},{5,7},{3,5},{1,3},{0,1},{10,8},{12,10},{14... | collective-permute-start | bytes 589832 | tf_op jit(solution)/shard_map/ppermute | solution.py:258
  31.1 9.6 %collective-permute-start.21 = (bf16[24,4096]{1,0:T(8,128)(2,1)S(1)}, bf16[24,4096]{1,0:T(8,128)(2,1)S(1)}, u32[]{:S(2)}, u32[]{:S(2)}) collective-permute-start(bf16[24,4096]{1,0:T(8,128)(2,1)S(1)} %collective-permute-done.15.refs_5_), channel_id=1, source_target_pairs={{0,2},{2,4},{4,6},{6,7},{7,5},{5,3},{3,1},{1,0},{8,10},{10,12},{12... | collective-permute-start | bytes 589832 | tf_op jit(solution)/shard_map/ppermute | solution.py:257
  35.1 13.5 %collective-permute-start.7 = (bf16[24,4096]{1,0:T(8,128)(2,1)S(1)}, bf16[24,4096]{1,0:T(8,128)(2,1)S(1)}, u32[]{:S(2)}, u32[]{:S(2)}) collective-permute-start(bf16[24,4096]{1,0:T(8,128)(2,1)S(1)} %get-tuple-element.51.refs_0_.refs_8_), channel_id=1, source_target_pairs={{2,0},{4,2},{6,4},{7,6},{5,7},{3,5},{1,3},{0,1},{10,8},{12,10},{14... | collective-permute-start | bytes 589832 | tf_op jit(solution)/shard_map/ppermute | solution.py:253
  36.7 17.3 %collective-permute-start.6 = (bf16[24,4096]{1,0:T(8,128)(2,1)S(1)}, bf16[24,4096]{1,0:T(8,128)(2,1)S(1)}, u32[]{:S(2)}, u32[]{:S(2)}) collective-permute-start(bf16[24,4096]{1,0:T(8,128)(2,1)S(1)} %get-tuple-element.51.refs_0_.refs_8_), channel_id=1, source_target_pairs={{0,2},{2,4},{4,6},{6,7},{7,5},{5,3},{3,1},{1,0},{8,10},{10,12},{12... | collective-permute-start | bytes 589832 | tf_op jit(solution)/shard_map/ppermute | solution.py:253
  37.1 9.4 %collective-permute-start.20 = (bf16[24,4096]{1,0:T(8,128)(2,1)S(1)}, bf16[24,4096]{1,0:T(8,128)(2,1)S(1)}, u32[]{:S(2)}, u32[]{:S(2)}) collective-permute-start(bf16[24,4096]{1,0:T(8,128)(2,1)S(1)} %get-tuple-element.43.refs_0_), channel_id=1, source_target_pairs={{2,0},{4,2},{6,4},{7,6},{5,7},{3,5},{1,3},{0,1},{10,8},{12,10},{14... | collective-permute-start | bytes 589832 | tf_op jit(solution)/shard_map/ppermute | solution.py:253
  38.7 7.8 %collective-permute-start.19 = (bf16[24,4096]{1,0:T(8,128)(2,1)S(1)}, bf16[24,4096]{1,0:T(8,128)(2,1)S(1)}, u32[]{:S(2)}, u32[]{:S(2)}) collective-permute-start(bf16[24,4096]{1,0:T(8,128)(2,1)S(1)} %get-tuple-element.43.refs_0_), channel_id=1, source_target_pairs={{0,2},{2,4},{4,6},{6,7},{7,5},{5,3},{3,1},{1,0},{8,10},{10,12},{12... | collective-permute-start | bytes 589832 | tf_op jit(solution)/shard_map/ppermute | solution.py:253
  40.8 29.2 %collective-permute-start.29 = (bf16[8,24,1024]{2,1,0:T(8,128)(2,1)S(1)}, bf16[8,24,1024]{2,1,0:T(8,128)(2,1)S(1)}, u32[]{:S(2)}, u32[]{:S(2)}) collective-permute-start(bf16[8,24,1024]{2,1,0:T(8,128)(2,1)S(1)} %shard_map.75.refs_1_), channel_id=1, source_target_pairs={{0,16},{8,24},{16,0},{24,8},{1,17},{9,25},{17,1},{25,9},{2,18},{10... | collective-permute-start | bytes 1179656 | tf_op jit(solution)/shard_map/ppermute | solution.py:233
  46.5 8.2 %collective-permute-start.22 = (bf16[24,4096]{1,0:T(8,128)(2,1)S(1)}, bf16[24,4096]{1,0:T(8,128)(2,1)S(1)}, u32[]{:S(2)}, u32[]{:S(2)}) collective-permute-start(bf16[24,4096]{1,0:T(8,128)(2,1)S(1)} %collective-permute-done.19.refs_1_), channel_id=1, source_target_pairs={{0,2},{2,4},{4,6},{6,7},{7,5},{5,3},{3,1},{1,0},{8,10},{10,12},{12... | collective-permute-start | bytes 589832 | tf_op jit(solution)/shard_map/ppermute | solution.py:253
  48.2 13.4 %collective-permute-start.23 = (bf16[24,4096]{1,0:T(8,128)(2,1)S(1)}, bf16[24,4096]{1,0:T(8,128)(2,1)S(1)}, u32[]{:S(2)}, u32[]{:S(2)}) collective-permute-start(bf16[24,4096]{1,0:T(8,128)(2,1)S(1)} %collective-permute-done.20.refs_2_), channel_id=1, source_target_pairs={{2,0},{4,2},{6,4},{7,6},{5,7},{3,5},{1,3},{0,1},{10,8},{12,10},{14... | collective-permute-start | bytes 589832 | tf_op jit(solution)/shard_map/ppermute | solution.py:253
  48.6 8.9 %collective-permute-start.9 = (bf16[24,4096]{1,0:T(8,128)(2,1)S(1)}, bf16[24,4096]{1,0:T(8,128)(2,1)S(1)}, u32[]{:S(2)}, u32[]{:S(2)}) collective-permute-start(bf16[24,4096]{1,0:T(8,128)(2,1)S(1)} %collective-permute-done.7.refs_2_.refs_10_), channel_id=1, source_target_pairs={{2,0},{4,2},{6,4},{7,6},{5,7},{3,5},{1,3},{0,1},{10,8},{12,10},{14... | collective-permute-start | bytes 589832 | tf_op jit(solution)/shard_map/ppermute | solution.py:253
  53.9 8.6 %collective-permute-start.8 = (bf16[24,4096]{1,0:T(8,128)(2,1)S(1)}, bf16[24,4096]{1,0:T(8,128)(2,1)S(1)}, u32[]{:S(2)}, u32[]{:S(2)}) collective-permute-start(bf16[24,4096]{1,0:T(8,128)(2,1)S(1)} %collective-permute-done.6.refs_1_.refs_9_), channel_id=1, source_target_pairs={{0,2},{2,4},{4,6},{6,7},{7,5},{5,3},{3,1},{1,0},{8,10},{10,12},{12... | collective-permute-start | bytes 589832 | tf_op jit(solution)/shard_map/ppermute | solution.py:253
  54.8 9.0 %collective-permute-start.24 = (bf16[24,4096]{1,0:T(8,128)(2,1)S(1)}, bf16[24,4096]{1,0:T(8,128)(2,1)S(1)}, u32[]{:S(2)}, u32[]{:S(2)}) collective-permute-start(bf16[24,4096]{1,0:T(8,128)(2,1)S(1)} %collective-permute-done.22.refs_3_), channel_id=1, source_target_pairs={{0,2},{2,4},{4,6},{6,7},{7,5},{5,3},{3,1},{1,0},{8,10},{10,12},{12... | collective-permute-start | bytes 589832 | tf_op jit(solution)/shard_map/ppermute | solution.py:253
  57.5 8.2 %collective-permute-start.11 = (bf16[24,4096]{1,0:T(8,128)(2,1)S(1)}, bf16[24,4096]{1,0:T(8,128)(2,1)S(1)}, u32[]{:S(2)}, u32[]{:S(2)}) collective-permute-start(bf16[24,4096]{1,0:T(8,128)(2,1)S(1)} %collective-permute-done.9.refs_4_.refs_12_), channel_id=1, source_target_pairs={{2,0},{4,2},{6,4},{7,6},{5,7},{3,5},{1,3},{0,1},{10,8},{12,10},{14... | collective-permute-start | bytes 589832 | tf_op jit(solution)/shard_map/ppermute | solution.py:253
  61.6 8.3 %collective-permute-start.25 = (bf16[24,4096]{1,0:T(8,128)(2,1)S(1)}, bf16[24,4096]{1,0:T(8,128)(2,1)S(1)}, u32[]{:S(2)}, u32[]{:S(2)}) collective-permute-start(bf16[24,4096]{1,0:T(8,128)(2,1)S(1)} %collective-permute-done.23.refs_4_), channel_id=1, source_target_pairs={{2,0},{4,2},{6,4},{7,6},{5,7},{3,5},{1,3},{0,1},{10,8},{12,10},{14... | collective-permute-start | bytes 589832 | tf_op jit(solution)/shard_map/ppermute | solution.py:253
  63.8 7.6 %collective-permute-start.27 = (bf16[24,4096]{1,0:T(8,128)(2,1)S(1)}, bf16[24,4096]{1,0:T(8,128)(2,1)S(1)}, u32[]{:S(2)}, u32[]{:S(2)}) collective-permute-start(bf16[24,4096]{1,0:T(8,128)(2,1)S(1)} %collective-permute-done.24.refs_5_), channel_id=1, source_target_pairs={{0,2},{2,4},{4,6},{6,7},{7,5},{5,3},{3,1},{1,0},{8,10},{10,12},{12... | collective-permute-start | bytes 589832 | tf_op jit(solution)/shard_map/ppermute | solution.py:257
  69.9 17.9 %collective-permute-start.28 = (bf16[8,24,1024]{2,1,0:T(8,128)(2,1)S(1)}, bf16[8,24,1024]{2,1,0:T(8,128)(2,1)S(1)}, u32[]{:S(2)}, u32[]{:S(2)}) collective-permute-start(bf16[8,24,1024]{2,1,0:T(8,128)(2,1)S(1)} %shard_map.75.refs_1_), channel_id=1, source_target_pairs={{0,8},{8,0},{16,24},{24,16},{1,9},{9,1},{17,25},{25,17},{2,10},{10... | collective-permute-start | bytes 1179656 | tf_op jit(solution)/shard_map/ppermute | solution.py:234
  70.0 17.8 %collective-permute-start.30 = (bf16[8,24,1024]{2,1,0:T(8,128)(2,1)S(1)}, bf16[8,24,1024]{2,1,0:T(8,128)(2,1)S(1)}, u32[]{:S(2)}, u32[]{:S(2)}) collective-permute-start(bf16[8,24,1024]{2,1,0:T(8,128)(2,1)S(1)} %collective-permute-done.29.refs_4_), channel_id=1, source_target_pairs={{0,8},{8,0},{16,24},{24,16},{1,9},{9,1},{17,25},{25,17},{2,10},{10... | collective-permute-start | bytes 1179656 | tf_op jit(solution)/shard_map/ppermute | solution.py:239
  71.4 11.7 %collective-permute-start.32 = (bf16[8,24,1024]{2,1,0:T(8,128)(2,1)S(1)}, bf16[8,24,1024]{2,1,0:T(8,128)(2,1)S(1)}, u32[]{:S(2)}, u32[]{:S(2)}) collective-permute-start(bf16[8,24,1024]{2,1,0:T(8,128)(2,1)S(1)} %shard_map.76.refs_2_), channel_id=1, source_target_pairs={{0,16},{8,24},{16,0},{24,8},{1,17},{9,25},{17,1},{25,9},{2,18},{10... | collective-permute-start | bytes 1179656 | tf_op jit(solution)/shard_map/ppermute | solution.py:233
  72.5 15.2 %collective-permute-start.31 = (bf16[8,24,1024]{2,1,0:T(8,128)(2,1)S(1)}, bf16[8,24,1024]{2,1,0:T(8,128)(2,1)S(1)}, u32[]{:S(2)}, u32[]{:S(2)}) collective-permute-start(bf16[8,24,1024]{2,1,0:T(8,128)(2,1)S(1)} %shard_map.76.refs_2_), channel_id=1, source_target_pairs={{0,8},{8,0},{16,24},{24,16},{1,9},{9,1},{17,25},{25,17},{2,10},{10... | collective-permute-start | bytes 1179656 | tf_op jit(solution)/shard_map/ppermute | solution.py:234
  95.6 8.0 %collective-permute-start.39 = (f32[1,24,192]{2,1,0:T(8,128)S(1)}, f32[1,24,192]{2,1,0:T(8,128)S(1)}, u32[]{:S(2)}, u32[]{:S(2)}) collective-permute-start(f32[1,24,192]{2,1,0:T(8,128)S(1)} %get-tuple-element.64), channel_id=1, source_target_pairs={{0,2},{1,3},{2,0},{3,1},{4,6},{5,7},{6,4},{7,5},{8,10},{9,11},{10,... | collective-permute-start | bytes 55304 | tf_op jit(solution)/shard_map/ppermute | solution.py:309
  (16 other events, 76.6 us)

commit v4 on v3

--- a/solution.py
+++ b/solution.py
@@ -156,7 +156,7 @@
 
     width = own_refs[0].shape[2]
     own = [stack([ref[i] for i in range(n)]) for ref in own_refs]
-    diag = sum(contract(image[:, k * width : (k + 1) * width], own[k]) for k in range(2))
+    diag = contract(image, jnp.concatenate(own, axis=1))
     for k in range(2):
         for flip, ref in enumerate((own_refs[k], *other_refs[3 * k : 3 * k + 3])):
 
@@ -203,7 +203,7 @@
     return tuple(call(kernel, out, [SCALARS] + [WHOLE] * 5)(partner, cross, *blocks))
 
 
-def multiply(chunk, first, count, pieces, mat, before, later=()):
+def multiply(chunk, first, count, pieces, mat, before):
     n = len(pieces)
     rows, width = pieces[0].shape
     depth, size, cols = width // n, n * rows, mat.shape[1]
@@ -218,8 +218,8 @@
     fresh = before is None
     kernel = functools.partial(part_kernel, chunk, first, n, fresh)
     before = mat if fresh else before
-    specs = [WHOLE] * n + [HBM, HBM if fresh else WHOLE] + [HBM] * len(later)
-    return call(kernel, total, specs, scratch, flops, moved)(*pieces, mat, before, *later)
+    specs = [WHOLE] * n + [HBM, HBM if fresh else WHOLE]
+    return call(kernel, total, specs, scratch, flops, moved)(*pieces, mat, before)
 
 
 WEIGHT = 3
@@ -261,9 +261,9 @@
     parts = cut(codes, exponents, n)
     lanes = [(p, p, [p]) for p in parts[:2]]
     for _ in range(1, n // 2):
-        lanes = [both_ways(lane) for lane in lanes]
+        before, lanes = lanes, [both_ways(lane) for lane in lanes]
     early = last_hops(lanes)
-    starts = [after(p, *lane[:2]) for p, lane in zip(parts[2:], lanes)]
+    starts = [after(parts[2], *before[1][:2]), after(parts[3], *lanes[0][:2])]
     lanes = [(p, p, [p]) for p in starts]
 
     first_own = slabs(early, n)
@@ -295,7 +295,7 @@
     sums = [block.reshape(n, rows, block.shape[1]) for block in (pair, cross)]
     bit = 1
     while bit < n:
-        radix = 4 if 1 < bit < n // 2 else 2
+        radix = 4 if bit < n // 2 else 2
         mine = (me // bit) % radix
         for at, block in enumerate(sums):
             split = block.reshape(block.shape[0] // radix, radix, *block.shape[1:])

time: 110 us -> 108 us (0.982)
  waiting for transfers between devices: 24.8 us -> 20 us
  starting transfers between devices: 47 us -> 49.9 us
    ppermute x12, starting transfers between devices: 10.3 us -> 19.6 us  [both_ways(): lax.ppermute(up, 'wide', forth)]
    ppermute x12, waiting for transfers between devices: 12.2 us -> 3.82 us  [both_ways(): lax.ppermute(up, 'wide', forth)]
    ppermute x12, starting transfers between devices: 16.6 us -> 8.29 us  [both_ways(): lax.ppermute(down, 'wide', back)]
    ppermute x12, waiting for transfers between devices: 5.42 us -> 10.5 us  [both_ways(): lax.ppermute(down, 'wide', back)]
    ppermute x8, waiting for transfers between devices: 6.19 us -> 3.03 us  [shards(): block += lax.ppermute(given, 'wide', ways)]
    ppermute x2, starting transfers between devices: 2.04 us -> 4.77 us  [last_hops(): one = lax.ppermute(lanes[0][0], 'wide', forth)]
    ppermute x2, starting transfers between devices: 2.11 us -> 0.01 us  [last_hops(): two = lax.ppermute(lanes[1][1], 'wide', back)]
    ppermute x8, starting transfers between devices: 10.1 us -> 11.8 us  [shards(): block += lax.ppermute(given, 'wide', ways)]
  transfers between devices with their start and end apart: 45 -> 45, of which waited for: 12 -> 12; matrix products, arithmetic and copies ran while one was open for 0% -> 0% of each run, Pallas kernels for 28% -> 29%
where the time goes in v4:
time: 108 us
  starting transfers between devices  49.9 us (46%)
  Pallas kernels  35.2 us (33%)
  waiting for transfers between devices  20 us (19%)
  local copies, waits for them, and re-layouts  1.84 us (2%)
    pallas_call x7, Pallas kernels, multiply(): call(kernel, total, specs, scratch, flops, moved)(*pieces, mat, before)  30.8 us
    ppermute x12, starting transfers between devices, both_ways(): lax.ppermute(up, 'wide', forth)  19.6 us
    ppermute x8, starting transfers between devices, shards(): block += lax.ppermute(given, 'wide', ways)  11.8 us
    ppermute x12, waiting for transfers between devices, both_ways(): lax.ppermute(down, 'wide', back)  10.5 us
    ppermute x12, starting transfers between devices, both_ways(): lax.ppermute(down, 'wide', back)  8.29 us
    ppermute x2, starting transfers between devices, last_hops(): one = lax.ppermute(lanes[0][0], 'wide', forth)  4.77 us
    ppermute x12, waiting for transfers between devices, both_ways(): lax.ppermute(up, 'wide', forth)  3.82 us
    ppermute x8, waiting for transfers between devices, shards(): block += lax.ppermute(given, 'wide', ways)  3.03 us
  transfers between devices with their start and end apart: 45, of which 12 were waited for; matrix products, arithmetic and copies ran while one was open for 0% of the time, Pallas kernels for 29%

profile of v4, /device:TPU:0, one launch (start us, length us, event | category | flops | bytes accessed | tf_op | source)
XLA Modules:
  0.0 107.9 jit_solution(16401198759917448321)
XLA Ops:
  3.2 3.1 %collective-permute-start = (bf16[24,4096]{1,0:T(8,128)(2,1)S(1)}, bf16[24,4096]{1,0:T(8,128)(2,1)S(1)}, u32[]{:S(2)}, u32[]{:S(2)}) collective-permute-start(bf16[24,4096]{1,0:T(8,128)(2,1)S(1)} %get-tuple-element.33.refs_0_), channel_id=1, source_target_pairs={{0,2},{2,4},{4,6},{6,7},{7,5},{5,3},{3,1},{1,0},{8,10},{10,12},{12... | collective-permute-start | bytes 589832 | tf_op jit(solution)/shard_map/ppermute | solution.py:253
  6.3 1.9 %collective-permute-start.3 = (bf16[24,4096]{1,0:T(8,128)(2,1)S(1)}, bf16[24,4096]{1,0:T(8,128)(2,1)S(1)}, u32[]{:S(2)}, u32[]{:S(2)}) collective-permute-start(bf16[24,4096]{1,0:T(8,128)(2,1)S(1)} %get-tuple-element.33.refs_0_), channel_id=1, source_target_pairs={{2,0},{4,2},{6,4},{7,6},{5,7},{3,5},{1,3},{0,1},{10,8},{12,10},{14... | collective-permute-start | bytes 589832 | tf_op jit(solution)/shard_map/ppermute | solution.py:253
  8.3 3.6 %collective-permute-done.refs_1_ = bf16[24,4096]{1,0:T(8,128)(2,1)S(1)} collective-permute-done((bf16[24,4096]{1,0:T(8,128)(2,1)S(1)}, bf16[24,4096]{1,0:T(8,128)(2,1)S(1)}, u32[]{:S(2)}, u32[]{:S(2)}) %collective-permute-start) | collective-permute-done | bytes 196640 | tf_op jit(solution)/shard_map/ppermute | solution.py:253
  11.9 2.1 %collective-permute-start.1 = (bf16[24,4096]{1,0:T(8,128)(2,1)S(1)}, bf16[24,4096]{1,0:T(8,128)(2,1)S(1)}, u32[]{:S(2)}, u32[]{:S(2)}) collective-permute-start(bf16[24,4096]{1,0:T(8,128)(2,1)S(1)} %collective-permute-done.refs_1_), channel_id=1, source_target_pairs={{0,2},{2,4},{4,6},{6,7},{7,5},{5,3},{3,1},{1,0},{8,10},{10,12},{12... | collective-permute-start | bytes 589832 | tf_op jit(solution)/shard_map/ppermute | solution.py:253
  14.1 4.2 %collective-permute-done.3.refs_2_ = bf16[24,4096]{1,0:T(8,128)(2,1)S(1)} collective-permute-done((bf16[24,4096]{1,0:T(8,128)(2,1)S(1)}, bf16[24,4096]{1,0:T(8,128)(2,1)S(1)}, u32[]{:S(2)}, u32[]{:S(2)}) %collective-permute-start.3) | collective-permute-done | bytes 196640 | tf_op jit(solution)/shard_map/ppermute | solution.py:253
  18.3 2.0 %collective-permute-start.14 = (bf16[24,4096]{1,0:T(8,128)(2,1)S(1)}, bf16[24,4096]{1,0:T(8,128)(2,1)S(1)}, u32[]{:S(2)}, u32[]{:S(2)}) collective-permute-start(bf16[24,4096]{1,0:T(8,128)(2,1)S(1)} %collective-permute-done.13.refs_1_.refs_9_), channel_id=1, source_target_pairs={{0,2},{2,4},{4,6},{6,7},{7,5},{5,3},{3,1},{1,0},{8,10},{10,12},{12... | collective-permute-start | bytes 589832 | tf_op jit(solution)/shard_map/ppermute | solution.py:253
  20.4 2.1 %collective-permute-start.2 = (bf16[24,4096]{1,0:T(8,128)(2,1)S(1)}, bf16[24,4096]{1,0:T(8,128)(2,1)S(1)}, u32[]{:S(2)}, u32[]{:S(2)}) collective-permute-start(bf16[24,4096]{1,0:T(8,128)(2,1)S(1)} %collective-permute-done.1.refs_3_), channel_id=1, source_target_pairs={{0,2},{2,4},{4,6},{6,7},{7,5},{5,3},{3,1},{1,0},{8,10},{10,12},{12... | collective-permute-start | bytes 589832 | tf_op jit(solution)/shard_map/ppermute | solution.py:253
  22.5 4.2 %collective-permute-done.4.refs_4_ = bf16[24,4096]{1,0:T(8,128)(2,1)S(1)} collective-permute-done((bf16[24,4096]{1,0:T(8,128)(2,1)S(1)}, bf16[24,4096]{1,0:T(8,128)(2,1)S(1)}, u32[]{:S(2)}, u32[]{:S(2)}) %collective-permute-start.4) | collective-permute-done | bytes 196640 | tf_op jit(solution)/shard_map/ppermute | solution.py:253
  26.8 2.0 %collective-permute-start.24 = (bf16[24,4096]{1,0:T(8,128)(2,1)S(1)}, bf16[24,4096]{1,0:T(8,128)(2,1)S(1)}, u32[]{:S(2)}, u32[]{:S(2)}) collective-permute-start(bf16[24,4096]{1,0:T(8,128)(2,1)S(1)} %collective-permute-done.14.refs_3_.refs_11_), channel_id=1, source_target_pairs={{0,2},{2,4},{4,6},{6,7},{7,5},{5,3},{3,1},{1,0},{8,10},{10,12},{12... | collective-permute-start | bytes 589832 | tf_op jit(solution)/shard_map/ppermute | solution.py:253
  29.0 2.2 %collective-permute-start.19 = (bf16[24,4096]{1,0:T(8,128)(2,1)S(1)}, bf16[24,4096]{1,0:T(8,128)(2,1)S(1)}, u32[]{:S(2)}, u32[]{:S(2)}) collective-permute-start(bf16[24,4096]{1,0:T(8,128)(2,1)S(1)} %collective-permute-done.2.refs_5_), channel_id=1, source_target_pairs={{0,2},{2,4},{4,6},{6,7},{7,5},{5,3},{3,1},{1,0},{8,10},{10,12},{12... | collective-permute-start | bytes 589832 | tf_op jit(solution)/shard_map/ppermute | solution.py:257
  31.2 1.9 %collective-permute-start.18 = (bf16[24,4096]{1,0:T(8,128)(2,1)S(1)}, bf16[24,4096]{1,0:T(8,128)(2,1)S(1)}, u32[]{:S(2)}, u32[]{:S(2)}) collective-permute-start(bf16[24,4096]{1,0:T(8,128)(2,1)S(1)} %get-tuple-element.43.refs_0_), channel_id=1, source_target_pairs={{2,0},{4,2},{6,4},{7,6},{5,7},{3,5},{1,3},{0,1},{10,8},{12,10},{14... | collective-permute-start | bytes 589832 | tf_op jit(solution)/shard_map/ppermute | solution.py:253
  33.2 2.0 %collective-permute-done.5.refs_6_ = bf16[24,4096]{1,0:T(8,128)(2,1)S(1)} collective-permute-done((bf16[24,4096]{1,0:T(8,128)(2,1)S(1)}, bf16[24,4096]{1,0:T(8,128)(2,1)S(1)}, u32[]{:S(2)}, u32[]{:S(2)}) %collective-permute-start.5) | collective-permute-done | bytes 196640 | tf_op jit(solution)/shard_map/ppermute | solution.py:253
  35.2 1.6 %collective-permute-start.17 = (bf16[24,4096]{1,0:T(8,128)(2,1)S(1)}, bf16[24,4096]{1,0:T(8,128)(2,1)S(1)}, u32[]{:S(2)}, u32[]{:S(2)}) collective-permute-start(bf16[24,4096]{1,0:T(8,128)(2,1)S(1)} %get-tuple-element.43.refs_0_), channel_id=1, source_target_pairs={{0,2},{2,4},{4,6},{6,7},{7,5},{5,3},{3,1},{1,0},{8,10},{10,12},{12... | collective-permute-start | bytes 589832 | tf_op jit(solution)/shard_map/ppermute | solution.py:253
  37.7 2.1 %collective-permute-start.6 = (bf16[24,4096]{1,0:T(8,128)(2,1)S(1)}, bf16[24,4096]{1,0:T(8,128)(2,1)S(1)}, u32[]{:S(2)}, u32[]{:S(2)}) collective-permute-start(bf16[24,4096]{1,0:T(8,128)(2,1)S(1)} %get-tuple-element.51.refs_0_.refs_8_), channel_id=1, source_target_pairs={{0,2},{2,4},{4,6},{6,7},{7,5},{5,3},{3,1},{1,0},{8,10},{10,12},{12... | collective-permute-start | bytes 589832 | tf_op jit(solution)/shard_map/ppermute | solution.py:253
  39.8 1.6 %collective-permute-start.29 = (bf16[8,24,1024]{2,1,0:T(8,128)(2,1)S(1)}, bf16[8,24,1024]{2,1,0:T(8,128)(2,1)S(1)}, u32[]{:S(2)}, u32[]{:S(2)}) collective-permute-start(bf16[8,24,1024]{2,1,0:T(8,128)(2,1)S(1)} %shard_map.75.refs_1_), channel_id=1, source_target_pairs={{0,16},{8,24},{16,0},{24,8},{1,17},{9,25},{17,1},{25,9},{2,18},{10... | collective-permute-start | bytes 1179656 | tf_op jit(solution)/shard_map/ppermute | solution.py:233
  41.4 4.1 %shard_map.68.refs_9_ = f32[192,2048]{1,0:T(8,128)S(1)} custom-call(bf16[24,4096]{1,0:T(8,128)(2,1)S(1)} %get-tuple-element.33.refs_0_, bf16[24,4096]{1,0:T(8,128)(2,1)S(1)} %collective-permute-done.refs_1_, bf16[24,4096]{1,0:T(8,128)(2,1)S(1)} %collective-permute-done.3.refs_2_, bf16[24,4096]{1,0:T(8,128)(2,1)S(1)} %collective-permute-done.1.refs_3_, ...), custom_call_target="tpu_custom_call" | custom-call | flops 4831838208 | bytes 25165824 | tf_op jit(solution)/shard_map/pallas_call | solution.py:222
  45.5 1.6 %collective-permute-start.20 = (bf16[24,4096]{1,0:T(8,128)(2,1)S(1)}, bf16[24,4096]{1,0:T(8,128)(2,1)S(1)}, u32[]{:S(2)}, u32[]{:S(2)}) collective-permute-start(bf16[24,4096]{1,0:T(8,128)(2,1)S(1)} %collective-permute-done.17.refs_1_), channel_id=1, source_target_pairs={{0,2},{2,4},{4,6},{6,7},{7,5},{5,3},{3,1},{1,0},{8,10},{10,12},{12... | collective-permute-start | bytes 589832 | tf_op jit(solution)/shard_map/ppermute | solution.py:253
  48.6 4.0 %shard_map.69.refs_9_ = f32[192,2048]{1,0:T(8,128)S(1)} custom-call(bf16[24,4096]{1,0:T(8,128)(2,1)S(1)} %get-tuple-element.33.refs_0_, bf16[24,4096]{1,0:T(8,128)(2,1)S(1)} %collective-permute-done.refs_1_, bf16[24,4096]{1,0:T(8,128)(2,1)S(1)} %collective-permute-done.3.refs_2_, bf16[24,4096]{1,0:T(8,128)(2,1)S(1)} %collective-permute-done.1.refs_3_, ...), custom_call_target="tpu_custom_call" | custom-call | flops 4831838208 | bytes 25165824 | tf_op jit(solution)/shard_map/pallas_call | solution.py:222
  53.8 1.6 %collective-permute-start.22 = (bf16[24,4096]{1,0:T(8,128)(2,1)S(1)}, bf16[24,4096]{1,0:T(8,128)(2,1)S(1)}, u32[]{:S(2)}, u32[]{:S(2)}) collective-permute-start(bf16[24,4096]{1,0:T(8,128)(2,1)S(1)} %collective-permute-done.20.refs_3_), channel_id=1, source_target_pairs={{0,2},{2,4},{4,6},{6,7},{7,5},{5,3},{3,1},{1,0},{8,10},{10,12},{12... | collective-permute-start | bytes 589832 | tf_op jit(solution)/shard_map/ppermute | solution.py:253
  55.8 4.1 %shard_map.70.refs_9_ = f32[192,2048]{1,0:T(8,128)S(1)} custom-call(bf16[24,4096]{1,0:T(8,128)(2,1)S(1)} %get-tuple-element.36.refs_0_.refs_8_, bf16[24,4096]{1,0:T(8,128)(2,1)S(1)} %collective-permute-done.13.refs_1_.refs_9_, bf16[24,4096]{1,0:T(8,128)(2,1)S(1)} %collective-permute-done.15.refs_2_.refs_10_, ...), custom_call_target="tpu_custom_call" | custom-call | flops 4831838208 | bytes 25165824 | tf_op jit(solution)/shard_map/pallas_call | solution.py:222
  59.9 2.1 %collective-permute-start.23 = (bf16[24,4096]{1,0:T(8,128)(2,1)S(1)}, bf16[24,4096]{1,0:T(8,128)(2,1)S(1)}, u32[]{:S(2)}, u32[]{:S(2)}) collective-permute-start(bf16[24,4096]{1,0:T(8,128)(2,1)S(1)} %collective-permute-done.21.refs_4_), channel_id=1, source_target_pairs={{2,0},{4,2},{6,4},{7,6},{5,7},{3,5},{1,3},{0,1},{10,8},{12,10},{14... | collective-permute-start | bytes 589832 | tf_op jit(solution)/shard_map/ppermute | solution.py:253
  62.1 2.5 %collective-permute-start.27 = (bf16[24,4096]{1,0:T(8,128)(2,1)S(1)}, bf16[24,4096]{1,0:T(8,128)(2,1)S(1)}, u32[]{:S(2)}, u32[]{:S(2)}) collective-permute-start(bf16[24,4096]{1,0:T(8,128)(2,1)S(1)} %collective-permute-done.22.refs_5_), channel_id=1, source_target_pairs={{0,2},{2,4},{4,6},{6,7},{7,5},{5,3},{3,1},{1,0},{8,10},{10,12},{12... | collective-permute-start | bytes 589832 | tf_op jit(solution)/shard_map/ppermute | solution.py:257
  64.6 4.0 %shard_map.71.refs_9_ = f32[192,2048]{1,0:T(8,128)S(1)} custom-call(bf16[24,4096]{1,0:T(8,128)(2,1)S(1)} %get-tuple-element.36.refs_0_.refs_8_, bf16[24,4096]{1,0:T(8,128)(2,1)S(1)} %collective-permute-done.13.refs_1_.refs_9_, bf16[24,4096]{1,0:T(8,128)(2,1)S(1)} %collective-permute-done.15.refs_2_.refs_10_, ...), custom_call_target="tpu_custom_call" | custom-call | flops 4831838208 | bytes 25165824 | tf_op jit(solution)/shard_map/pallas_call | solution.py:222
  70.9 6.5 %shard_map.72.refs_9_ = f32[192,2048]{1,0:T(8,128)S(1)} custom-call(bf16[24,4096]{1,0:T(8,128)(2,1)S(1)} %get-tuple-element.43.refs_0_, bf16[24,4096]{1,0:T(8,128)(2,1)S(1)} %collective-permute-done.17.refs_1_, bf16[24,4096]{1,0:T(8,128)(2,1)S(1)} %collective-permute-done.18.refs_2_, bf16[24,4096]{1,0:T(8,128)(2,1)S(1)} %collective-permute-done.20.refs_3_, ...), custom_call_target="tpu_custom_call" | custom-call | flops 9663676416 | bytes 50331648 | tf_op jit(solution)/shard_map/pallas_call | solution.py:222
  77.4 4.1 %shard_map.73.refs_9_ = f32[192,2048]{1,0:T(8,128)S(1)} custom-call(bf16[24,4096]{1,0:T(8,128)(2,1)S(1)} %get-tuple-element.51.refs_0_.refs_8_, bf16[24,4096]{1,0:T(8,128)(2,1)S(1)} %collective-permute-done.6.refs_1_.refs_9_, bf16[24,4096]{1,0:T(8,128)(2,1)S(1)} %collective-permute-done.7.refs_2_.refs_10_, ...), custom_call_target="tpu_custom_call" | custom-call | flops 4831838208 | bytes 25165824 | tf_op jit(solution)/shard_map/pallas_call | solution.py:222
  82.1 4.1 %shard_map.74.refs_0_ = f32[192,2048]{1,0:T(8,128)S(1)} custom-call(bf16[24,4096]{1,0:T(8,128)(2,1)S(1)} %get-tuple-element.51.refs_0_.refs_8_, bf16[24,4096]{1,0:T(8,128)(2,1)S(1)} %collective-permute-done.6.refs_1_.refs_9_, bf16[24,4096]{1,0:T(8,128)(2,1)S(1)} %collective-permute-done.7.refs_2_.refs_10_, ...), custom_call_target="tpu_custom_call" | custom-call | flops 4831838208 | bytes 25165824 | tf_op jit(solution)/shard_map/pallas_call | solution.py:222
  86.2 2.3 %shard_map.77 = (f32[192,384]{1,0:T(8,128)S(1)}, f32[192,192]{1,0:T(8,128)S(1)}) custom-call(s32[4]{0:T(128)S(1)} %copy-done.1, f32[192,2048]{1,0:T(8,128)S(1)} %shard_map.74.refs_0_, bf16[8,24,1024]{2,1,0:T(8,128)(2,1)S(1)} %shard_map.75.refs_1_, bf16[8,24,1024]{2,1,0:T(8,128)(2,1)S(1)} %shard_map.76.refs_2_, ...), custom_call_target="tpu_custom_call" | custom-call | tf_op jit(solution)/shard_map/pallas_call | solution.py:183
  89.9 1.7 %collective-permute-start.39 = (f32[2,24,192]{2,1,0:T(8,128)S(1)}, f32[2,24,192]{2,1,0:T(8,128)S(1)}, u32[]{:S(2)}, u32[]{:S(2)}) collective-permute-start(f32[2,24,192]{2,1,0:T(8,128)S(1)} %get-tuple-element.65), channel_id=1, source_target_pairs={{0,2},{1,3},{2,0},{3,1},{4,6},{5,7},{6,4},{7,5},{8,10},{9,11},{10,... | collective-permute-start | bytes 110600 | tf_op jit(solution)/shard_map/ppermute | solution.py:307
  93.5 1.7 %collective-permute-start.35 = (f32[2,24,384]{2,1,0:T(8,128)S(1)}, f32[2,24,384]{2,1,0:T(8,128)S(1)}, u32[]{:S(2)}, u32[]{:S(2)}) collective-permute-start(f32[2,24,384]{2,1,0:T(8,128)S(1)} %get-tuple-element.62), channel_id=1, source_target_pairs={{0,2},{1,3},{2,0},{3,1},{4,6},{5,7},{6,4},{7,5},{8,10},{9,11},{10,... | collective-permute-start | bytes 221192 | tf_op jit(solution)/shard_map/ppermute | solution.py:307
  96.7 2.6 %collective-permute-start.41 = (f32[1,24,192]{2,1,0:T(8,128)S(1)}, f32[1,24,192]{2,1,0:T(8,128)S(1)}, u32[]{:S(2)}, u32[]{:S(2)}) collective-permute-start(f32[1,24,192]{2,1,0:T(8,128)S(1)} %constant_dynamic-slice_fusion), channel_id=1, source_target_pairs={{0,4},{1,5},{2,6},{3,7},{4,0},{5,1},{6,2},{7,3},{8,12},{9,13},{10,... | collective-permute-start | bytes 55304 | tf_op jit(solution)/shard_map/ppermute | solution.py:309
  100.4 2.1 %collective-permute-start.37 = (f32[1,24,384]{2,1,0:T(8,128)S(1)}, f32[1,24,384]{2,1,0:T(8,128)S(1)}, u32[]{:S(2)}, u32[]{:S(2)}) collective-permute-start(f32[1,24,384]{2,1,0:T(8,128)S(1)} %constant_dynamic-slice_fusion.1), channel_id=1, source_target_pairs={{0,4},{1,5},{2,6},{3,7},{4,0},{5,1},{6,2},{7,3},{8,12},{9,13},{10,... | collective-permute-start | bytes 110600 | tf_op jit(solution)/shard_map/ppermute | solution.py:309
  102.7 2.0 %collective-permute-start.43 = (f32[1,24,192]{2,1,0:T(8,128)S(1)}, f32[1,24,192]{2,1,0:T(8,128)S(1)}, u32[]{:S(2)}, u32[]{:S(2)}) collective-permute-start(f32[1,24,192]{2,1,0:T(8,128)S(1)} %dynamic-slice_add_fusion.1.refs_0_), channel_id=1, source_target_pairs={{0,16},{8,24},{16,0},{24,8},{1,17},{9,25},{17,1},{25,9},{2,18},{10... | collective-permute-start | bytes 55304 | tf_op jit(solution)/shard_map/ppermute | solution.py:313
  (84 shorter events, 19.2 us)
Async XLA Ops:
  3.2 8.7 %collective-permute-start = (bf16[24,4096]{1,0:T(8,128)(2,1)S(1)}, bf16[24,4096]{1,0:T(8,128)(2,1)S(1)}, u32[]{:S(2)}, u32[]{:S(2)}) collective-permute-start(bf16[24,4096]{1,0:T(8,128)(2,1)S(1)} %get-tuple-element.33.refs_0_), channel_id=1, source_target_pairs={{0,2},{2,4},{4,6},{6,7},{7,5},{5,3},{3,1},{1,0},{8,10},{10,12},{12... | collective-permute-start | bytes 589832 | tf_op jit(solution)/shard_map/ppermute | solution.py:253
  6.3 7.8 %collective-permute-start.15 = (bf16[24,4096]{1,0:T(8,128)(2,1)S(1)}, bf16[24,4096]{1,0:T(8,128)(2,1)S(1)}, u32[]{:S(2)}, u32[]{:S(2)}) collective-permute-start(bf16[24,4096]{1,0:T(8,128)(2,1)S(1)} %get-tuple-element.36.refs_0_.refs_8_), channel_id=1, source_target_pairs={{2,0},{4,2},{6,4},{7,6},{5,7},{3,5},{1,3},{0,1},{10,8},{12,10},{14... | collective-permute-start | bytes 589832 | tf_op jit(solution)/shard_map/ppermute | solution.py:253
  6.3 12.0 %collective-permute-start.3 = (bf16[24,4096]{1,0:T(8,128)(2,1)S(1)}, bf16[24,4096]{1,0:T(8,128)(2,1)S(1)}, u32[]{:S(2)}, u32[]{:S(2)}) collective-permute-start(bf16[24,4096]{1,0:T(8,128)(2,1)S(1)} %get-tuple-element.33.refs_0_), channel_id=1, source_target_pairs={{2,0},{4,2},{6,4},{7,6},{5,7},{3,5},{1,3},{0,1},{10,8},{12,10},{14... | collective-permute-start | bytes 589832 | tf_op jit(solution)/shard_map/ppermute | solution.py:253
  8.2 10.1 %collective-permute-start.13 = (bf16[24,4096]{1,0:T(8,128)(2,1)S(1)}, bf16[24,4096]{1,0:T(8,128)(2,1)S(1)}, u32[]{:S(2)}, u32[]{:S(2)}) collective-permute-start(bf16[24,4096]{1,0:T(8,128)(2,1)S(1)} %get-tuple-element.36.refs_0_.refs_8_), channel_id=1, source_target_pairs={{0,2},{2,4},{4,6},{6,7},{7,5},{5,3},{3,1},{1,0},{8,10},{10,12},{12... | collective-permute-start | bytes 589832 | tf_op jit(solution)/shard_map/ppermute | solution.py:253
  11.9 8.4 %collective-permute-start.1 = (bf16[24,4096]{1,0:T(8,128)(2,1)S(1)}, bf16[24,4096]{1,0:T(8,128)(2,1)S(1)}, u32[]{:S(2)}, u32[]{:S(2)}) collective-permute-start(bf16[24,4096]{1,0:T(8,128)(2,1)S(1)} %collective-permute-done.refs_1_), channel_id=1, source_target_pairs={{0,2},{2,4},{4,6},{6,7},{7,5},{5,3},{3,1},{1,0},{8,10},{10,12},{12... | collective-permute-start | bytes 589832 | tf_op jit(solution)/shard_map/ppermute | solution.py:253
  14.1 8.4 %collective-permute-start.16 = (bf16[24,4096]{1,0:T(8,128)(2,1)S(1)}, bf16[24,4096]{1,0:T(8,128)(2,1)S(1)}, u32[]{:S(2)}, u32[]{:S(2)}) collective-permute-start(bf16[24,4096]{1,0:T(8,128)(2,1)S(1)} %collective-permute-done.15.refs_2_.refs_10_), channel_id=1, source_target_pairs={{2,0},{4,2},{6,4},{7,6},{5,7},{3,5},{1,3},{0,1},{10,8},{12,10},{14... | collective-permute-start | bytes 589832 | tf_op jit(solution)/shard_map/ppermute | solution.py:253
  18.3 8.4 %collective-permute-start.4 = (bf16[24,4096]{1,0:T(8,128)(2,1)S(1)}, bf16[24,4096]{1,0:T(8,128)(2,1)S(1)}, u32[]{:S(2)}, u32[]{:S(2)}) collective-permute-start(bf16[24,4096]{1,0:T(8,128)(2,1)S(1)} %collective-permute-done.3.refs_2_), channel_id=1, source_target_pairs={{2,0},{4,2},{6,4},{7,6},{5,7},{3,5},{1,3},{0,1},{10,8},{12,10},{14... | collective-permute-start | bytes 589832 | tf_op jit(solution)/shard_map/ppermute | solution.py:253
  18.3 8.4 %collective-permute-start.14 = (bf16[24,4096]{1,0:T(8,128)(2,1)S(1)}, bf16[24,4096]{1,0:T(8,128)(2,1)S(1)}, u32[]{:S(2)}, u32[]{:S(2)}) collective-permute-start(bf16[24,4096]{1,0:T(8,128)(2,1)S(1)} %collective-permute-done.13.refs_1_.refs_9_), channel_id=1, source_target_pairs={{0,2},{2,4},{4,6},{6,7},{7,5},{5,3},{3,1},{1,0},{8,10},{10,12},{12... | collective-permute-start | bytes 589832 | tf_op jit(solution)/shard_map/ppermute | solution.py:253
  20.4 8.6 %collective-permute-start.2 = (bf16[24,4096]{1,0:T(8,128)(2,1)S(1)}, bf16[24,4096]{1,0:T(8,128)(2,1)S(1)}, u32[]{:S(2)}, u32[]{:S(2)}) collective-permute-start(bf16[24,4096]{1,0:T(8,128)(2,1)S(1)} %collective-permute-done.1.refs_3_), channel_id=1, source_target_pairs={{0,2},{2,4},{4,6},{6,7},{7,5},{5,3},{3,1},{1,0},{8,10},{10,12},{12... | collective-permute-start | bytes 589832 | tf_op jit(solution)/shard_map/ppermute | solution.py:253
  22.5 8.7 %collective-permute-start.25 = (bf16[24,4096]{1,0:T(8,128)(2,1)S(1)}, bf16[24,4096]{1,0:T(8,128)(2,1)S(1)}, u32[]{:S(2)}, u32[]{:S(2)}) collective-permute-start(bf16[24,4096]{1,0:T(8,128)(2,1)S(1)} %collective-permute-done.16.refs_4_.refs_12_), channel_id=1, source_target_pairs={{2,0},{4,2},{6,4},{7,6},{5,7},{3,5},{1,3},{0,1},{10,8},{12,10},{14... | collective-permute-start | bytes 589832 | tf_op jit(solution)/shard_map/ppermute | solution.py:253
  26.7 8.4 %collective-permute-start.5 = (bf16[24,4096]{1,0:T(8,128)(2,1)S(1)}, bf16[24,4096]{1,0:T(8,128)(2,1)S(1)}, u32[]{:S(2)}, u32[]{:S(2)}) collective-permute-start(bf16[24,4096]{1,0:T(8,128)(2,1)S(1)} %collective-permute-done.4.refs_4_), channel_id=1, source_target_pairs={{2,0},{4,2},{6,4},{7,6},{5,7},{3,5},{1,3},{0,1},{10,8},{12,10},{14... | collective-permute-start | bytes 589832 | tf_op jit(solution)/shard_map/ppermute | solution.py:253
  26.8 10.0 %collective-permute-start.24 = (bf16[24,4096]{1,0:T(8,128)(2,1)S(1)}, bf16[24,4096]{1,0:T(8,128)(2,1)S(1)}, u32[]{:S(2)}, u32[]{:S(2)}) collective-permute-start(bf16[24,4096]{1,0:T(8,128)(2,1)S(1)} %collective-permute-done.14.refs_3_.refs_11_), channel_id=1, source_target_pairs={{0,2},{2,4},{4,6},{6,7},{7,5},{5,3},{3,1},{1,0},{8,10},{10,12},{12... | collective-permute-start | bytes 589832 | tf_op jit(solution)/shard_map/ppermute | solution.py:253
  29.0 8.7 %collective-permute-start.19 = (bf16[24,4096]{1,0:T(8,128)(2,1)S(1)}, bf16[24,4096]{1,0:T(8,128)(2,1)S(1)}, u32[]{:S(2)}, u32[]{:S(2)}) collective-permute-start(bf16[24,4096]{1,0:T(8,128)(2,1)S(1)} %collective-permute-done.2.refs_5_), channel_id=1, source_target_pairs={{0,2},{2,4},{4,6},{6,7},{7,5},{5,3},{3,1},{1,0},{8,10},{10,12},{12... | collective-permute-start | bytes 589832 | tf_op jit(solution)/shard_map/ppermute | solution.py:257
  31.2 8.6 %collective-permute-start.26 = (bf16[24,4096]{1,0:T(8,128)(2,1)S(1)}, bf16[24,4096]{1,0:T(8,128)(2,1)S(1)}, u32[]{:S(2)}, u32[]{:S(2)}) collective-permute-start(bf16[24,4096]{1,0:T(8,128)(2,1)S(1)} %collective-permute-done.25.refs_6_.refs_14_), channel_id=1, source_target_pairs={{2,0},{4,2},{6,4},{7,6},{5,7},{3,5},{1,3},{0,1},{10,8},{12,10},{14... | collective-permute-start | bytes 589832 | tf_op jit(solution)/shard_map/ppermute | solution.py:258
  31.2 14.3 %collective-permute-start.18 = (bf16[24,4096]{1,0:T(8,128)(2,1)S(1)}, bf16[24,4096]{1,0:T(8,128)(2,1)S(1)}, u32[]{:S(2)}, u32[]{:S(2)}) collective-permute-start(bf16[24,4096]{1,0:T(8,128)(2,1)S(1)} %get-tuple-element.43.refs_0_), channel_id=1, source_target_pairs={{2,0},{4,2},{6,4},{7,6},{5,7},{3,5},{1,3},{0,1},{10,8},{12,10},{14... | collective-permute-start | bytes 589832 | tf_op jit(solution)/shard_map/ppermute | solution.py:253
  35.2 10.3 %collective-permute-start.17 = (bf16[24,4096]{1,0:T(8,128)(2,1)S(1)}, bf16[24,4096]{1,0:T(8,128)(2,1)S(1)}, u32[]{:S(2)}, u32[]{:S(2)}) collective-permute-start(bf16[24,4096]{1,0:T(8,128)(2,1)S(1)} %get-tuple-element.43.refs_0_), channel_id=1, source_target_pairs={{0,2},{2,4},{4,6},{6,7},{7,5},{5,3},{3,1},{1,0},{8,10},{10,12},{12... | collective-permute-start | bytes 589832 | tf_op jit(solution)/shard_map/ppermute | solution.py:253
  36.8 10.8 %collective-permute-start.7 = (bf16[24,4096]{1,0:T(8,128)(2,1)S(1)}, bf16[24,4096]{1,0:T(8,128)(2,1)S(1)}, u32[]{:S(2)}, u32[]{:S(2)}) collective-permute-start(bf16[24,4096]{1,0:T(8,128)(2,1)S(1)} %get-tuple-element.51.refs_0_.refs_8_), channel_id=1, source_target_pairs={{2,0},{4,2},{6,4},{7,6},{5,7},{3,5},{1,3},{0,1},{10,8},{12,10},{14... | collective-permute-start | bytes 589832 | tf_op jit(solution)/shard_map/ppermute | solution.py:253
  37.7 14.9 %collective-permute-start.6 = (bf16[24,4096]{1,0:T(8,128)(2,1)S(1)}, bf16[24,4096]{1,0:T(8,128)(2,1)S(1)}, u32[]{:S(2)}, u32[]{:S(2)}) collective-permute-start(bf16[24,4096]{1,0:T(8,128)(2,1)S(1)} %get-tuple-element.51.refs_0_.refs_8_), channel_id=1, source_target_pairs={{0,2},{2,4},{4,6},{6,7},{7,5},{5,3},{3,1},{1,0},{8,10},{10,12},{12... | collective-permute-start | bytes 589832 | tf_op jit(solution)/shard_map/ppermute | solution.py:253
  39.8 28.9 %collective-permute-start.29 = (bf16[8,24,1024]{2,1,0:T(8,128)(2,1)S(1)}, bf16[8,24,1024]{2,1,0:T(8,128)(2,1)S(1)}, u32[]{:S(2)}, u32[]{:S(2)}) collective-permute-start(bf16[8,24,1024]{2,1,0:T(8,128)(2,1)S(1)} %shard_map.75.refs_1_), channel_id=1, source_target_pairs={{0,16},{8,24},{16,0},{24,8},{1,17},{9,25},{17,1},{25,9},{2,18},{10... | collective-permute-start | bytes 1179656 | tf_op jit(solution)/shard_map/ppermute | solution.py:233
  45.5 8.2 %collective-permute-start.20 = (bf16[24,4096]{1,0:T(8,128)(2,1)S(1)}, bf16[24,4096]{1,0:T(8,128)(2,1)S(1)}, u32[]{:S(2)}, u32[]{:S(2)}) collective-permute-start(bf16[24,4096]{1,0:T(8,128)(2,1)S(1)} %collective-permute-done.17.refs_1_), channel_id=1, source_target_pairs={{0,2},{2,4},{4,6},{6,7},{7,5},{5,3},{3,1},{1,0},{8,10},{10,12},{12... | collective-permute-start | bytes 589832 | tf_op jit(solution)/shard_map/ppermute | solution.py:253
  47.1 12.7 %collective-permute-start.21 = (bf16[24,4096]{1,0:T(8,128)(2,1)S(1)}, bf16[24,4096]{1,0:T(8,128)(2,1)S(1)}, u32[]{:S(2)}, u32[]{:S(2)}) collective-permute-start(bf16[24,4096]{1,0:T(8,128)(2,1)S(1)} %collective-permute-done.18.refs_2_), channel_id=1, source_target_pairs={{2,0},{4,2},{6,4},{7,6},{5,7},{3,5},{1,3},{0,1},{10,8},{12,10},{14... | collective-permute-start | bytes 589832 | tf_op jit(solution)/shard_map/ppermute | solution.py:253
  47.6 7.8 %collective-permute-start.9 = (bf16[24,4096]{1,0:T(8,128)(2,1)S(1)}, bf16[24,4096]{1,0:T(8,128)(2,1)S(1)}, u32[]{:S(2)}, u32[]{:S(2)}) collective-permute-start(bf16[24,4096]{1,0:T(8,128)(2,1)S(1)} %collective-permute-done.7.refs_2_.refs_10_), channel_id=1, source_target_pairs={{2,0},{4,2},{6,4},{7,6},{5,7},{3,5},{1,3},{0,1},{10,8},{12,10},{14... | collective-permute-start | bytes 589832 | tf_op jit(solution)/shard_map/ppermute | solution.py:253
  52.7 9.3 %collective-permute-start.8 = (bf16[24,4096]{1,0:T(8,128)(2,1)S(1)}, bf16[24,4096]{1,0:T(8,128)(2,1)S(1)}, u32[]{:S(2)}, u32[]{:S(2)}) collective-permute-start(bf16[24,4096]{1,0:T(8,128)(2,1)S(1)} %collective-permute-done.6.refs_1_.refs_9_), channel_id=1, source_target_pairs={{0,2},{2,4},{4,6},{6,7},{7,5},{5,3},{3,1},{1,0},{8,10},{10,12},{12... | collective-permute-start | bytes 589832 | tf_op jit(solution)/shard_map/ppermute | solution.py:253
  53.8 8.3 %collective-permute-start.22 = (bf16[24,4096]{1,0:T(8,128)(2,1)S(1)}, bf16[24,4096]{1,0:T(8,128)(2,1)S(1)}, u32[]{:S(2)}, u32[]{:S(2)}) collective-permute-start(bf16[24,4096]{1,0:T(8,128)(2,1)S(1)} %collective-permute-done.20.refs_3_), channel_id=1, source_target_pairs={{0,2},{2,4},{4,6},{6,7},{7,5},{5,3},{3,1},{1,0},{8,10},{10,12},{12... | collective-permute-start | bytes 589832 | tf_op jit(solution)/shard_map/ppermute | solution.py:253
  55.4 9.2 %collective-permute-start.11 = (bf16[24,4096]{1,0:T(8,128)(2,1)S(1)}, bf16[24,4096]{1,0:T(8,128)(2,1)S(1)}, u32[]{:S(2)}, u32[]{:S(2)}) collective-permute-start(bf16[24,4096]{1,0:T(8,128)(2,1)S(1)} %collective-permute-done.9.refs_4_.refs_12_), channel_id=1, source_target_pairs={{2,0},{4,2},{6,4},{7,6},{5,7},{3,5},{1,3},{0,1},{10,8},{12,10},{14... | collective-permute-start | bytes 589832 | tf_op jit(solution)/shard_map/ppermute | solution.py:253
  59.9 8.9 %collective-permute-start.23 = (bf16[24,4096]{1,0:T(8,128)(2,1)S(1)}, bf16[24,4096]{1,0:T(8,128)(2,1)S(1)}, u32[]{:S(2)}, u32[]{:S(2)}) collective-permute-start(bf16[24,4096]{1,0:T(8,128)(2,1)S(1)} %collective-permute-done.21.refs_4_), channel_id=1, source_target_pairs={{2,0},{4,2},{6,4},{7,6},{5,7},{3,5},{1,3},{0,1},{10,8},{12,10},{14... | collective-permute-start | bytes 589832 | tf_op jit(solution)/shard_map/ppermute | solution.py:253
  62.1 8.2 %collective-permute-start.27 = (bf16[24,4096]{1,0:T(8,128)(2,1)S(1)}, bf16[24,4096]{1,0:T(8,128)(2,1)S(1)}, u32[]{:S(2)}, u32[]{:S(2)}) collective-permute-start(bf16[24,4096]{1,0:T(8,128)(2,1)S(1)} %collective-permute-done.22.refs_5_), channel_id=1, source_target_pairs={{0,2},{2,4},{4,6},{6,7},{7,5},{5,3},{3,1},{1,0},{8,10},{10,12},{12... | collective-permute-start | bytes 589832 | tf_op jit(solution)/shard_map/ppermute | solution.py:257
  68.7 17.5 %collective-permute-start.28 = (bf16[8,24,1024]{2,1,0:T(8,128)(2,1)S(1)}, bf16[8,24,1024]{2,1,0:T(8,128)(2,1)S(1)}, u32[]{:S(2)}, u32[]{:S(2)}) collective-permute-start(bf16[8,24,1024]{2,1,0:T(8,128)(2,1)S(1)} %shard_map.75.refs_1_), channel_id=1, source_target_pairs={{0,8},{8,0},{16,24},{24,16},{1,9},{9,1},{17,25},{25,17},{2,10},{10... | collective-permute-start | bytes 1179656 | tf_op jit(solution)/shard_map/ppermute | solution.py:234
  68.8 17.4 %collective-permute-start.30 = (bf16[8,24,1024]{2,1,0:T(8,128)(2,1)S(1)}, bf16[8,24,1024]{2,1,0:T(8,128)(2,1)S(1)}, u32[]{:S(2)}, u32[]{:S(2)}) collective-permute-start(bf16[8,24,1024]{2,1,0:T(8,128)(2,1)S(1)} %collective-permute-done.29.refs_4_), channel_id=1, source_target_pairs={{0,8},{8,0},{16,24},{24,16},{1,9},{9,1},{17,25},{25,17},{2,10},{10... | collective-permute-start | bytes 1179656 | tf_op jit(solution)/shard_map/ppermute | solution.py:239
  70.3 11.2 %collective-permute-start.32 = (bf16[8,24,1024]{2,1,0:T(8,128)(2,1)S(1)}, bf16[8,24,1024]{2,1,0:T(8,128)(2,1)S(1)}, u32[]{:S(2)}, u32[]{:S(2)}) collective-permute-start(bf16[8,24,1024]{2,1,0:T(8,128)(2,1)S(1)} %shard_map.76.refs_2_), channel_id=1, source_target_pairs={{0,16},{8,24},{16,0},{24,8},{1,17},{9,25},{17,1},{25,9},{2,18},{10... | collective-permute-start | bytes 1179656 | tf_op jit(solution)/shard_map/ppermute | solution.py:233
  70.9 15.2 %collective-permute-start.31 = (bf16[8,24,1024]{2,1,0:T(8,128)(2,1)S(1)}, bf16[8,24,1024]{2,1,0:T(8,128)(2,1)S(1)}, u32[]{:S(2)}, u32[]{:S(2)}) collective-permute-start(bf16[8,24,1024]{2,1,0:T(8,128)(2,1)S(1)} %shard_map.76.refs_2_), channel_id=1, source_target_pairs={{0,8},{8,0},{16,24},{24,16},{1,9},{9,1},{17,25},{25,17},{2,10},{10... | collective-permute-start | bytes 1179656 | tf_op jit(solution)/shard_map/ppermute | solution.py:234
  92.1 7.2 %collective-permute-start.34 = (f32[2,24,384]{2,1,0:T(8,128)S(1)}, f32[2,24,384]{2,1,0:T(8,128)S(1)}, u32[]{:S(2)}, u32[]{:S(2)}) collective-permute-start(f32[2,24,384]{2,1,0:T(8,128)S(1)} %get-tuple-element.61), channel_id=1, source_target_pairs={{0,1},{1,0},{2,3},{3,2},{4,5},{5,4},{6,7},{7,6},{8,9},{9,8},{10,11... | collective-permute-start | bytes 221192 | tf_op jit(solution)/shard_map/ppermute | solution.py:307
  (16 other events, 72.4 us)

commit v5 on v4

--- a/solution.py
+++ b/solution.py
@@ -292,7 +292,7 @@
     cross, pair = contractions(partner, total, [first_own, last_own], other, n)
 
     size = n * rows
-    sums = [block.reshape(n, rows, block.shape[1]) for block in (pair, cross)]
+    sums = [jnp.concatenate([pair, cross], axis=1).reshape(n, rows, 3 * size)]
     bit = 1
     while bit < n:
         radix = 4 if bit < n // 2 else 2
@@ -304,11 +304,13 @@
                 given = lax.dynamic_index_in_dim(split, mine ^ flip, 1, keepdims=False)
                 ways = [(i, i ^ flip * bit) for i in range(n)]
                 if bit == 1:
-                    block += lax.ppermute(given, "wide", ways)
+                    block += lax.ppermute(given.astype(jnp.bfloat16), "wide", ways).astype(jnp.float32)
                 else:
                     block += lax.ppermute(given, "wide", ways)
             sums[at] = block
         bit *= radix
+        if len(sums) == 1 and (1 or bit >= n):
+            sums = [sums[0][..., :size], sums[0][..., size:]]
     spread_rows = [
         lax.ppermute(sums[0], "grp", [(i, i ^ flip) for i in range(4)]) for flip in (1, 2, 3)
     ]

time: 108 us -> 108 us (level)
  starting transfers between devices: 49.9 us -> 44.4 us
  waiting for transfers between devices: 20 us -> 25.2 us
    ppermute x8 -> x2, starting transfers between devices: 11.8 us -> 2.99 us  [shards(): block += lax.ppermute(given, 'wide', ways)]
    ppermute x0 -> x3, waiting for transfers between devices: none -> 4.63 us  [shards(): lax.ppermute(given.astype(jnp.bfloat16), 'wide', ways).astype(jnp.float32)]
    ppermute x0 -> x3, starting transfers between devices: none -> 3.55 us  [shards(): lax.ppermute(given.astype(jnp.bfloat16), 'wide', ways).astype(jnp.float32)]
    ppermute x8 -> x2, waiting for transfers between devices: 3.03 us -> 2.59 us  [shards(): block += lax.ppermute(given, 'wide', ways)]
  transfers between devices with their start and end apart: 45 -> 42, of which waited for: 12 -> 13; matrix products, arithmetic and copies ran while one was open for 0% -> 0% of each run, Pallas kernels for 29% -> 29%
where the time goes in v5:
time: 108 us
  starting transfers between devices  44.4 us (41%)
  Pallas kernels  35.2 us (33%)
  waiting for transfers between devices  25.2 us (23%)
  local copies, waits for them, and re-layouts  1.92 us (2%)
    pallas_call x7, Pallas kernels, multiply(): call(kernel, total, specs, scratch, flops, moved)(*pieces, mat, before)  30.8 us
    ppermute x12, starting transfers between devices, both_ways(): lax.ppermute(up, 'wide', forth)  19.6 us
    ppermute x12, waiting for transfers between devices, both_ways(): lax.ppermute(down, 'wide', back)  10.5 us
    ppermute x12, starting transfers between devices, both_ways(): lax.ppermute(down, 'wide', back)  8.29 us
    ppermute x2, starting transfers between devices, last_hops(): one = lax.ppermute(lanes[0][0], 'wide', forth)  4.77 us
    ppermute x3, waiting for transfers between devices, shards(): lax.ppermute(given.astype(jnp.bfloat16), 'wide', ways).astype(jnp.float32)  4.63 us
    ppermute x12, waiting for transfers between devices, both_ways(): lax.ppermute(up, 'wide', forth)  3.82 us
    ppermute x3, starting transfers between devices, shards(): lax.ppermute(given.astype(jnp.bfloat16), 'wide', ways).astype(jnp.float32)  3.55 us
  transfers between devices with their start and end apart: 42, of which 13 were waited for; matrix products, arithmetic and copies ran while one was open for 0% of the time, Pallas kernels for 29%

profile of v5, /device:TPU:0, one launch (start us, length us, event | category | flops | bytes accessed | tf_op | source)
XLA Modules:
  0.0 107.8 jit_solution(18051438407422444657)
XLA Ops:
  3.2 3.1 %collective-permute-start = (bf16[24,4096]{1,0:T(8,128)(2,1)S(1)}, bf16[24,4096]{1,0:T(8,128)(2,1)S(1)}, u32[]{:S(2)}, u32[]{:S(2)}) collective-permute-start(bf16[24,4096]{1,0:T(8,128)(2,1)S(1)} %get-tuple-element.33.refs_0_), channel_id=1, source_target_pairs={{0,2},{2,4},{4,6},{6,7},{7,5},{5,3},{3,1},{1,0},{8,10},{10,12},{12... | collective-permute-start | bytes 589832 | tf_op jit(solution)/shard_map/ppermute | solution.py:253
  6.3 1.9 %collective-permute-start.3 = (bf16[24,4096]{1,0:T(8,128)(2,1)S(1)}, bf16[24,4096]{1,0:T(8,128)(2,1)S(1)}, u32[]{:S(2)}, u32[]{:S(2)}) collective-permute-start(bf16[24,4096]{1,0:T(8,128)(2,1)S(1)} %get-tuple-element.33.refs_0_), channel_id=1, source_target_pairs={{2,0},{4,2},{6,4},{7,6},{5,7},{3,5},{1,3},{0,1},{10,8},{12,10},{14... | collective-permute-start | bytes 589832 | tf_op jit(solution)/shard_map/ppermute | solution.py:253
  8.3 3.6 %collective-permute-done.refs_1_ = bf16[24,4096]{1,0:T(8,128)(2,1)S(1)} collective-permute-done((bf16[24,4096]{1,0:T(8,128)(2,1)S(1)}, bf16[24,4096]{1,0:T(8,128)(2,1)S(1)}, u32[]{:S(2)}, u32[]{:S(2)}) %collective-permute-start) | collective-permute-done | bytes 196640 | tf_op jit(solution)/shard_map/ppermute | solution.py:253
  11.9 2.1 %collective-permute-start.1 = (bf16[24,4096]{1,0:T(8,128)(2,1)S(1)}, bf16[24,4096]{1,0:T(8,128)(2,1)S(1)}, u32[]{:S(2)}, u32[]{:S(2)}) collective-permute-start(bf16[24,4096]{1,0:T(8,128)(2,1)S(1)} %collective-permute-done.refs_1_), channel_id=1, source_target_pairs={{0,2},{2,4},{4,6},{6,7},{7,5},{5,3},{3,1},{1,0},{8,10},{10,12},{12... | collective-permute-start | bytes 589832 | tf_op jit(solution)/shard_map/ppermute | solution.py:253
  14.1 4.2 %collective-permute-done.3.refs_2_ = bf16[24,4096]{1,0:T(8,128)(2,1)S(1)} collective-permute-done((bf16[24,4096]{1,0:T(8,128)(2,1)S(1)}, bf16[24,4096]{1,0:T(8,128)(2,1)S(1)}, u32[]{:S(2)}, u32[]{:S(2)}) %collective-permute-start.3) | collective-permute-done | bytes 196640 | tf_op jit(solution)/shard_map/ppermute | solution.py:253
  18.3 2.0 %collective-permute-start.14 = (bf16[24,4096]{1,0:T(8,128)(2,1)S(1)}, bf16[24,4096]{1,0:T(8,128)(2,1)S(1)}, u32[]{:S(2)}, u32[]{:S(2)}) collective-permute-start(bf16[24,4096]{1,0:T(8,128)(2,1)S(1)} %collective-permute-done.13.refs_1_.refs_9_), channel_id=1, source_target_pairs={{0,2},{2,4},{4,6},{6,7},{7,5},{5,3},{3,1},{1,0},{8,10},{10,12},{12... | collective-permute-start | bytes 589832 | tf_op jit(solution)/shard_map/ppermute | solution.py:253
  20.4 2.1 %collective-permute-start.2 = (bf16[24,4096]{1,0:T(8,128)(2,1)S(1)}, bf16[24,4096]{1,0:T(8,128)(2,1)S(1)}, u32[]{:S(2)}, u32[]{:S(2)}) collective-permute-start(bf16[24,4096]{1,0:T(8,128)(2,1)S(1)} %collective-permute-done.1.refs_3_), channel_id=1, source_target_pairs={{0,2},{2,4},{4,6},{6,7},{7,5},{5,3},{3,1},{1,0},{8,10},{10,12},{12... | collective-permute-start | bytes 589832 | tf_op jit(solution)/shard_map/ppermute | solution.py:253
  22.5 4.2 %collective-permute-done.4.refs_4_ = bf16[24,4096]{1,0:T(8,128)(2,1)S(1)} collective-permute-done((bf16[24,4096]{1,0:T(8,128)(2,1)S(1)}, bf16[24,4096]{1,0:T(8,128)(2,1)S(1)}, u32[]{:S(2)}, u32[]{:S(2)}) %collective-permute-start.4) | collective-permute-done | bytes 196640 | tf_op jit(solution)/shard_map/ppermute | solution.py:253
  26.8 2.0 %collective-permute-start.24 = (bf16[24,4096]{1,0:T(8,128)(2,1)S(1)}, bf16[24,4096]{1,0:T(8,128)(2,1)S(1)}, u32[]{:S(2)}, u32[]{:S(2)}) collective-permute-start(bf16[24,4096]{1,0:T(8,128)(2,1)S(1)} %collective-permute-done.14.refs_3_.refs_11_), channel_id=1, source_target_pairs={{0,2},{2,4},{4,6},{6,7},{7,5},{5,3},{3,1},{1,0},{8,10},{10,12},{12... | collective-permute-start | bytes 589832 | tf_op jit(solution)/shard_map/ppermute | solution.py:253
  29.0 2.2 %collective-permute-start.19 = (bf16[24,4096]{1,0:T(8,128)(2,1)S(1)}, bf16[24,4096]{1,0:T(8,128)(2,1)S(1)}, u32[]{:S(2)}, u32[]{:S(2)}) collective-permute-start(bf16[24,4096]{1,0:T(8,128)(2,1)S(1)} %collective-permute-done.2.refs_5_), channel_id=1, source_target_pairs={{0,2},{2,4},{4,6},{6,7},{7,5},{5,3},{3,1},{1,0},{8,10},{10,12},{12... | collective-permute-start | bytes 589832 | tf_op jit(solution)/shard_map/ppermute | solution.py:257
  31.2 1.9 %collective-permute-start.18 = (bf16[24,4096]{1,0:T(8,128)(2,1)S(1)}, bf16[24,4096]{1,0:T(8,128)(2,1)S(1)}, u32[]{:S(2)}, u32[]{:S(2)}) collective-permute-start(bf16[24,4096]{1,0:T(8,128)(2,1)S(1)} %get-tuple-element.43.refs_0_), channel_id=1, source_target_pairs={{2,0},{4,2},{6,4},{7,6},{5,7},{3,5},{1,3},{0,1},{10,8},{12,10},{14... | collective-permute-start | bytes 589832 | tf_op jit(solution)/shard_map/ppermute | solution.py:253
  33.2 2.0 %collective-permute-done.5.refs_6_ = bf16[24,4096]{1,0:T(8,128)(2,1)S(1)} collective-permute-done((bf16[24,4096]{1,0:T(8,128)(2,1)S(1)}, bf16[24,4096]{1,0:T(8,128)(2,1)S(1)}, u32[]{:S(2)}, u32[]{:S(2)}) %collective-permute-start.5) | collective-permute-done | bytes 196640 | tf_op jit(solution)/shard_map/ppermute | solution.py:253
  35.2 1.6 %collective-permute-start.17 = (bf16[24,4096]{1,0:T(8,128)(2,1)S(1)}, bf16[24,4096]{1,0:T(8,128)(2,1)S(1)}, u32[]{:S(2)}, u32[]{:S(2)}) collective-permute-start(bf16[24,4096]{1,0:T(8,128)(2,1)S(1)} %get-tuple-element.43.refs_0_), channel_id=1, source_target_pairs={{0,2},{2,4},{4,6},{6,7},{7,5},{5,3},{3,1},{1,0},{8,10},{10,12},{12... | collective-permute-start | bytes 589832 | tf_op jit(solution)/shard_map/ppermute | solution.py:253
  37.7 2.1 %collective-permute-start.6 = (bf16[24,4096]{1,0:T(8,128)(2,1)S(1)}, bf16[24,4096]{1,0:T(8,128)(2,1)S(1)}, u32[]{:S(2)}, u32[]{:S(2)}) collective-permute-start(bf16[24,4096]{1,0:T(8,128)(2,1)S(1)} %get-tuple-element.51.refs_0_.refs_8_), channel_id=1, source_target_pairs={{0,2},{2,4},{4,6},{6,7},{7,5},{5,3},{3,1},{1,0},{8,10},{10,12},{12... | collective-permute-start | bytes 589832 | tf_op jit(solution)/shard_map/ppermute | solution.py:253
  39.8 1.6 %collective-permute-start.29 = (bf16[8,24,1024]{2,1,0:T(8,128)(2,1)S(1)}, bf16[8,24,1024]{2,1,0:T(8,128)(2,1)S(1)}, u32[]{:S(2)}, u32[]{:S(2)}) collective-permute-start(bf16[8,24,1024]{2,1,0:T(8,128)(2,1)S(1)} %shard_map.75.refs_1_), channel_id=1, source_target_pairs={{0,16},{8,24},{16,0},{24,8},{1,17},{9,25},{17,1},{25,9},{2,18},{10... | collective-permute-start | bytes 1179656 | tf_op jit(solution)/shard_map/ppermute | solution.py:233
  41.4 4.1 %shard_map.68.refs_9_ = f32[192,2048]{1,0:T(8,128)S(1)} custom-call(bf16[24,4096]{1,0:T(8,128)(2,1)S(1)} %get-tuple-element.33.refs_0_, bf16[24,4096]{1,0:T(8,128)(2,1)S(1)} %collective-permute-done.refs_1_, bf16[24,4096]{1,0:T(8,128)(2,1)S(1)} %collective-permute-done.3.refs_2_, bf16[24,4096]{1,0:T(8,128)(2,1)S(1)} %collective-permute-done.1.refs_3_, ...), custom_call_target="tpu_custom_call" | custom-call | flops 4831838208 | bytes 25165824 | tf_op jit(solution)/shard_map/pallas_call | solution.py:222
  45.5 1.6 %collective-permute-start.20 = (bf16[24,4096]{1,0:T(8,128)(2,1)S(1)}, bf16[24,4096]{1,0:T(8,128)(2,1)S(1)}, u32[]{:S(2)}, u32[]{:S(2)}) collective-permute-start(bf16[24,4096]{1,0:T(8,128)(2,1)S(1)} %collective-permute-done.17.refs_1_), channel_id=1, source_target_pairs={{0,2},{2,4},{4,6},{6,7},{7,5},{5,3},{3,1},{1,0},{8,10},{10,12},{12... | collective-permute-start | bytes 589832 | tf_op jit(solution)/shard_map/ppermute | solution.py:253
  48.6 4.0 %shard_map.69.refs_9_ = f32[192,2048]{1,0:T(8,128)S(1)} custom-call(bf16[24,4096]{1,0:T(8,128)(2,1)S(1)} %get-tuple-element.33.refs_0_, bf16[24,4096]{1,0:T(8,128)(2,1)S(1)} %collective-permute-done.refs_1_, bf16[24,4096]{1,0:T(8,128)(2,1)S(1)} %collective-permute-done.3.refs_2_, bf16[24,4096]{1,0:T(8,128)(2,1)S(1)} %collective-permute-done.1.refs_3_, ...), custom_call_target="tpu_custom_call" | custom-call | flops 4831838208 | bytes 25165824 | tf_op jit(solution)/shard_map/pallas_call | solution.py:222
  53.8 1.6 %collective-permute-start.22 = (bf16[24,4096]{1,0:T(8,128)(2,1)S(1)}, bf16[24,4096]{1,0:T(8,128)(2,1)S(1)}, u32[]{:S(2)}, u32[]{:S(2)}) collective-permute-start(bf16[24,4096]{1,0:T(8,128)(2,1)S(1)} %collective-permute-done.20.refs_3_), channel_id=1, source_target_pairs={{0,2},{2,4},{4,6},{6,7},{7,5},{5,3},{3,1},{1,0},{8,10},{10,12},{12... | collective-permute-start | bytes 589832 | tf_op jit(solution)/shard_map/ppermute | solution.py:253
  55.8 4.1 %shard_map.70.refs_9_ = f32[192,2048]{1,0:T(8,128)S(1)} custom-call(bf16[24,4096]{1,0:T(8,128)(2,1)S(1)} %get-tuple-element.36.refs_0_.refs_8_, bf16[24,4096]{1,0:T(8,128)(2,1)S(1)} %collective-permute-done.13.refs_1_.refs_9_, bf16[24,4096]{1,0:T(8,128)(2,1)S(1)} %collective-permute-done.15.refs_2_.refs_10_, ...), custom_call_target="tpu_custom_call" | custom-call | flops 4831838208 | bytes 25165824 | tf_op jit(solution)/shard_map/pallas_call | solution.py:222
  59.9 2.1 %collective-permute-start.23 = (bf16[24,4096]{1,0:T(8,128)(2,1)S(1)}, bf16[24,4096]{1,0:T(8,128)(2,1)S(1)}, u32[]{:S(2)}, u32[]{:S(2)}) collective-permute-start(bf16[24,4096]{1,0:T(8,128)(2,1)S(1)} %collective-permute-done.21.refs_4_), channel_id=1, source_target_pairs={{2,0},{4,2},{6,4},{7,6},{5,7},{3,5},{1,3},{0,1},{10,8},{12,10},{14... | collective-permute-start | bytes 589832 | tf_op jit(solution)/shard_map/ppermute | solution.py:253
  62.1 2.5 %collective-permute-start.27 = (bf16[24,4096]{1,0:T(8,128)(2,1)S(1)}, bf16[24,4096]{1,0:T(8,128)(2,1)S(1)}, u32[]{:S(2)}, u32[]{:S(2)}) collective-permute-start(bf16[24,4096]{1,0:T(8,128)(2,1)S(1)} %collective-permute-done.22.refs_5_), channel_id=1, source_target_pairs={{0,2},{2,4},{4,6},{6,7},{7,5},{5,3},{3,1},{1,0},{8,10},{10,12},{12... | collective-permute-start | bytes 589832 | tf_op jit(solution)/shard_map/ppermute | solution.py:257
  64.6 4.0 %shard_map.71.refs_9_ = f32[192,2048]{1,0:T(8,128)S(1)} custom-call(bf16[24,4096]{1,0:T(8,128)(2,1)S(1)} %get-tuple-element.36.refs_0_.refs_8_, bf16[24,4096]{1,0:T(8,128)(2,1)S(1)} %collective-permute-done.13.refs_1_.refs_9_, bf16[24,4096]{1,0:T(8,128)(2,1)S(1)} %collective-permute-done.15.refs_2_.refs_10_, ...), custom_call_target="tpu_custom_call" | custom-call | flops 4831838208 | bytes 25165824 | tf_op jit(solution)/shard_map/pallas_call | solution.py:222
  70.9 6.5 %shard_map.72.refs_9_ = f32[192,2048]{1,0:T(8,128)S(1)} custom-call(bf16[24,4096]{1,0:T(8,128)(2,1)S(1)} %get-tuple-element.43.refs_0_, bf16[24,4096]{1,0:T(8,128)(2,1)S(1)} %collective-permute-done.17.refs_1_, bf16[24,4096]{1,0:T(8,128)(2,1)S(1)} %collective-permute-done.18.refs_2_, bf16[24,4096]{1,0:T(8,128)(2,1)S(1)} %collective-permute-done.20.refs_3_, ...), custom_call_target="tpu_custom_call" | custom-call | flops 9663676416 | bytes 50331648 | tf_op jit(solution)/shard_map/pallas_call | solution.py:222
  77.4 4.1 %shard_map.73.refs_9_ = f32[192,2048]{1,0:T(8,128)S(1)} custom-call(bf16[24,4096]{1,0:T(8,128)(2,1)S(1)} %get-tuple-element.51.refs_0_.refs_8_, bf16[24,4096]{1,0:T(8,128)(2,1)S(1)} %collective-permute-done.6.refs_1_.refs_9_, bf16[24,4096]{1,0:T(8,128)(2,1)S(1)} %collective-permute-done.7.refs_2_.refs_10_, ...), custom_call_target="tpu_custom_call" | custom-call | flops 4831838208 | bytes 25165824 | tf_op jit(solution)/shard_map/pallas_call | solution.py:222
  82.1 4.1 %shard_map.74.refs_0_ = f32[192,2048]{1,0:T(8,128)S(1)} custom-call(bf16[24,4096]{1,0:T(8,128)(2,1)S(1)} %get-tuple-element.51.refs_0_.refs_8_, bf16[24,4096]{1,0:T(8,128)(2,1)S(1)} %collective-permute-done.6.refs_1_.refs_9_, bf16[24,4096]{1,0:T(8,128)(2,1)S(1)} %collective-permute-done.7.refs_2_.refs_10_, ...), custom_call_target="tpu_custom_call" | custom-call | flops 4831838208 | bytes 25165824 | tf_op jit(solution)/shard_map/pallas_call | solution.py:222
  86.2 2.3 %shard_map.77 = (f32[192,384]{1,0:T(8,128)S(1)}, f32[192,192]{1,0:T(8,128)S(1)}) custom-call(s32[4]{0:T(128)S(1)} %copy-done.1, f32[192,2048]{1,0:T(8,128)S(1)} %shard_map.74.refs_0_, bf16[8,24,1024]{2,1,0:T(8,128)(2,1)S(1)} %shard_map.75.refs_1_, bf16[8,24,1024]{2,1,0:T(8,128)(2,1)S(1)} %shard_map.76.refs_2_, ...), custom_call_target="tpu_custom_call" | custom-call | tf_op jit(solution)/shard_map/pallas_call | solution.py:183
  90.1 1.7 %collective-permute-start.35 = (bf16[2,24,576]{2,1,0:T(8,128)(2,1)S(1)}, bf16[2,24,576]{2,1,0:T(8,128)(2,1)S(1)}, u32[]{:S(2)}, u32[]{:S(2)}) collective-permute-start(bf16[2,24,576]{2,1,0:T(8,128)(2,1)S(1)} %get-tuple-element.62), channel_id=1, source_target_pairs={{0,2},{1,3},{2,0},{3,1},{4,6},{5,7},{6,4},{7,5},{8,10},{9,11},{10,... | collective-permute-start | bytes 165896 | tf_op jit(solution)/shard_map/ppermute | solution.py:307
  93.0 1.6 %collective-permute-done.35 = bf16[2,24,576]{2,1,0:T(8,128)(2,1)S(1)} collective-permute-done((bf16[2,24,576]{2,1,0:T(8,128)(2,1)S(1)}, bf16[2,24,576]{2,1,0:T(8,128)(2,1)S(1)}, u32[]{:S(2)}, u32[]{:S(2)}) %collective-permute-start.35) | collective-permute-done | bytes 55328 | tf_op jit(solution)/shard_map/ppermute | solution.py:307
  94.6 2.3 %collective-permute-done.36 = bf16[2,24,576]{2,1,0:T(8,128)(2,1)S(1)} collective-permute-done((bf16[2,24,576]{2,1,0:T(8,128)(2,1)S(1)}, bf16[2,24,576]{2,1,0:T(8,128)(2,1)S(1)}, u32[]{:S(2)}, u32[]{:S(2)}) %collective-permute-start.36) | collective-permute-done | bytes 55328 | tf_op jit(solution)/shard_map/ppermute | solution.py:307
  97.0 2.1 %collective-permute-start.38 = (f32[1,24,192]{2,1,0:T(8,128)S(1)}, f32[1,24,192]{2,1,0:T(8,128)S(1)}, u32[]{:S(2)}, u32[]{:S(2)}) collective-permute-start(f32[1,24,192]{2,1,0:T(8,128)S(1)} %constant_dynamic-slice_fusion), channel_id=1, source_target_pairs={{0,4},{1,5},{2,6},{3,7},{4,0},{5,1},{6,2},{7,3},{8,12},{9,13},{10,... | collective-permute-start | bytes 55304 | tf_op jit(solution)/shard_map/ppermute | solution.py:309
  100.0 2.6 %collective-permute-done.38 = f32[1,24,192]{2,1,0:T(8,128)S(1)} collective-permute-done((f32[1,24,192]{2,1,0:T(8,128)S(1)}, f32[1,24,192]{2,1,0:T(8,128)S(1)}, u32[]{:S(2)}, u32[]{:S(2)}) %collective-permute-start.38) | collective-permute-done | bytes 18464 | tf_op jit(solution)/shard_map/ppermute | solution.py:309
  (79 shorter events, 18.8 us)
Async XLA Ops:
  3.2 8.7 %collective-permute-start = (bf16[24,4096]{1,0:T(8,128)(2,1)S(1)}, bf16[24,4096]{1,0:T(8,128)(2,1)S(1)}, u32[]{:S(2)}, u32[]{:S(2)}) collective-permute-start(bf16[24,4096]{1,0:T(8,128)(2,1)S(1)} %get-tuple-element.33.refs_0_), channel_id=1, source_target_pairs={{0,2},{2,4},{4,6},{6,7},{7,5},{5,3},{3,1},{1,0},{8,10},{10,12},{12... | collective-permute-start | bytes 589832 | tf_op jit(solution)/shard_map/ppermute | solution.py:253
  6.3 7.8 %collective-permute-start.15 = (bf16[24,4096]{1,0:T(8,128)(2,1)S(1)}, bf16[24,4096]{1,0:T(8,128)(2,1)S(1)}, u32[]{:S(2)}, u32[]{:S(2)}) collective-permute-start(bf16[24,4096]{1,0:T(8,128)(2,1)S(1)} %get-tuple-element.36.refs_0_.refs_8_), channel_id=1, source_target_pairs={{2,0},{4,2},{6,4},{7,6},{5,7},{3,5},{1,3},{0,1},{10,8},{12,10},{14... | collective-permute-start | bytes 589832 | tf_op jit(solution)/shard_map/ppermute | solution.py:253
  6.3 12.0 %collective-permute-start.3 = (bf16[24,4096]{1,0:T(8,128)(2,1)S(1)}, bf16[24,4096]{1,0:T(8,128)(2,1)S(1)}, u32[]{:S(2)}, u32[]{:S(2)}) collective-permute-start(bf16[24,4096]{1,0:T(8,128)(2,1)S(1)} %get-tuple-element.33.refs_0_), channel_id=1, source_target_pairs={{2,0},{4,2},{6,4},{7,6},{5,7},{3,5},{1,3},{0,1},{10,8},{12,10},{14... | collective-permute-start | bytes 589832 | tf_op jit(solution)/shard_map/ppermute | solution.py:253
  8.2 10.1 %collective-permute-start.13 = (bf16[24,4096]{1,0:T(8,128)(2,1)S(1)}, bf16[24,4096]{1,0:T(8,128)(2,1)S(1)}, u32[]{:S(2)}, u32[]{:S(2)}) collective-permute-start(bf16[24,4096]{1,0:T(8,128)(2,1)S(1)} %get-tuple-element.36.refs_0_.refs_8_), channel_id=1, source_target_pairs={{0,2},{2,4},{4,6},{6,7},{7,5},{5,3},{3,1},{1,0},{8,10},{10,12},{12... | collective-permute-start | bytes 589832 | tf_op jit(solution)/shard_map/ppermute | solution.py:253
  11.9 8.4 %collective-permute-start.1 = (bf16[24,4096]{1,0:T(8,128)(2,1)S(1)}, bf16[24,4096]{1,0:T(8,128)(2,1)S(1)}, u32[]{:S(2)}, u32[]{:S(2)}) collective-permute-start(bf16[24,4096]{1,0:T(8,128)(2,1)S(1)} %collective-permute-done.refs_1_), channel_id=1, source_target_pairs={{0,2},{2,4},{4,6},{6,7},{7,5},{5,3},{3,1},{1,0},{8,10},{10,12},{12... | collective-permute-start | bytes 589832 | tf_op jit(solution)/shard_map/ppermute | solution.py:253
  14.1 8.4 %collective-permute-start.16 = (bf16[24,4096]{1,0:T(8,128)(2,1)S(1)}, bf16[24,4096]{1,0:T(8,128)(2,1)S(1)}, u32[]{:S(2)}, u32[]{:S(2)}) collective-permute-start(bf16[24,4096]{1,0:T(8,128)(2,1)S(1)} %collective-permute-done.15.refs_2_.refs_10_), channel_id=1, source_target_pairs={{2,0},{4,2},{6,4},{7,6},{5,7},{3,5},{1,3},{0,1},{10,8},{12,10},{14... | collective-permute-start | bytes 589832 | tf_op jit(solution)/shard_map/ppermute | solution.py:253
  18.3 8.4 %collective-permute-start.4 = (bf16[24,4096]{1,0:T(8,128)(2,1)S(1)}, bf16[24,4096]{1,0:T(8,128)(2,1)S(1)}, u32[]{:S(2)}, u32[]{:S(2)}) collective-permute-start(bf16[24,4096]{1,0:T(8,128)(2,1)S(1)} %collective-permute-done.3.refs_2_), channel_id=1, source_target_pairs={{2,0},{4,2},{6,4},{7,6},{5,7},{3,5},{1,3},{0,1},{10,8},{12,10},{14... | collective-permute-start | bytes 589832 | tf_op jit(solution)/shard_map/ppermute | solution.py:253
  18.3 8.4 %collective-permute-start.14 = (bf16[24,4096]{1,0:T(8,128)(2,1)S(1)}, bf16[24,4096]{1,0:T(8,128)(2,1)S(1)}, u32[]{:S(2)}, u32[]{:S(2)}) collective-permute-start(bf16[24,4096]{1,0:T(8,128)(2,1)S(1)} %collective-permute-done.13.refs_1_.refs_9_), channel_id=1, source_target_pairs={{0,2},{2,4},{4,6},{6,7},{7,5},{5,3},{3,1},{1,0},{8,10},{10,12},{12... | collective-permute-start | bytes 589832 | tf_op jit(solution)/shard_map/ppermute | solution.py:253
  20.4 8.6 %collective-permute-start.2 = (bf16[24,4096]{1,0:T(8,128)(2,1)S(1)}, bf16[24,4096]{1,0:T(8,128)(2,1)S(1)}, u32[]{:S(2)}, u32[]{:S(2)}) collective-permute-start(bf16[24,4096]{1,0:T(8,128)(2,1)S(1)} %collective-permute-done.1.refs_3_), channel_id=1, source_target_pairs={{0,2},{2,4},{4,6},{6,7},{7,5},{5,3},{3,1},{1,0},{8,10},{10,12},{12... | collective-permute-start | bytes 589832 | tf_op jit(solution)/shard_map/ppermute | solution.py:253
  22.5 8.7 %collective-permute-start.25 = (bf16[24,4096]{1,0:T(8,128)(2,1)S(1)}, bf16[24,4096]{1,0:T(8,128)(2,1)S(1)}, u32[]{:S(2)}, u32[]{:S(2)}) collective-permute-start(bf16[24,4096]{1,0:T(8,128)(2,1)S(1)} %collective-permute-done.16.refs_4_.refs_12_), channel_id=1, source_target_pairs={{2,0},{4,2},{6,4},{7,6},{5,7},{3,5},{1,3},{0,1},{10,8},{12,10},{14... | collective-permute-start | bytes 589832 | tf_op jit(solution)/shard_map/ppermute | solution.py:253
  26.7 8.4 %collective-permute-start.5 = (bf16[24,4096]{1,0:T(8,128)(2,1)S(1)}, bf16[24,4096]{1,0:T(8,128)(2,1)S(1)}, u32[]{:S(2)}, u32[]{:S(2)}) collective-permute-start(bf16[24,4096]{1,0:T(8,128)(2,1)S(1)} %collective-permute-done.4.refs_4_), channel_id=1, source_target_pairs={{2,0},{4,2},{6,4},{7,6},{5,7},{3,5},{1,3},{0,1},{10,8},{12,10},{14... | collective-permute-start | bytes 589832 | tf_op jit(solution)/shard_map/ppermute | solution.py:253
  26.8 10.0 %collective-permute-start.24 = (bf16[24,4096]{1,0:T(8,128)(2,1)S(1)}, bf16[24,4096]{1,0:T(8,128)(2,1)S(1)}, u32[]{:S(2)}, u32[]{:S(2)}) collective-permute-start(bf16[24,4096]{1,0:T(8,128)(2,1)S(1)} %collective-permute-done.14.refs_3_.refs_11_), channel_id=1, source_target_pairs={{0,2},{2,4},{4,6},{6,7},{7,5},{5,3},{3,1},{1,0},{8,10},{10,12},{12... | collective-permute-start | bytes 589832 | tf_op jit(solution)/shard_map/ppermute | solution.py:253
  29.0 8.7 %collective-permute-start.19 = (bf16[24,4096]{1,0:T(8,128)(2,1)S(1)}, bf16[24,4096]{1,0:T(8,128)(2,1)S(1)}, u32[]{:S(2)}, u32[]{:S(2)}) collective-permute-start(bf16[24,4096]{1,0:T(8,128)(2,1)S(1)} %collective-permute-done.2.refs_5_), channel_id=1, source_target_pairs={{0,2},{2,4},{4,6},{6,7},{7,5},{5,3},{3,1},{1,0},{8,10},{10,12},{12... | collective-permute-start | bytes 589832 | tf_op jit(solution)/shard_map/ppermute | solution.py:257
  31.2 8.6 %collective-permute-start.26 = (bf16[24,4096]{1,0:T(8,128)(2,1)S(1)}, bf16[24,4096]{1,0:T(8,128)(2,1)S(1)}, u32[]{:S(2)}, u32[]{:S(2)}) collective-permute-start(bf16[24,4096]{1,0:T(8,128)(2,1)S(1)} %collective-permute-done.25.refs_6_.refs_14_), channel_id=1, source_target_pairs={{2,0},{4,2},{6,4},{7,6},{5,7},{3,5},{1,3},{0,1},{10,8},{12,10},{14... | collective-permute-start | bytes 589832 | tf_op jit(solution)/shard_map/ppermute | solution.py:258
  31.2 14.3 %collective-permute-start.18 = (bf16[24,4096]{1,0:T(8,128)(2,1)S(1)}, bf16[24,4096]{1,0:T(8,128)(2,1)S(1)}, u32[]{:S(2)}, u32[]{:S(2)}) collective-permute-start(bf16[24,4096]{1,0:T(8,128)(2,1)S(1)} %get-tuple-element.43.refs_0_), channel_id=1, source_target_pairs={{2,0},{4,2},{6,4},{7,6},{5,7},{3,5},{1,3},{0,1},{10,8},{12,10},{14... | collective-permute-start | bytes 589832 | tf_op jit(solution)/shard_map/ppermute | solution.py:253
  35.2 10.3 %collective-permute-start.17 = (bf16[24,4096]{1,0:T(8,128)(2,1)S(1)}, bf16[24,4096]{1,0:T(8,128)(2,1)S(1)}, u32[]{:S(2)}, u32[]{:S(2)}) collective-permute-start(bf16[24,4096]{1,0:T(8,128)(2,1)S(1)} %get-tuple-element.43.refs_0_), channel_id=1, source_target_pairs={{0,2},{2,4},{4,6},{6,7},{7,5},{5,3},{3,1},{1,0},{8,10},{10,12},{12... | collective-permute-start | bytes 589832 | tf_op jit(solution)/shard_map/ppermute | solution.py:253
  36.8 10.8 %collective-permute-start.7 = (bf16[24,4096]{1,0:T(8,128)(2,1)S(1)}, bf16[24,4096]{1,0:T(8,128)(2,1)S(1)}, u32[]{:S(2)}, u32[]{:S(2)}) collective-permute-start(bf16[24,4096]{1,0:T(8,128)(2,1)S(1)} %get-tuple-element.51.refs_0_.refs_8_), channel_id=1, source_target_pairs={{2,0},{4,2},{6,4},{7,6},{5,7},{3,5},{1,3},{0,1},{10,8},{12,10},{14... | collective-permute-start | bytes 589832 | tf_op jit(solution)/shard_map/ppermute | solution.py:253
  37.7 14.9 %collective-permute-start.6 = (bf16[24,4096]{1,0:T(8,128)(2,1)S(1)}, bf16[24,4096]{1,0:T(8,128)(2,1)S(1)}, u32[]{:S(2)}, u32[]{:S(2)}) collective-permute-start(bf16[24,4096]{1,0:T(8,128)(2,1)S(1)} %get-tuple-element.51.refs_0_.refs_8_), channel_id=1, source_target_pairs={{0,2},{2,4},{4,6},{6,7},{7,5},{5,3},{3,1},{1,0},{8,10},{10,12},{12... | collective-permute-start | bytes 589832 | tf_op jit(solution)/shard_map/ppermute | solution.py:253
  39.8 28.9 %collective-permute-start.29 = (bf16[8,24,1024]{2,1,0:T(8,128)(2,1)S(1)}, bf16[8,24,1024]{2,1,0:T(8,128)(2,1)S(1)}, u32[]{:S(2)}, u32[]{:S(2)}) collective-permute-start(bf16[8,24,1024]{2,1,0:T(8,128)(2,1)S(1)} %shard_map.75.refs_1_), channel_id=1, source_target_pairs={{0,16},{8,24},{16,0},{24,8},{1,17},{9,25},{17,1},{25,9},{2,18},{10... | collective-permute-start | bytes 1179656 | tf_op jit(solution)/shard_map/ppermute | solution.py:233
  45.5 8.2 %collective-permute-start.20 = (bf16[24,4096]{1,0:T(8,128)(2,1)S(1)}, bf16[24,4096]{1,0:T(8,128)(2,1)S(1)}, u32[]{:S(2)}, u32[]{:S(2)}) collective-permute-start(bf16[24,4096]{1,0:T(8,128)(2,1)S(1)} %collective-permute-done.17.refs_1_), channel_id=1, source_target_pairs={{0,2},{2,4},{4,6},{6,7},{7,5},{5,3},{3,1},{1,0},{8,10},{10,12},{12... | collective-permute-start | bytes 589832 | tf_op jit(solution)/shard_map/ppermute | solution.py:253
  47.1 12.7 %collective-permute-start.21 = (bf16[24,4096]{1,0:T(8,128)(2,1)S(1)}, bf16[24,4096]{1,0:T(8,128)(2,1)S(1)}, u32[]{:S(2)}, u32[]{:S(2)}) collective-permute-start(bf16[24,4096]{1,0:T(8,128)(2,1)S(1)} %collective-permute-done.18.refs_2_), channel_id=1, source_target_pairs={{2,0},{4,2},{6,4},{7,6},{5,7},{3,5},{1,3},{0,1},{10,8},{12,10},{14... | collective-permute-start | bytes 589832 | tf_op jit(solution)/shard_map/ppermute | solution.py:253
  47.6 7.8 %collective-permute-start.9 = (bf16[24,4096]{1,0:T(8,128)(2,1)S(1)}, bf16[24,4096]{1,0:T(8,128)(2,1)S(1)}, u32[]{:S(2)}, u32[]{:S(2)}) collective-permute-start(bf16[24,4096]{1,0:T(8,128)(2,1)S(1)} %collective-permute-done.7.refs_2_.refs_10_), channel_id=1, source_target_pairs={{2,0},{4,2},{6,4},{7,6},{5,7},{3,5},{1,3},{0,1},{10,8},{12,10},{14... | collective-permute-start | bytes 589832 | tf_op jit(solution)/shard_map/ppermute | solution.py:253
  52.7 9.3 %collective-permute-start.8 = (bf16[24,4096]{1,0:T(8,128)(2,1)S(1)}, bf16[24,4096]{1,0:T(8,128)(2,1)S(1)}, u32[]{:S(2)}, u32[]{:S(2)}) collective-permute-start(bf16[24,4096]{1,0:T(8,128)(2,1)S(1)} %collective-permute-done.6.refs_1_.refs_9_), channel_id=1, source_target_pairs={{0,2},{2,4},{4,6},{6,7},{7,5},{5,3},{3,1},{1,0},{8,10},{10,12},{12... | collective-permute-start | bytes 589832 | tf_op jit(solution)/shard_map/ppermute | solution.py:253
  53.8 8.3 %collective-permute-start.22 = (bf16[24,4096]{1,0:T(8,128)(2,1)S(1)}, bf16[24,4096]{1,0:T(8,128)(2,1)S(1)}, u32[]{:S(2)}, u32[]{:S(2)}) collective-permute-start(bf16[24,4096]{1,0:T(8,128)(2,1)S(1)} %collective-permute-done.20.refs_3_), channel_id=1, source_target_pairs={{0,2},{2,4},{4,6},{6,7},{7,5},{5,3},{3,1},{1,0},{8,10},{10,12},{12... | collective-permute-start | bytes 589832 | tf_op jit(solution)/shard_map/ppermute | solution.py:253
  55.4 9.2 %collective-permute-start.11 = (bf16[24,4096]{1,0:T(8,128)(2,1)S(1)}, bf16[24,4096]{1,0:T(8,128)(2,1)S(1)}, u32[]{:S(2)}, u32[]{:S(2)}) collective-permute-start(bf16[24,4096]{1,0:T(8,128)(2,1)S(1)} %collective-permute-done.9.refs_4_.refs_12_), channel_id=1, source_target_pairs={{2,0},{4,2},{6,4},{7,6},{5,7},{3,5},{1,3},{0,1},{10,8},{12,10},{14... | collective-permute-start | bytes 589832 | tf_op jit(solution)/shard_map/ppermute | solution.py:253
  59.9 8.9 %collective-permute-start.23 = (bf16[24,4096]{1,0:T(8,128)(2,1)S(1)}, bf16[24,4096]{1,0:T(8,128)(2,1)S(1)}, u32[]{:S(2)}, u32[]{:S(2)}) collective-permute-start(bf16[24,4096]{1,0:T(8,128)(2,1)S(1)} %collective-permute-done.21.refs_4_), channel_id=1, source_target_pairs={{2,0},{4,2},{6,4},{7,6},{5,7},{3,5},{1,3},{0,1},{10,8},{12,10},{14... | collective-permute-start | bytes 589832 | tf_op jit(solution)/shard_map/ppermute | solution.py:253
  62.0 6.7 %collective-permute-start.10 = (bf16[24,4096]{1,0:T(8,128)(2,1)S(1)}, bf16[24,4096]{1,0:T(8,128)(2,1)S(1)}, u32[]{:S(2)}, u32[]{:S(2)}) collective-permute-start(bf16[24,4096]{1,0:T(8,128)(2,1)S(1)} %collective-permute-done.8.refs_3_.refs_11_), channel_id=1, source_target_pairs={{0,2},{2,4},{4,6},{6,7},{7,5},{5,3},{3,1},{1,0},{8,10},{10,12},{12... | collective-permute-start | bytes 589832 | tf_op jit(solution)/shard_map/ppermute | solution.py:253
  62.1 8.2 %collective-permute-start.27 = (bf16[24,4096]{1,0:T(8,128)(2,1)S(1)}, bf16[24,4096]{1,0:T(8,128)(2,1)S(1)}, u32[]{:S(2)}, u32[]{:S(2)}) collective-permute-start(bf16[24,4096]{1,0:T(8,128)(2,1)S(1)} %collective-permute-done.22.refs_5_), channel_id=1, source_target_pairs={{0,2},{2,4},{4,6},{6,7},{7,5},{5,3},{3,1},{1,0},{8,10},{10,12},{12... | collective-permute-start | bytes 589832 | tf_op jit(solution)/shard_map/ppermute | solution.py:257
  68.7 17.5 %collective-permute-start.28 = (bf16[8,24,1024]{2,1,0:T(8,128)(2,1)S(1)}, bf16[8,24,1024]{2,1,0:T(8,128)(2,1)S(1)}, u32[]{:S(2)}, u32[]{:S(2)}) collective-permute-start(bf16[8,24,1024]{2,1,0:T(8,128)(2,1)S(1)} %shard_map.75.refs_1_), channel_id=1, source_target_pairs={{0,8},{8,0},{16,24},{24,16},{1,9},{9,1},{17,25},{25,17},{2,10},{10... | collective-permute-start | bytes 1179656 | tf_op jit(solution)/shard_map/ppermute | solution.py:234
  68.8 17.4 %collective-permute-start.30 = (bf16[8,24,1024]{2,1,0:T(8,128)(2,1)S(1)}, bf16[8,24,1024]{2,1,0:T(8,128)(2,1)S(1)}, u32[]{:S(2)}, u32[]{:S(2)}) collective-permute-start(bf16[8,24,1024]{2,1,0:T(8,128)(2,1)S(1)} %collective-permute-done.29.refs_4_), channel_id=1, source_target_pairs={{0,8},{8,0},{16,24},{24,16},{1,9},{9,1},{17,25},{25,17},{2,10},{10... | collective-permute-start | bytes 1179656 | tf_op jit(solution)/shard_map/ppermute | solution.py:239
  70.3 11.2 %collective-permute-start.32 = (bf16[8,24,1024]{2,1,0:T(8,128)(2,1)S(1)}, bf16[8,24,1024]{2,1,0:T(8,128)(2,1)S(1)}, u32[]{:S(2)}, u32[]{:S(2)}) collective-permute-start(bf16[8,24,1024]{2,1,0:T(8,128)(2,1)S(1)} %shard_map.76.refs_2_), channel_id=1, source_target_pairs={{0,16},{8,24},{16,0},{24,8},{1,17},{9,25},{17,1},{25,9},{2,18},{10... | collective-permute-start | bytes 1179656 | tf_op jit(solution)/shard_map/ppermute | solution.py:233
  70.9 15.2 %collective-permute-start.31 = (bf16[8,24,1024]{2,1,0:T(8,128)(2,1)S(1)}, bf16[8,24,1024]{2,1,0:T(8,128)(2,1)S(1)}, u32[]{:S(2)}, u32[]{:S(2)}) collective-permute-start(bf16[8,24,1024]{2,1,0:T(8,128)(2,1)S(1)} %shard_map.76.refs_2_), channel_id=1, source_target_pairs={{0,8},{8,0},{16,24},{24,16},{1,9},{9,1},{17,25},{25,17},{2,10},{10... | collective-permute-start | bytes 1179656 | tf_op jit(solution)/shard_map/ppermute | solution.py:234
  (13 other events, 51.5 us)
